TPU v7x, 256 devices: a whole 4x4x8 slice. The times are simulated.
256 devices in a mesh: lon: 32 (over x, z), lat: 8 (over y, core).
Axes of the slice: x: 4, y: 4, z: 8, core: 2. Of those that a mesh axis runs over, the one named last changes fastest.
Arguments:
- right_side: float32 [4096, 8192], P('lat', 'lon'), may hold values from -60 to 60
- depth: float32 [4096, 8192], P('lat', 'lon'), may hold values from 0.2 to 6
- mask: int32 [4096, 8192], P('lat', 'lon'), may hold values 0 or 1
- basis: float32 [4096, 8192], P('lat', 'lon'), may hold values from 0.5 to 2
- coarse_inverse: float32 [2048, 2048], P(('lon', 'lat')), may hold values from -0.00018310547 to 0.00018310547, as said below
Outputs:
- solution_field: float32 [4096, 8192], P('lat', 'lon')
- residual: float32 [4096, 8192], P('lat', 'lon')
Inputs may be any that keep to these rules, and one draw needn't show every extreme that they name: coarse_inverse is exactly symmetric. `mask`: 1 marks an ocean cell, 0 a land cell.
All inputs are finite; a program needn't handle non-finite values. No bound on the sum of `mask` on one device may be relied on, other than what follows from the above.
Results may differ from a plain program's by a relative error of at most 0.0003.
Values sent between devices are 32-bit elements; how exact they have to be, the bound alone decides.
No kernel may reach another device: no remote copies, remote signals or barrier semaphores. Data moves between devices by JAX's collectives and lax.ppermute only.
A program may use at most 64 MiB of HBM per device.

v0:
```python
import jax
import jax.numpy as jnp
from jax import lax
from jax.sharding import PartitionSpec as P

ITERS = 2
SWEEPS = 4
AGG_LAT = 4
AGG_LON = 2


low_edge = 0.1
high_edge = 2.0
shift_scale = 1e-05


def with_halo(x, sides, width):
    for axis, dim in sides:
        size, length = (lax.axis_size(axis), x.shape[dim])
        up = [(i, (i + 1) % size) for i in range(size)]
        down = [(j, i) for i, j in up]
        last = lax.slice_in_dim(x, length - width, length, axis=dim)
        first = lax.slice_in_dim(x, 0, width, axis=dim)
        before = lax.ppermute(last, axis, up)
        after = lax.ppermute(first, axis, down)
        x = jnp.concatenate([before, x, after], axis=dim)
    return x


def chebyshev_plan(sweep_total):
    interval_mid = (high_edge + low_edge) / 2.0
    interval_half = (high_edge - low_edge) / 2.0
    mid_ratio = interval_mid / interval_half
    previous = 1.0 / mid_ratio
    sweep_pairs = []
    for sweep_number in range(sweep_total - 1):
        fresh_rho = 1.0 / (2.0 * mid_ratio - previous)
        sweep_pairs.append((fresh_rho * previous, 2.0 * fresh_rho / interval_half))
        previous = fresh_rho
    return (1.0 / interval_mid, sweep_pairs)


def crop_to(source_array, have_radius, want_radius, row_move=0, col_move=0):
    margin_cut = have_radius - want_radius
    return source_array[
        margin_cut + row_move : source_array.shape[0] - margin_cut + row_move,
        margin_cut + col_move : source_array.shape[1] - margin_cut + col_move,
    ]


def body(right_side, depth, mask, basis, coarse_inverse):
    tile_rows, tile_cols = right_side.shape
    total_rows = tile_rows * lax.axis_size("lat")
    mask_float = mask.astype(jnp.float32)
    wet_depth = depth * mask_float
    widened = with_halo(wet_depth, (("lon", 1), ("lat", 0)), SWEEPS + 1)
    row_index = (
        lax.axis_index("lat") * tile_rows
        - SWEEPS
        + jnp.arange(tile_rows + 2 * SWEEPS, dtype=jnp.int32)
    )
    latitude = (row_index.astype(jnp.float32) + 0.5) * (2.6 / total_rows) - 1.3
    center = widened[1:-1, 1:-1]
    east_face = jnp.minimum(center, widened[1:-1, 2:]) / jnp.cos(latitude)[:, None]
    inside = ((row_index >= 0) & (row_index <= total_rows - 2)).astype(jnp.float32)
    north_face = (
        jnp.minimum(center, widened[2:, 1:-1])
        * jnp.cos(latitude + 1.3 / total_rows)[:, None]
        * inside[:, None]
    )
    shift_field = jnp.broadcast_to((shift_scale * jnp.cos(latitude))[:, None], center.shape)
    outer_radius = SWEEPS - 1
    diagonal = (
        crop_to(shift_field, SWEEPS, outer_radius)
        + crop_to(east_face, SWEEPS, outer_radius)
        + crop_to(east_face, SWEEPS, outer_radius, 0, -1)
        + crop_to(north_face, SWEEPS, outer_radius)
        + crop_to(north_face, SWEEPS, outer_radius, -1, 0)
    )
    inverse_diag = 1.0 / diagonal
    inverse_tile = crop_to(inverse_diag, outer_radius, 0)
    sweep_start, sweep_pairs = chebyshev_plan(SWEEPS)
    block_rows = tile_rows // AGG_LAT
    block_cols = tile_cols // AGG_LON

    def apply_stencil(padded, radius):
        want_radius = radius - 1
        inner = padded[1:-1, 1:-1]
        return (
            crop_to(shift_field, SWEEPS, want_radius) * inner
            + crop_to(east_face, SWEEPS, want_radius) * (inner - padded[1:-1, 2:])
            + crop_to(east_face, SWEEPS, want_radius, 0, -1) * (inner - padded[1:-1, :-2])
            + crop_to(north_face, SWEEPS, want_radius) * (inner - padded[2:, 1:-1])
            + crop_to(north_face, SWEEPS, want_radius, -1, 0) * (inner - padded[:-2, 1:-1])
        )

    def smooth(residual):
        step_direction = sweep_start * (inverse_tile * residual)
        estimate = step_direction
        for first_coef, second_coef in sweep_pairs:
            padded = with_halo(estimate, (("lon", 1), ("lat", 0)), 1)
            remain = residual - apply_stencil(padded, 1)
            step_direction = first_coef * step_direction + second_coef * (inverse_tile * remain)
            estimate = estimate + step_direction
        return estimate

    def coarse_part(residual):
        restricted = jnp.sum(
            (basis * residual).reshape(AGG_LAT, block_rows, AGG_LON, block_cols), axis=(1, 3)
        ).reshape(-1)
        gathered = lax.all_gather(restricted, ("lon", "lat"), axis=0, tiled=True)
        solved = jnp.dot(coarse_inverse, gathered, precision=lax.Precision.HIGHEST)
        spread = jnp.broadcast_to(
            solved.reshape(AGG_LAT, 1, AGG_LON, 1), (AGG_LAT, block_rows, AGG_LON, block_cols)
        )
        return basis * spread.reshape(tile_rows, tile_cols)

    def precondition(residual):
        return mask_float * (smooth(residual) + coarse_part(residual))

    solution_field = jnp.zeros_like(right_side)
    residual = right_side * mask_float
    update = precondition(residual)
    search = update
    for turn_index in range(ITERS):
        operate_padded = with_halo(search, (("lon", 1), ("lat", 0)), 1)
        applied_search = apply_stencil(operate_padded, 1)
        curvature_sum, projection = lax.psum(
            (jnp.sum(search * applied_search), jnp.sum(search * residual)), ("lon", "lat")
        )
        step_size = projection / curvature_sum
        solution_field = solution_field + step_size * search
        residual = residual - step_size * applied_search
        if turn_index + 1 < ITERS:
            update = precondition(residual)
            coupling = lax.psum(jnp.sum(update * applied_search), ("lon", "lat"))
            blend_factor = -coupling / curvature_sum
            search = update + blend_factor * search
    return (solution_field, residual)


def solution(mesh):
    in_specs = (
        P("lat", "lon"),
        P("lat", "lon"),
        P("lat", "lon"),
        P("lat", "lon"),
        P(("lon", "lat"), None),
    )
    out_specs = (P("lat", "lon"), P("lat", "lon"))
    return jax.shard_map(body, mesh=mesh, in_specs=in_specs, out_specs=out_specs, check_vma=False)
```

profile of v0, /device:TPU:1, one launch (start us, length us, event | category | flops | bytes accessed | tf_op | source)
XLA Modules:
  0.0 554.2 jit_solution(9191135415230480525)
XLA Ops:
  4.6 6.2 %collective-permute-start.1 = (f32[512,5]{1,0:T(8,128)S(1)}, f32[512,5]{1,0:T(8,128)S(1)}, u32[]{:S(2)}, u32[]{:S(2)}) collective-permute-start(f32[512,5]{1,0:T(8,128)S(1)} %get-tuple-element.68), channel_id=1, source_target_pairs={{8,0},{16,8},{24,16},{32,24},{40,32},{48,40},{56,48},{64,56},{72,6... | collective-permute-start | bytes 30728 | tf_op jit(solution)/shard_map/ppermute | solution.py:25
  11.1 5.7 %collective-permute-done = f32[512,5]{1,0:T(8,128)S(1)} collective-permute-done((f32[512,5]{1,0:T(8,128)S(1)}, f32[512,5]{1,0:T(8,128)S(1)}, u32[]{:S(2)}, u32[]{:S(2)}) %collective-permute-start) | collective-permute-done | bytes 10272 | tf_op jit(solution)/shard_map/ppermute | solution.py:24
  26.1 4.9 collective-permute-start.4
  31.1 5.6 %collective-permute-done.4 = f32[512,1]{1,0:T(8,128)S(1)} collective-permute-done((f32[512,1]{1,0:T(8,128)S(1)}, f32[512,1]{1,0:T(8,128)S(1)}, u32[]{:S(2)}, u32[]{:S(2)}) %collective-permute-start.4) | collective-permute-done | bytes 2080 | tf_op jit(solution)/shard_map/ppermute | solution.py:25
  36.7 5.2 collective-permute-done.5
  49.5 3.8 collective-permute-done.8
  57.4 4.7 collective-permute-start.10
  72.6 77.8 %all-reduce = f32[2048]{0:T(1024)S(1)} all-reduce(f32[2048]{0:T(1024)S(1)} %dynamic-update-slice), channel_id=1, replica_groups=mesh['lon'=32,'lat'=8] {'lon','lat'}, use_global_device_ids=true, to_apply=%add | all-reduce | flops 2048 | bytes 16384
  160.5 4.2 collective-permute-done.16
  164.6 4.6 collective-permute-done.17
  176.8 74.1 %all-reduce.3 = (f32[]{:T(128)}, f32[]{:T(128)}) all-reduce(f32[]{:T(128)} %get-tuple-element.5, f32[]{:T(128)} %get-tuple-element.4), channel_id=1, replica_groups=mesh['lon'=32,'lat'=8] {'lon','lat'}, use_global_device_ids=true, to_apply=%region_2.0 | all-reduce | flops 2 | bytes 16 | tf_op jit(solution)/shard_map/psum | solution.py:128
  253.6 4.1 collective-permute-start.20
  257.7 5.0 collective-permute-done.20
  262.6 5.2 collective-permute-done.21
  274.7 3.8 collective-permute-done.24
  278.4 3.6 collective-permute-done.25
  282.8 4.2 collective-permute-start.26
  289.8 4.2 fusion.136
  296.5 77.0 %all-reduce.1 = f32[2048]{0:T(1024)S(1)} all-reduce(f32[2048]{0:T(1024)S(1)} %dynamic-update-slice.1), channel_id=1, replica_groups=mesh['lon'=32,'lat'=8] {'lon','lat'}, use_global_device_ids=true, to_apply=%add.1 | all-reduce | flops 2048 | bytes 16384
  377.6 4.4 multiply_reduce_fusion.2
  382.0 73.6 %psum.37 = f32[]{:T(128)} all-reduce(f32[]{:T(128)} %get-tuple-element.11), channel_id=1, replica_groups=mesh['lon'=32,'lat'=8] {'lon','lat'}, use_global_device_ids=true, to_apply=%region_7.0 | all-reduce | flops 1 | bytes 8 | tf_op jit(solution)/shard_map/psum | solution.py:136
  461.4 5.0 collective-permute-done.32
  466.3 5.2 collective-permute-done.33
  477.2 73.5 %all-reduce.2 = (f32[]{:T(128)}, f32[]{:T(128)}) all-reduce(f32[]{:T(128)} %get-tuple-element.3, f32[]{:T(128)} %get-tuple-element.2), channel_id=1, replica_groups=mesh['lon'=32,'lat'=8] {'lon','lat'}, use_global_device_ids=true, to_apply=%region_9.0 | all-reduce | flops 2 | bytes 16 | tf_op jit(solution)/shard_map/psum | solution.py:128
  (150 shorter events, 83.6 us)
Async XLA Ops:
  2.1 14.7 %collective-permute-start = (f32[512,5]{1,0:T(8,128)S(1)}, f32[512,5]{1,0:T(8,128)S(1)}, u32[]{:S(2)}, u32[]{:S(2)}) collective-permute-start(f32[512,5]{1,0:T(8,128)S(1)} %get-tuple-element.67), channel_id=1, source_target_pairs={{0,8},{8,16},{16,24},{24,32},{32,40},{40,48},{48,56},{56,64},{64,7... | collective-permute-start | bytes 30728 | tf_op jit(solution)/shard_map/ppermute | solution.py:24
  4.6 12.2 %collective-permute-start.1 = (f32[512,5]{1,0:T(8,128)S(1)}, f32[512,5]{1,0:T(8,128)S(1)}, u32[]{:S(2)}, u32[]{:S(2)}) collective-permute-start(f32[512,5]{1,0:T(8,128)S(1)} %get-tuple-element.68), channel_id=1, source_target_pairs={{8,0},{16,8},{24,16},{32,24},{40,32},{48,40},{56,48},{64,56},{72,6... | collective-permute-start | bytes 30728 | tf_op jit(solution)/shard_map/ppermute | solution.py:25
  16.9 3.2 collective-permute-start.2
  19.3 3.1 collective-permute-start.3
  26.1 10.6 %collective-permute-start.4 = (f32[512,1]{1,0:T(8,128)S(1)}, f32[512,1]{1,0:T(8,128)S(1)}, u32[]{:S(2)}, u32[]{:S(2)}) collective-permute-start(f32[512,1]{1,0:T(8,128)S(1)} %get-tuple-element.66), channel_id=1, source_target_pairs={{8,0},{16,8},{24,16},{32,24},{40,32},{48,40},{56,48},{64,56},{72,6... | collective-permute-start | bytes 6152 | tf_op jit(solution)/shard_map/ppermute | solution.py:25
  31.0 10.9 %collective-permute-start.5 = (f32[512,1]{1,0:T(8,128)S(1)}, f32[512,1]{1,0:T(8,128)S(1)}, u32[]{:S(2)}, u32[]{:S(2)}) collective-permute-start(f32[512,1]{1,0:T(8,128)S(1)} %get-tuple-element.65), channel_id=1, source_target_pairs={{0,8},{8,16},{16,24},{24,32},{32,40},{40,48},{48,56},{56,64},{64,7... | collective-permute-start | bytes 6152 | tf_op jit(solution)/shard_map/ppermute | solution.py:24
  48.0 5.3 collective-permute-start.8
  48.1 8.6 %collective-permute-start.9 = (f32[512,1]{1,0:T(8,128)S(1)}, f32[512,1]{1,0:T(8,128)S(1)}, u32[]{:S(2)}, u32[]{:S(2)}) collective-permute-start(f32[512,1]{1,0:T(8,128)S(1)} %get-tuple-element.63), channel_id=1, source_target_pairs={{0,8},{8,16},{16,24},{24,32},{32,40},{40,48},{48,56},{56,64},{64,7... | collective-permute-start | bytes 6152 | tf_op jit(solution)/shard_map/ppermute | solution.py:24
  57.4 9.4 %collective-permute-start.10 = (f32[1,258]{1,0:T(1,128)S(1)}, f32[1,258]{1,0:T(1,128)S(1)}, u32[]{:S(2)}, u32[]{:S(2)}) collective-permute-start(f32[1,258]{1,0:T(1,128)S(1)} %get-tuple-element.39), channel_id=1, source_target_pairs={{1,0},{2,1},{3,2},{4,3},{5,4},{6,5},{7,6},{0,7},{9,8},{10,9},{11,1... | collective-permute-start | bytes 3104 | tf_op jit(solution)/shard_map/ppermute | solution.py:25
  62.2 4.6 collective-permute-start.11
  71.1 79.3 %collective-permute-start.12 = (f32[512,1]{1,0:T(8,128)}, f32[512,1]{1,0:T(8,128)S(1)}, u32[]{:S(2)}, u32[]{:S(2)}) collective-permute-start(f32[512,1]{1,0:T(8,128)} %get-tuple-element.62), channel_id=1, source_target_pairs={{8,0},{16,8},{24,16},{32,24},{40,32},{48,40},{56,48},{64,56},{72,6... | collective-permute-start | bytes 6152 | tf_op jit(solution)/shard_map/ppermute | solution.py:25
  71.1 79.3 %collective-permute-start.13 = (f32[512,1]{1,0:T(8,128)S(1)}, f32[512,1]{1,0:T(8,128)S(1)}, u32[]{:S(2)}, u32[]{:S(2)}) collective-permute-start(f32[512,1]{1,0:T(8,128)S(1)} %get-tuple-element.61), channel_id=1, source_target_pairs={{0,8},{8,16},{16,24},{24,32},{32,40},{40,48},{48,56},{56,64},{64,7... | collective-permute-start | bytes 6152 | tf_op jit(solution)/shard_map/ppermute | solution.py:24
  158.9 5.7 %collective-permute-start.16 = (f32[512,1]{1,0:T(8,128)S(1)}, f32[512,1]{1,0:T(8,128)S(1)}, u32[]{:S(2)}, u32[]{:S(2)}) collective-permute-start(f32[512,1]{1,0:T(8,128)S(1)} %get-tuple-element.60), channel_id=1, source_target_pairs={{8,0},{16,8},{24,16},{32,24},{40,32},{48,40},{56,48},{64,56},{72,6... | collective-permute-start | bytes 6152 | tf_op jit(solution)/shard_map/ppermute | solution.py:25
  160.3 8.9 %collective-permute-start.17 = (f32[512,1]{1,0:T(8,128)S(1)}, f32[512,1]{1,0:T(8,128)S(1)}, u32[]{:S(2)}, u32[]{:S(2)}) collective-permute-start(f32[512,1]{1,0:T(8,128)S(1)} %get-tuple-element.59), channel_id=1, source_target_pairs={{0,8},{8,16},{16,24},{24,32},{32,40},{40,48},{48,56},{56,64},{64,7... | collective-permute-start | bytes 6152 | tf_op jit(solution)/shard_map/ppermute | solution.py:24
  169.3 4.1 collective-permute-start.18
  253.6 9.1 %collective-permute-start.20 = (f32[512,1]{1,0:T(8,128)S(1)}, f32[512,1]{1,0:T(8,128)S(1)}, u32[]{:S(2)}, u32[]{:S(2)}) collective-permute-start(f32[512,1]{1,0:T(8,128)S(1)} %get-tuple-element.58), channel_id=1, source_target_pairs={{8,0},{16,8},{24,16},{32,24},{40,32},{48,40},{56,48},{64,56},{72,6... | collective-permute-start | bytes 6152 | tf_op jit(solution)/shard_map/ppermute | solution.py:25
  257.7 10.2 %collective-permute-start.21 = (f32[512,1]{1,0:T(8,128)S(1)}, f32[512,1]{1,0:T(8,128)S(1)}, u32[]{:S(2)}, u32[]{:S(2)}) collective-permute-start(f32[512,1]{1,0:T(8,128)S(1)} %get-tuple-element.57), channel_id=1, source_target_pairs={{0,8},{8,16},{16,24},{24,32},{32,40},{40,48},{48,56},{56,64},{64,7... | collective-permute-start | bytes 6152 | tf_op jit(solution)/shard_map/ppermute | solution.py:24
  273.1 5.3 collective-permute-start.24
  273.5 8.6 %collective-permute-start.25 = (f32[512,1]{1,0:T(8,128)S(1)}, f32[512,1]{1,0:T(8,128)S(1)}, u32[]{:S(2)}, u32[]{:S(2)}) collective-permute-start(f32[512,1]{1,0:T(8,128)S(1)} %get-tuple-element.55), channel_id=1, source_target_pairs={{0,8},{8,16},{16,24},{24,32},{32,40},{40,48},{48,56},{56,64},{64,7... | collective-permute-start | bytes 6152 | tf_op jit(solution)/shard_map/ppermute | solution.py:24
  282.8 7.0 %collective-permute-start.26 = (f32[1,258]{1,0:T(1,128)S(1)}, f32[1,258]{1,0:T(1,128)S(1)}, u32[]{:S(2)}, u32[]{:S(2)}) collective-permute-start(f32[1,258]{1,0:T(1,128)S(1)} %get-tuple-element.31), channel_id=1, source_target_pairs={{1,0},{2,1},{3,2},{4,3},{5,4},{6,5},{7,6},{0,7},{9,8},{10,9},{11,1... | collective-permute-start | bytes 3104 | tf_op jit(solution)/shard_map/ppermute | solution.py:25
  295.0 78.5 %collective-permute-start.28 = (f32[512,1]{1,0:T(8,128)}, f32[512,1]{1,0:T(8,128)S(1)}, u32[]{:S(2)}, u32[]{:S(2)}) collective-permute-start(f32[512,1]{1,0:T(8,128)} %get-tuple-element.54), channel_id=1, source_target_pairs={{8,0},{16,8},{24,16},{32,24},{40,32},{48,40},{56,48},{64,56},{72,6... | collective-permute-start | bytes 6152 | tf_op jit(solution)/shard_map/ppermute | solution.py:25
  295.0 78.5 %collective-permute-start.29 = (f32[512,1]{1,0:T(8,128)}, f32[512,1]{1,0:T(8,128)}, u32[]{:S(2)}, u32[]{:S(2)}) collective-permute-start(f32[512,1]{1,0:T(8,128)} %get-tuple-element.53), channel_id=1, source_target_pairs={{0,8},{8,16},{16,24},{24,32},{32,40},{40,48},{48,56},{56,64},{64,7... | collective-permute-start | bytes 6152 | tf_op jit(solution)/shard_map/ppermute | solution.py:24
  458.2 8.2 %collective-permute-start.32 = (f32[512,1]{1,0:T(8,128)S(1)}, f32[512,1]{1,0:T(8,128)S(1)}, u32[]{:S(2)}, u32[]{:S(2)}) collective-permute-start(f32[512,1]{1,0:T(8,128)S(1)} %get-tuple-element.52), channel_id=1, source_target_pairs={{8,0},{16,8},{24,16},{32,24},{40,32},{48,40},{56,48},{64,56},{72,6... | collective-permute-start | bytes 6152 | tf_op jit(solution)/shard_map/ppermute | solution.py:25
  461.3 10.2 %collective-permute-start.33 = (f32[512,1]{1,0:T(8,128)S(1)}, f32[512,1]{1,0:T(8,128)S(1)}, u32[]{:S(2)}, u32[]{:S(2)}) collective-permute-start(f32[512,1]{1,0:T(8,128)S(1)} %get-tuple-element.51), channel_id=1, source_target_pairs={{0,8},{8,16},{16,24},{24,32},{32,40},{40,48},{48,56},{56,64},{64,7... | collective-permute-start | bytes 6152 | tf_op jit(solution)/shard_map/ppermute | solution.py:24
  (30 other events, 411.2 us)
where the time goes:
time: 555 us; the launch traced here: 554 us
  blocking collectives  376 us (68%)
  waiting for transfers between devices  71.4 us (13%)
  starting transfers between devices  52 us (9%)
  other arithmetic  38.3 us (7%)
  local copies, waits for them, and re-layouts  11.2 us (2%)
    unnamed x2, blocking collectives  155 us
    psum x2, blocking collectives, body(): lax.psum((jnp.sum(search * applied_search), jnp.sum(search * residual)),...  148 us
    psum x1, blocking collectives, body(): coupling = lax.psum(jnp.sum(update * applied_search), ('lon', 'lat'))  73.6 us
    ppermute x18, starting transfers between devices, with_halo(): after = lax.ppermute(first, axis, down)  39.2 us
    ppermute x18, waiting for transfers between devices, with_halo(): after = lax.ppermute(first, axis, down)  35.9 us
    ppermute x18, waiting for transfers between devices, with_halo(): before = lax.ppermute(last, axis, up)  35.4 us
    ppermute x18, starting transfers between devices, with_halo(): before = lax.ppermute(last, axis, up)  12.8 us
    add x4, other arithmetic, smooth(): estimate = estimate + step_direction  11.7 us
  transfers between devices with their start and end apart: 36, of which 23 were waited for; matrix products, arithmetic and copies ran while one was open for 2% of the time, Pallas kernels for 0%

commit v1 on v0

v1 whole, which is shorter than its diff:
```python
import functools

import jax
import jax.numpy as jnp
from jax import lax
from jax.experimental import pallas as pl
from jax.experimental.pallas import tpu as pltpu
from jax.sharding import PartitionSpec as P

SWEEPS = 4
AGG_LAT = 4
AGG_LON = 2
LOW_EDGE = 0.1
HIGH_EDGE = 2.0
SHIFT_SCALE = 1.0e-5

NY = 512
NX = 256
HY = 16
WX = 9
ROWS = NY + 2 * HY
LANES = 128
BLK = 3
BAND = NY // AGG_LAT
STEP = 32
SLOTS = LANES // 8
AXES = ("lon", "lat")
F32 = jnp.float32


def chebyshev_plan(sweep_total):
    interval_mid = (HIGH_EDGE + LOW_EDGE) / 2.0
    interval_half = (HIGH_EDGE - LOW_EDGE) / 2.0
    mid_ratio = interval_mid / interval_half
    previous = 1.0 / mid_ratio
    pairs = []
    for _ in range(sweep_total - 1):
        fresh = 1.0 / (2.0 * mid_ratio - previous)
        pairs.append((fresh * previous, 2.0 * fresh / interval_half))
        previous = fresh
    return 1.0 / interval_mid, pairs


def lane_ids(rows):
    return lax.broadcasted_iota(jnp.int32, (rows, LANES), 1)


def east_of(blocks):
    lane = lane_ids(blocks[0].shape[0])
    rolled = [pltpu.roll(v, LANES - 1, 1) for v in blocks]
    return [jnp.where(lane == LANES - 1, rolled[(b + 1) % BLK], rolled[b]) for b in range(BLK)]


def west_of(blocks):
    lane = lane_ids(blocks[0].shape[0])
    rolled = [pltpu.roll(v, 1, 1) for v in blocks]
    return [jnp.where(lane == 0, rolled[(b + BLK - 1) % BLK], rolled[b]) for b in range(BLK)]


def load(ref, start, rows):
    return [ref[b, pl.ds(start, rows), :] for b in range(BLK)]


def store(ref, start, rows, blocks):
    for b in range(BLK):
        ref[b, pl.ds(start, rows), :] = blocks[b]


def for_strips(fn):
    fn(HY - 8, 8)

    def step(i, carry):
        fn(pl.multiple_of(HY + i * STEP, 8), STEP)
        return carry

    lax.fori_loop(0, NY // STEP, step, 0)
    fn(HY + NY, 8)


def clear_ends(ref):
    zero = jnp.zeros((8, LANES), F32)
    for b in range(BLK):
        ref[b, 0:8, :] = zero
        ref[b, ROWS - 8 : ROWS, :] = zero


def operate(v_ref, east_ref, west_ref, north_ref, shift_ref, start, rows):
    here = load(v_ref, start, rows)
    up, down = load(v_ref, start + 1, rows), load(v_ref, start - 1, rows)
    right, left = east_of(here), west_of(here)
    ef, wf = load(east_ref, start, rows), load(west_ref, start, rows)
    nf, sf = load(north_ref, start, rows), load(north_ref, start - 1, rows)
    shift = shift_ref[pl.ds(start, rows), :]
    out = [
        shift * here[b]
        + ef[b] * (here[b] - right[b])
        + wf[b] * (here[b] - left[b])
        + nf[b] * (here[b] - up[b])
        + sf[b] * (here[b] - down[b])
        for b in range(BLK)
    ]
    return here, out


def fold(x):
    return jnp.sum(x.reshape(-1, 8, LANES), axis=0)


def total(x):
    return jnp.sum(jnp.sum(x, axis=1, keepdims=True), axis=0, keepdims=True)


def own_row(tile_ref, values, scalars=()):
    lane = lane_ids(1)
    base = (tile_ref[0] % SLOTS) * 8
    other = ((tile_ref[0] + SLOTS // 2) % SLOTS) * 8
    row = jnp.zeros((1, LANES), F32)
    for k, value in enumerate(values):
        row = jnp.where(lane == base + k, value, row)
    for k, value in enumerate(scalars):
        row = jnp.where(lane == other + k, value, row)
    return row


def own_row_sums(got_ref, count):
    rows = got_ref.shape[0]
    lane = lane_ids(rows)
    slot = lax.broadcasted_iota(jnp.int32, (rows, LANES), 0) % SLOTS
    other = ((slot + SLOTS // 2) % SLOTS) * 8
    got = got_ref[...]
    return [total(fold(jnp.where(lane == other + k, got, 0.0))) for k in range(count)]


def fill_rows(ref, row):
    ref[...] = jnp.broadcast_to(row, ref.shape)


def pack_kernel(tile_ref, rhs_ref, depth_ref, mask_ref, basis_ref, inverse_ref, gather_ref, west_ref, east_ref):
    groups = inverse_ref.shape[1] // LANES
    lane = lane_ids(STEP)
    sums = []
    for g in range(AGG_LAT):

        def step(i, carry, g=g):
            start = pl.multiple_of(g * BAND + i * STEP, 8)
            out_row = pl.multiple_of(i * STEP, 8)
            accs = []
            fields = []
            for b in range(AGG_LON):
                at = (pl.ds(start, STEP), pl.ds(b * LANES, LANES))
                mask = mask_ref[at].astype(F32)
                wet = depth_ref[at] * mask
                res = rhs_ref[at] * mask
                weight = basis_ref[at] * mask
                accs.append(carry[b] + fold(weight * res))
                fields.append((wet, res, weight))
            for ref, b, extra in ((west_ref, 0, 0), (east_ref, 1, WX)):
                if g == 0:
                    packed = jnp.zeros((STEP, LANES), F32)
                else:
                    packed = ref[pl.ds(out_row, STEP), :]
                for f in range(3):
                    lo = 32 * g + WX * f
                    moved = pltpu.roll(fields[b][f], (lo + extra) % LANES, 1)
                    packed = jnp.where((lane >= lo) & (lane < lo + WX), moved, packed)
                ref[pl.ds(out_row, STEP), :] = packed
            return tuple(accs)

        zero = jnp.zeros((8, LANES), F32)
        for acc in lax.fori_loop(0, BAND // STEP, step, (zero,) * AGG_LON):
            sums.append(total(acc))
    fill_rows(gather_ref, own_row(tile_ref, sums))
    for g in range(groups):
        part = inverse_ref[:, g * LANES : (g + 1) * LANES]
        west_ref[BAND + 8 * g : BAND + 8 * g + 8, :] = part
        east_ref[BAND + 8 * g : BAND + 8 * g + 8, :] = part


def unpack_columns(left_ref, right_ref, g, start, rows):
    lane = lane_ids(rows)
    left, right = left_ref[pl.ds(start, rows), :], right_ref[pl.ds(start, rows), :]
    out = []
    for f in range(3):
        lo = 32 * g + WX * f
        from_right = pltpu.roll(right, (LANES - lo) % LANES, 1)
        from_left = pltpu.roll(left, (2 * LANES - lo - WX) % LANES, 1)
        out.append(jnp.where(lane < WX, from_right, jnp.where(lane >= LANES - WX, from_left, 0.0)))
    return out


def own_fields(rhs_ref, depth_ref, mask_ref, basis_ref, start, rows, b):
    at = (pl.ds(start, rows), pl.ds(b * LANES, LANES))
    mask = mask_ref[at].astype(F32)
    return depth_ref[at] * mask, rhs_ref[at] * mask, basis_ref[at] * mask


def edge_kernel(rhs_ref, depth_ref, mask_ref, basis_ref, inverse_ref, left_ref, right_ref, south_ref, north_ref):
    groups = inverse_ref.shape[1] // LANES
    sub = lax.broadcasted_iota(jnp.int32, (8, LANES), 0)
    for ref, start, g, band in ((south_ref, 0, 0, 0), (north_ref, NY - HY, AGG_LAT - 1, AGG_LAT - 1)):
        blocks = [own_fields(rhs_ref, depth_ref, mask_ref, basis_ref, start, HY, b) for b in range(2)]
        blocks.append(unpack_columns(left_ref, right_ref, g, start % BAND, HY))
        for f in range(3):
            for b in range(BLK):
                at = (f * BLK + b) * HY
                ref[at : at + HY, :] = blocks[b][f]
        base = 3 * BLK * HY
        for i in range(groups):
            own = inverse_ref[:, i * LANES : (i + 1) * LANES]
            left = left_ref[BAND + 8 * i : BAND + 8 * i + 8, :]
            right = right_ref[BAND + 8 * i : BAND + 8 * i + 8, :]
            own = pltpu.roll(own, (8 - 2 * band) % 8, 0) if band else own
            left = pltpu.roll(left, (2 - 2 * band - 1 + 16) % 8, 0)
            right = pltpu.roll(right, (3 - 2 * band + 16) % 8, 0)
            picked = jnp.where(sub < 2, own, jnp.where(sub == 2, left, right))
            ref[base + 8 * i : base + 8 * i + 8, :] = picked


def smooth(res_ref, inv_ref, ops, est_refs, step_ref, finish):
    first, pairs = chebyshev_plan(SWEEPS)

    def start_strip(start, rows):
        inv, res = load(inv_ref, start, rows), load(res_ref, start, rows)
        value = [first * (inv[b] * res[b]) for b in range(BLK)]
        store(step_ref, start, rows, value)
        store(est_refs[0], start, rows, value)

    for_strips(start_strip)
    for k, (c1, c2) in enumerate(pairs):
        src, dst = est_refs[k % 2], est_refs[(k + 1) % 2]

        def strip(start, rows, src=src, dst=dst, c1=c1, c2=c2, last=k == len(pairs) - 1):
            here, applied = operate(src, *ops, start, rows)
            inv, res, step = load(inv_ref, start, rows), load(res_ref, start, rows), load(step_ref, start, rows)
            step = [c1 * step[b] + c2 * (inv[b] * (res[b] - applied[b])) for b in range(BLK)]
            value = [here[b] + step[b] for b in range(BLK)]
            if last:
                finish(start, rows, value)
            else:
                store(step_ref, start, rows, step)
                store(dst, start, rows, value)

        for_strips(strip)


def setup_kernel(
    rhs_ref, depth_ref, mask_ref, basis_ref, left_ref, right_ref, below_ref, above_ref, geo_ref,
    east_ref, west_ref, north_ref, inv_ref, basis_out, res_ref, smooth_ref,
    wet_ref, est_a, est_b, step_ref,
):
    outs = (wet_ref, res_ref, basis_out)
    for f, ref in enumerate(outs):
        for b in range(BLK):
            at = (f * BLK + b) * HY
            ref[b, 0:HY, :] = below_ref[at : at + HY, :]
            ref[b, HY + NY : ROWS, :] = above_ref[at : at + HY, :]
    for g in range(AGG_LAT):

        def fill(i, carry, g=g):
            start = pl.multiple_of(g * BAND + i * STEP, 8)
            for b in range(2):
                for f, value in enumerate(own_fields(rhs_ref, depth_ref, mask_ref, basis_ref, start, STEP, b)):
                    outs[f][b, pl.ds(HY + start, STEP), :] = value
            part = pl.multiple_of(i * STEP, 8)
            for f, value in enumerate(unpack_columns(left_ref, right_ref, g, part, STEP)):
                outs[f][2, pl.ds(HY + start, STEP), :] = value
            return carry

        lax.fori_loop(0, BAND // STEP, fill, 0)

    def east_west(start, rows):
        wet = load(wet_ref, start, rows)
        over = geo_ref[0, pl.ds(start, rows), :]
        nxt = east_of(wet)
        face = [jnp.minimum(wet[b], nxt[b]) * over for b in range(BLK)]
        store(east_ref, start, rows, face)
        store(west_ref, start, rows, west_of(face))

    def north(start, rows):
        wet, nxt = load(wet_ref, start, rows), load(wet_ref, start + 1, rows)
        cosine = geo_ref[1, pl.ds(start, rows), :]
        store(north_ref, start, rows, [jnp.minimum(wet[b], nxt[b]) * cosine for b in range(BLK)])

    for_strips(east_west)
    north(0, 8)
    for_strips(north)
    shift_ref = geo_ref.at[2]

    def diagonal(start, rows):
        ef, wf = load(east_ref, start, rows), load(west_ref, start, rows)
        nf, sf = load(north_ref, start, rows), load(north_ref, start - 1, rows)
        shift = shift_ref[pl.ds(start, rows), :]
        store(inv_ref, start, rows, [1.0 / (shift + ef[b] + wf[b] + nf[b] + sf[b]) for b in range(BLK)])

    for_strips(diagonal)
    for ref in (est_a, est_b, smooth_ref):
        clear_ends(ref)

    def finish(start, rows, value):
        wet = load(wet_ref, start, rows)
        store(smooth_ref, start, rows, [jnp.where(wet[b] > 0.0, value[b], 0.0) for b in range(BLK)])

    smooth(res_ref, inv_ref, (east_ref, west_ref, north_ref, shift_ref), (est_a, est_b), step_ref, finish)


def coarse_solve(got_ref, inverse_ref, left_ref, right_ref, below_ref, above_ref):
    groups = inverse_ref.shape[1] // LANES
    count = got_ref.shape[0] // groups
    base = 3 * BLK * HY
    accs = [jnp.zeros((8, LANES), F32) for _ in range(5)]
    mine = lane_ids(count) // 8 == lax.broadcasted_iota(jnp.int32, (count, LANES), 0)
    for i in range(groups):
        vec = jnp.sum(jnp.where(mine, got_ref[i * count : (i + 1) * count, :], 0.0), axis=0, keepdims=True)
        at = slice(BAND + 8 * i, BAND + 8 * i + 8)
        band = slice(base + 8 * i, base + 8 * i + 8)
        parts = (
            inverse_ref[:, i * LANES : (i + 1) * LANES],
            left_ref[at, :],
            right_ref[at, :],
            below_ref[band, :],
            above_ref[band, :],
        )
        accs = [acc + part * vec for acc, part in zip(accs, parts)]
    own, left, right, below, above = [jnp.sum(acc, axis=1, keepdims=True) for acc in accs]
    low = lane_ids(1) < LANES // 2

    def spread(value):
        return jnp.broadcast_to(value, (1, LANES))

    def edge(x):
        halo = jnp.where(low, spread(x[3:4]), spread(x[2:3]))
        return [spread(x[0:1]), spread(x[1:2]), halo]

    rows = [edge(below)]
    for a in range(AGG_LAT):
        halo = jnp.where(low, spread(right[2 * a : 2 * a + 1]), spread(left[2 * a + 1 : 2 * a + 2]))
        rows.append([spread(own[2 * a : 2 * a + 1]), spread(own[2 * a + 1 : 2 * a + 2]), halo])
    rows.append(edge(above))
    return rows


def for_bands(fn, carry_of=None):
    out = []
    fn(0, HY, 0, None)
    for a in range(AGG_LAT):

        def step(i, carry, a=a):
            return fn(pl.multiple_of(HY + a * BAND + i * STEP, 8), STEP, a + 1, carry)

        out.append(lax.fori_loop(0, BAND // STEP, step, carry_of))
    fn(HY + NY, HY, AGG_LAT + 1, None)
    return out


def search_kernel(
    tile_ref, got_ref, inverse_ref, left_ref, right_ref, below_ref, above_ref,
    east_ref, west_ref, north_ref, basis_ref, smooth_ref, geo_ref, res_ref,
    send_ref, search_ref, applied_ref,
):
    coarse = coarse_solve(got_ref, inverse_ref, left_ref, right_ref, below_ref, above_ref)

    def direction(start, rows, band, carry):
        part, weight = load(smooth_ref, start, rows), load(basis_ref, start, rows)
        store(search_ref, start, rows, [part[b] + weight[b] * coarse[band][b] for b in range(BLK)])
        return 0

    for_bands(direction, 0)
    ops = (east_ref, west_ref, north_ref, geo_ref.at[2])
    clear_ends(applied_ref)

    def apply(start, rows):
        here, out = operate(search_ref, *ops, start, rows)
        store(applied_ref, start, rows, out)
        return here, out

    apply(HY - 8, 8)
    sums = []
    zero = jnp.zeros((8, LANES), F32)
    curvature, projection = zero, zero
    for a in range(AGG_LAT):

        def step(i, carry, a=a):
            start = pl.multiple_of(HY + a * BAND + i * STEP, 8)
            here, out = apply(start, STEP)
            accs = [carry[b] + fold(basis_ref[b, pl.ds(start, STEP), :] * out[b]) for b in range(AGG_LON)]
            curvature, projection = carry[AGG_LON:]
            for b in range(AGG_LON):
                curvature = curvature + fold(here[b] * out[b])
                projection = projection + fold(here[b] * res_ref[b, pl.ds(start, STEP), :])
            return (*accs, curvature, projection)

        *accs, curvature, projection = lax.fori_loop(
            0, BAND // STEP, step, (zero,) * AGG_LON + (curvature, projection)
        )
        sums += [total(x) for x in accs]
    apply(HY + NY, 8)
    fill_rows(send_ref, own_row(tile_ref, sums, (total(curvature), total(projection))))


def second_kernel(
    applied_ref, inv_ref, east_ref, west_ref, north_ref, basis_ref, geo_ref,
    out_ref, est_a, est_b, step_ref,
):
    for ref in (est_a, est_b, out_ref):
        clear_ends(ref)

    def finish(start, rows, value):
        weight = load(basis_ref, start, rows)
        store(out_ref, start, rows, [jnp.where(weight[b] > 0.0, value[b], 0.0) for b in range(BLK)])

    smooth(applied_ref, inv_ref, (east_ref, west_ref, north_ref, geo_ref.at[2]), (est_a, est_b), step_ref, finish)


def sums_kernel(
    got_ref, inverse_ref, left_ref, right_ref, below_ref, above_ref,
    east_ref, west_ref, north_ref, basis_ref, smooth_ref, geo_ref, search_ref, applied_ref, res_ref,
    send_ref, known_ref, update_ref, operated_ref, rest_ref, full_ref,
):
    coarse = coarse_solve(got_ref, inverse_ref, left_ref, right_ref, below_ref, above_ref)
    curvature, projection = own_row_sums(got_ref, 2)
    lane = lane_ids(1)
    alpha = jnp.broadcast_to(projection, (1, LANES)) / jnp.broadcast_to(curvature, (1, LANES))
    known_ref[...] = jnp.broadcast_to(jnp.where(lane == 0, curvature, alpha), (8, LANES))

    def build(start, rows, band, carry):
        part, weight = load(smooth_ref, start, rows), load(basis_ref, start, rows)
        search = load(search_ref, start, rows)
        store(
            full_ref, start, rows,
            [search[b] - alpha * (part[b] + weight[b] * coarse[band][b]) for b in range(BLK)],
        )
        return 0

    for_bands(build, 0)
    ops = (east_ref, west_ref, north_ref, geo_ref.at[2])

    def step(i, carry):
        start = pl.multiple_of(HY + i * STEP, 8)
        own = pl.ds(pl.multiple_of(i * STEP, 8), STEP)
        here, out = operate(full_ref, *ops, start, STEP)
        search, applied, res = load(search_ref, start, STEP), load(applied_ref, start, STEP), load(res_ref, start, STEP)
        carry = list(carry)
        for b in range(AGG_LON):
            rest = res[b] - alpha * applied[b]
            update_ref[b, own, :] = here[b]
            operated_ref[b, own, :] = out[b]
            rest_ref[b, own, :] = rest
            pairs = ((here[b], applied[b]), (here[b], out[b]), (here[b], rest), (search[b], rest))
            carry = [acc + fold(x * y) for acc, (x, y) in zip(carry, pairs)]
        return tuple(carry)

    zero = jnp.zeros((8, LANES), F32)
    accs = lax.fori_loop(0, NY // STEP, step, (zero,) * 4)
    row = jnp.zeros((1, LANES), F32)
    for k, acc in enumerate(accs):
        row = jnp.where(lane == k, total(acc), row)
    fill_rows(send_ref, row)


def final_kernel(got_ref, known_ref, search_ref, applied_ref, update_ref, operated_ref, rest_ref, field_ref, out_ref):
    sums = jnp.sum(got_ref[...], axis=0, keepdims=True)
    lane = lane_ids(1)

    def pick(row, k):
        return jnp.broadcast_to(jnp.sum(jnp.where(lane == k, row, 0.0), axis=1, keepdims=True), (1, LANES))

    u_ap, u_au, u_r, p_r = [pick(sums, k) for k in range(4)]
    p_ap, alpha = pick(known_ref[0:1, :], 0), pick(known_ref[0:1, :], 1)
    beta = -u_ap / p_ap
    curvature = u_au + 2.0 * beta * u_ap + beta * beta * p_ap
    step_size = (u_r + beta * p_r) / curvature
    along = alpha + step_size * beta
    back = step_size * beta

    def step(i, carry):
        start = pl.multiple_of(i * STEP, 8)
        own, halo = pl.ds(start, STEP), pl.ds(pl.multiple_of(HY + i * STEP, 8), STEP)
        for b in range(AGG_LON):
            at = (own, pl.ds(b * LANES, LANES))
            field_ref[at] = along * search_ref[b, halo, :] + step_size * update_ref[b, own, :]
            out_ref[at] = rest_ref[b, own, :] - step_size * operated_ref[b, own, :] - back * applied_ref[b, halo, :]
        return carry

    lax.fori_loop(0, NY // STEP, step, 0)


def call(kernel, outs, scratch=(), scalars=0, ins=0, flops=0):
    specs = [pl.BlockSpec(memory_space=pltpu.SMEM)] * scalars + [pl.BlockSpec(memory_space=pltpu.VMEM)] * ins
    return pl.pallas_call(
        kernel,
        out_shape=[jax.ShapeDtypeStruct(s, F32) for s in outs],
        in_specs=specs,
        out_specs=[pl.BlockSpec(memory_space=pltpu.VMEM)] * len(outs),
        scratch_shapes=[pltpu.VMEM(s, F32) for s in scratch],
        compiler_params=pltpu.CompilerParams(vmem_limit_bytes=40 * 1024 * 1024),
        cost_estimate=pl.CostEstimate(flops=flops, bytes_accessed=4 * 1024 * 1024, transcendentals=0),
    )


def exchange(x):
    return lax.all_to_all(x, AXES, 0, 0, tiled=True)


def body(rhs, depth, mask, basis, inverse):
    n_lon, n_lat = lax.axis_size("lon"), lax.axis_size("lat")
    devices = n_lon * n_lat
    total_rows = NY * n_lat
    lat = lax.axis_index("lat")
    tile = (lax.axis_index("lon") * n_lat + lat).astype(jnp.int32).reshape(1)
    full = (BLK, ROWS, LANES)
    half = (AGG_LON, NY, LANES)
    rows8 = 8 * (inverse.shape[1] // LANES)
    own = (rhs, depth, mask, basis)

    row_index = lat * NY - HY + jnp.arange(ROWS, dtype=jnp.int32)
    latitude = (row_index.astype(F32) + 0.5) * (2.6 / total_rows) - 1.3
    inside = ((row_index >= 0) & (row_index <= total_rows - 2)).astype(F32)
    geo = jnp.stack(
        [1.0 / jnp.cos(latitude), jnp.cos(latitude + 1.3 / total_rows) * inside, SHIFT_SCALE * jnp.cos(latitude)]
    )
    geo = jnp.broadcast_to(geo[:, :, None], (3, ROWS, LANES))

    gather, to_west, to_east = call(
        pack_kernel, [(devices, LANES), (BAND + rows8, LANES), (BAND + rows8, LANES)], scalars=1, ins=5
    )(tile, *own, inverse)
    ring = [(i, (i + 1) % n_lon) for i in range(n_lon)]
    left = lax.ppermute(to_east, "lon", ring)
    right = lax.ppermute(to_west, "lon", [(j, i) for i, j in ring])
    got = exchange(gather)
    edge_rows = 3 * BLK * HY + rows8
    to_south, to_north = call(edge_kernel, [(edge_rows, LANES)] * 2, ins=7)(*own, inverse, left, right)
    line = [(i, i + 1) for i in range(n_lat - 1)]
    below = lax.ppermute(to_north, "lat", line)
    above = lax.ppermute(to_south, "lat", [(j, i) for i, j in line])

    east, west, north, inv, weight, res, smoothed = call(
        setup_kernel, [full] * 7, scratch=[full] * 4, ins=9, flops=40000000
    )(*own, left, right, below, above, geo)
    solver = (inverse, left, right, below, above)
    faces = (east, west, north, weight)
    send, search, applied = call(search_kernel, [(devices, LANES), full, full], scalars=1, ins=13, flops=8000000)(
        tile, got, *solver, *faces, smoothed, geo, res
    )
    got = exchange(send)
    (smoothed,) = call(second_kernel, [full], scratch=[full] * 3, ins=7, flops=20000000)(applied, inv, *faces, geo)
    send, known, *second = call(
        sums_kernel, [(devices, LANES), (8, LANES), half, half, half], scratch=[full], ins=15, flops=8000000
    )(got, *solver, *faces, smoothed, geo, search, applied, res)
    got = exchange(send)
    field, out = call(final_kernel, [(NY, NX)] * 2, ins=7, flops=1000000)(got, known, search, applied, *second)
    return field, out


def solution(mesh):
    tile = P("lat", "lon")
    return jax.shard_map(
        body,
        mesh=mesh,
        in_specs=(tile, tile, tile, tile, P(AXES, None)),
        out_specs=(tile, tile),
        check_vma=False,
    )
```

time: 555 us -> 132 us (0.24)
  blocking collectives: 376 us -> 24.8 us
  waiting for transfers between devices: 71.4 us -> 6.44 us
  other arithmetic: 38.3 us -> 0.27 us
  Pallas kernels: 0 us -> 27.2 us
  local copies, waits for them, and re-layouts: 11.2 us -> 32.4 us
  starting transfers between devices: 52 us -> 39 us
    psum x3 -> x0, blocking collectives: 221 us -> none  [the longest x2 148 us: body(): lax.psum((jnp.sum(search * applied_search), jnp.sum(search * residual)),...]
    unnamed x2 -> x0, blocking collectives: 155 us -> none
    ppermute x36 -> x4, waiting for transfers between devices: 71.4 us -> 4.81 us  [the longest x1 4.53 us: body(): above = lax.ppermute(to_south, 'lat', [(j, i) for i, j in line])]
    ppermute x36 -> x4, starting transfers between devices: 52 us -> 14.2 us  [the longest x1 6.14 us: body(): right = lax.ppermute(to_west, 'lon', [(j, i) for i, j in ring])]
    unnamed x40 -> x88, local copies, waits for them, and re-layouts: 3.51 us -> 32.1 us
    pallas_call x0 -> x7, Pallas kernels: none -> 27.2 us  [the longest x1 10.9 us: body(): call(setup_kernel, [full] * 7, scratch=[full] * 4, ins=9, flops=40000000)]
    all_to_all x0 -> x2, starting transfers between devices: none -> 24.8 us  [exchange(): return lax.all_to_all(x, AXES, 0, 0, tiled=True)]
    all_to_all x0 -> x1, blocking collectives: none -> 24.8 us  [exchange(): return lax.all_to_all(x, AXES, 0, 0, tiled=True)]
  transfers between devices with their start and end apart: 36 -> 6, of which waited for: 23 -> 3; matrix products, arithmetic and copies ran while one was open for 2% -> 0% of each run, Pallas kernels for 0% -> 13%
where the time goes in v1:
time: 132 us; the launch traced here: 131 us
  starting transfers between devices  39 us (30%)
  local copies, waits for them, and re-layouts  32.4 us (25%)
  Pallas kernels  27.2 us (21%)
  blocking collectives  24.8 us (19%)
  waiting for transfers between devices  6.44 us (5%)
    unnamed x88, local copies, waits for them, and re-layouts  32.1 us
    all_to_all x2, starting transfers between devices, exchange(): return lax.all_to_all(x, AXES, 0, 0, tiled=True)  24.8 us
    all_to_all x1, blocking collectives, exchange(): return lax.all_to_all(x, AXES, 0, 0, tiled=True)  24.8 us
    pallas_call x1, Pallas kernels, body(): call(setup_kernel, [full] * 7, scratch=[full] * 4, ins=9, flops=40000000)  10.9 us
    pallas_call x1, Pallas kernels, body(): call(second_kernel, [full], scratch=[full] * 3, ins=7, flops=20000000)  6.15 us
    ppermute x1, starting transfers between devices, body(): right = lax.ppermute(to_west, 'lon', [(j, i) for i, j in ring])  6.14 us
    ppermute x1, waiting for transfers between devices, body(): above = lax.ppermute(to_south, 'lat', [(j, i) for i, j in line])  4.53 us
    ppermute x1, starting transfers between devices, body(): below = lax.ppermute(to_north, 'lat', line)  3.66 us
  transfers between devices with their start and end apart: 6, of which 3 were waited for; matrix products, arithmetic and copies ran while one was open for 0% of the time, Pallas kernels for 13%

profile of v1, /device:TPU:1, one launch (start us, length us, event | category | flops | bytes accessed | tf_op | source)
XLA Modules:
  0.0 131.0 jit_solution(12255486107228597571)
XLA Ops:
  5.7 2.3 %shard_map.68 = (f32[256,128]{1,0:T(8,128)}, f32[256,128]{1,0:T(8,128)S(1)}, f32[256,128]{1,0:T(8,128)S(1)}) custom-call(s32[1]{0:T(128)} %bitcast.tile_ref, f32[512,256]{1,0:T(8,128)S(1)} %copy-done.8, f32[512,256]{1,0:T(8,128)S(1)} %copy-done.11, s32[512,256]{1,0:T(8,128)S(1)} %copy-done.14, f32[512,256]{1,0:T(8,128)S(1)} %copy-done.17, ...), custom_call_target="tpu_custom_call" | custom-call | bytes 4194304 | tf_op jit(solution)/shard_map/pallas_call | solution.py:523
  8.0 2.5 %collective-permute-start = (f32[256,128]{1,0:T(8,128)S(1)}, f32[256,128]{1,0:T(8,128)S(1)}, u32[]{:S(2)}, u32[]{:S(2)}) collective-permute-start(f32[256,128]{1,0:T(8,128)S(1)} %get-tuple-element.23), channel_id=1, source_target_pairs={{0,8},{8,16},{16,24},{24,32},{32,40},{40,48},{48,56},{56,64},{64,7... | collective-permute-start | bytes 393224 | tf_op jit(solution)/shard_map/ppermute | solution.py:527
  10.5 6.1 %collective-permute-start.1 = (f32[256,128]{1,0:T(8,128)S(1)}, f32[256,128]{1,0:T(8,128)S(1)}, u32[]{:S(2)}, u32[]{:S(2)}) collective-permute-start(f32[256,128]{1,0:T(8,128)S(1)} %get-tuple-element.24), channel_id=1, source_target_pairs={{8,0},{16,8},{24,16},{32,24},{40,32},{48,40},{56,48},{64,56},{72,6... | collective-permute-start | bytes 393224 | tf_op jit(solution)/shard_map/ppermute | solution.py:528
  16.6 11.3 %all-to-all-start = ((f32[256,1,128]{2,1,0:T(1,128)}), f32[256,1,128]{2,1,0:T(1,128)}, u32[]{:S(2)}, u32[]{:S(2)}) async-start(f32[256,1,128]{2,1,0:T(1,128)} %bitcast.2), calls=%async_computation | async-start | bytes 262144 | tf_op jit(solution)/shard_map/all_to_all | solution.py:501
  28.8 3.7 %collective-permute-start.2 = (f32[272,128]{1,0:T(8,128)S(1)}, f32[272,128]{1,0:T(8,128)S(1)}, u32[]{:S(2)}, u32[]{:S(2)}) collective-permute-start(f32[272,128]{1,0:T(8,128)S(1)} %get-tuple-element.25), channel_id=1, source_target_pairs={{0,1},{1,2},{2,3},{3,4},{4,5},{5,6},{6,7},{8,9},{9,10},{10,11},{11... | collective-permute-start | bytes 417800 | tf_op jit(solution)/shard_map/ppermute | solution.py:533
  32.5 1.9 %collective-permute-start.3 = (f32[272,128]{1,0:T(8,128)S(1)}, f32[272,128]{1,0:T(8,128)S(1)}, u32[]{:S(2)}, u32[]{:S(2)}) collective-permute-start(f32[272,128]{1,0:T(8,128)S(1)} %get-tuple-element.26), channel_id=1, source_target_pairs={{1,0},{2,1},{3,2},{4,3},{5,4},{6,5},{7,6},{9,8},{10,9},{11,10},{12... | collective-permute-start | bytes 417800 | tf_op jit(solution)/shard_map/ppermute | solution.py:534
  34.8 4.5 %collective-permute-done.3.above_ref = f32[272,128]{1,0:T(8,128)S(1)} collective-permute-done((f32[272,128]{1,0:T(8,128)S(1)}, f32[272,128]{1,0:T(8,128)S(1)}, u32[]{:S(2)}, u32[]{:S(2)}) %collective-permute-start.3) | collective-permute-done | bytes 139296 | tf_op jit(solution)/shard_map/ppermute | solution.py:534
  40.0 10.9 %shard_map.70 = (f32[3,544,128]{2,1,0:T(8,128)S(1)}, f32[3,544,128]{2,1,0:T(8,128)S(1)}, f32[3,544,128]{2,1,0:T(8,128)S(1)}, f32[3,544,128]{2,1,0:T(8,128)S(1)},...) custom-call(f32[512,256]{1,0:T(8,128)S(1)} %copy-done.10, ...), custom_call_target="tpu_custom_call" | custom-call | flops 40000000 | bytes 4194304 | tf_op jit(solution)/shard_map/pallas_call | solution.py:536
  55.5 1.1 copy-done.1
  56.6 1.1 copy-done.5
  62.8 3.3 %shard_map.71 = (f32[256,128]{1,0:T(8,128)S(1)}, f32[3,544,128]{2,1,0:T(8,128)S(1)}, f32[3,544,128]{2,1,0:T(8,128)S(1)}) custom-call(s32[1]{0:T(128)} %bitcast.tile_ref, f32[256,128]{1,0:T(8,128)} %bitcast.3.got_ref, f32[8,2048]{1,0:T(8,128)S(1)} %copy-done.38, f32[256,128]{1,0:T(8,128)S(1)} %collective-permute-done.left_ref, f32[256,128]{1,0:T(8,128)S(1)} %copy-done.29, ...), custom_call_target="tpu_custom_call" | custom-call | flops 8000000 | bytes 4194304 | tf_op jit(solution)/shard_map/pallas_call | solution.py:541
  67.6 13.5 %all-to-all-start.1 = ((f32[256,1,128]{2,1,0:T(1,128)}), f32[256,1,128]{2,1,0:T(1,128)}, u32[]{:S(2)}, u32[]{:S(2)}) async-start(f32[256,1,128]{2,1,0:T(1,128)} %bitcast.15), calls=%async_computation.1 | async-start | bytes 262144 | tf_op jit(solution)/shard_map/all_to_all | solution.py:501
  82.3 1.1 copy-done.6
  83.5 1.1 copy-done.40
  84.6 6.1 %shard_map.72.smooth_ref = f32[3,544,128]{2,1,0:T(8,128)S(1)} custom-call(f32[3,544,128]{2,1,0:T(8,128)S(1)} %get-tuple-element.34.applied_ref, f32[3,544,128]{2,1,0:T(8,128)S(1)} %copy-done.40, f32[3,544,128]{2,1,0:T(8,128)S(1)} %get-tuple-element.27.east_ref, f32[3,544,128]{2,1,0:T(8,128)S(1)} %get-tuple-element.28.west_ref, f32[3,544,128]{2,1,0:T(8,128)S(1)} %copy-done.2, ...), custom_call_target="tpu_custom_call" | custom-call | flops 20000000 | bytes 4194304 | tf_op jit(solution)/shard_map/pallas_call | solution.py:545
  91.7 1.6 %all-to-all-done.1 = f32[256,1,128]{2,1,0:T(1,128)} async-done(((f32[256,1,128]{2,1,0:T(1,128)}), f32[256,1,128]{2,1,0:T(1,128)}, u32[]{:S(2)}, u32[]{:S(2)}) %all-to-all-start.1) | async-done | bytes 131104 | tf_op jit(solution)/shard_map/all_to_all | solution.py:501
  93.3 1.1 copy-done.3
  94.5 1.1 copy-done.7
  95.6 1.1 copy-done.21
  96.8 1.1 copy-done.23
  97.9 1.1 copy-done.26
  101.8 3.1 %shard_map.73 = (f32[256,128]{1,0:T(8,128)S(1)}, f32[8,128]{1,0:T(8,128)S(1)}, f32[2,512,128]{2,1,0:T(8,128)S(1)}, f32[2,512,128]{2,1,0:T(8,128)S(1)}, f32[2,512,128]{2,1,0:T(8,128)S(1)}) custom-call(f32[256,128]{1,0:T(8,128)} %bitcast.6.got_ref, f32[8,2048]{1,0:T(8,128)S(1)} %copy-done.38, f32[256,128]{1,0:T(8,128)S(1)} %collective-permute-done.left_ref, ...), custom_call_target="tpu_custom_call" | custom-call | flops 8000000 | bytes 4194304 | tf_op jit(solution)/shard_map/pallas_call | solution.py:546
  104.9 24.8 %all_to_all.33 = f32[256,1,128]{2,1,0:T(1,128)S(1)} all-to-all(f32[256,1,128]{2,1,0:T(1,128)S(1)} %bitcast.14), channel_id=1, replica_groups=mesh['lon'=32,'lat'=8] {'lon','lat'}, dimensions={0} | all-to-all | bytes 262144 | tf_op jit(solution)/shard_map/all_to_all | solution.py:501
  129.7 1.3 shard_map.74
  (88 shorter events, 22.7 us)
Async XLA Ops:
  5.6 22.5 %copy-start.9 = (f32[512,256]{1,0:T(8,128)S(1)}, f32[512,256]{1,0:T(8,128)}, u32[]{:S(2)}) copy-start(f32[512,256]{1,0:T(8,128)} %rhs_ref.5) | copy-start | bytes 1572868
  5.6 22.5 %copy-start.12 = (f32[512,256]{1,0:T(8,128)S(1)}, f32[512,256]{1,0:T(8,128)}, u32[]{:S(2)}) copy-start(f32[512,256]{1,0:T(8,128)} %depth_ref.5) | copy-start | bytes 1572868
  5.7 22.5 %copy-start.15 = (s32[512,256]{1,0:T(8,128)S(1)}, s32[512,256]{1,0:T(8,128)}, u32[]{:S(2)}) copy-start(s32[512,256]{1,0:T(8,128)} %mask_ref.5) | copy-start | bytes 1572868
  5.7 22.5 %copy-start.18 = (f32[512,256]{1,0:T(8,128)S(1)}, f32[512,256]{1,0:T(8,128)}, u32[]{:S(2)}) copy-start(f32[512,256]{1,0:T(8,128)} %basis_ref.5) | copy-start | bytes 1572868
  8.0 20.1 %collective-permute-start = (f32[256,128]{1,0:T(8,128)S(1)}, f32[256,128]{1,0:T(8,128)S(1)}, u32[]{:S(2)}, u32[]{:S(2)}) collective-permute-start(f32[256,128]{1,0:T(8,128)S(1)} %get-tuple-element.23), channel_id=1, source_target_pairs={{0,8},{8,16},{16,24},{24,32},{32,40},{40,48},{48,56},{56,64},{64,7... | collective-permute-start | bytes 393224 | tf_op jit(solution)/shard_map/ppermute | solution.py:527
  10.5 17.6 %collective-permute-start.1 = (f32[256,128]{1,0:T(8,128)S(1)}, f32[256,128]{1,0:T(8,128)S(1)}, u32[]{:S(2)}, u32[]{:S(2)}) collective-permute-start(f32[256,128]{1,0:T(8,128)S(1)} %get-tuple-element.24), channel_id=1, source_target_pairs={{8,0},{16,8},{24,16},{32,24},{40,32},{48,40},{56,48},{64,56},{72,6... | collective-permute-start | bytes 393224 | tf_op jit(solution)/shard_map/ppermute | solution.py:528
  16.6 11.5 %copy-start.38 = (f32[8,2048]{1,0:T(8,128)S(1)}, f32[8,2048]{1,0:T(8,128)}, u32[]{:S(2)}) copy-start(f32[8,2048]{1,0:T(8,128)} %inverse_ref.7) | copy-start | bytes 196612
  16.6 38.8 %all-to-all-start = ((f32[256,1,128]{2,1,0:T(1,128)}), f32[256,1,128]{2,1,0:T(1,128)}, u32[]{:S(2)}, u32[]{:S(2)}) async-start(f32[256,1,128]{2,1,0:T(1,128)} %bitcast.2), calls=%async_computation | async-start | bytes 262144 | tf_op jit(solution)/shard_map/all_to_all | solution.py:501
  28.2 11.8 %copy-start.13 = (f32[512,256]{1,0:T(8,128)S(1)}, f32[512,256]{1,0:T(8,128)}, u32[]{:S(2)}) copy-start(f32[512,256]{1,0:T(8,128)} %depth_ref.5) | copy-start | bytes 1572868
  28.2 11.8 %copy-start.16 = (s32[512,256]{1,0:T(8,128)S(1)}, s32[512,256]{1,0:T(8,128)}, u32[]{:S(2)}) copy-start(s32[512,256]{1,0:T(8,128)} %mask_ref.5) | copy-start | bytes 1572868
  28.2 11.8 %copy-start.19 = (f32[512,256]{1,0:T(8,128)S(1)}, f32[512,256]{1,0:T(8,128)}, u32[]{:S(2)}) copy-start(f32[512,256]{1,0:T(8,128)} %basis_ref.5) | copy-start | bytes 1572868
  28.8 11.2 %copy-start.10 = (f32[512,256]{1,0:T(8,128)S(1)}, f32[512,256]{1,0:T(8,128)}, u32[]{:S(2)}) copy-start(f32[512,256]{1,0:T(8,128)} %rhs_ref.5) | copy-start | bytes 1572868
  28.8 6.0 %collective-permute-start.2 = (f32[272,128]{1,0:T(8,128)S(1)}, f32[272,128]{1,0:T(8,128)S(1)}, u32[]{:S(2)}, u32[]{:S(2)}) collective-permute-start(f32[272,128]{1,0:T(8,128)S(1)} %get-tuple-element.25), channel_id=1, source_target_pairs={{0,1},{1,2},{2,3},{3,4},{4,5},{5,6},{6,7},{8,9},{9,10},{10,11},{11... | collective-permute-start | bytes 417800 | tf_op jit(solution)/shard_map/ppermute | solution.py:533
  32.5 6.9 %collective-permute-start.3 = (f32[272,128]{1,0:T(8,128)S(1)}, f32[272,128]{1,0:T(8,128)S(1)}, u32[]{:S(2)}, u32[]{:S(2)}) collective-permute-start(f32[272,128]{1,0:T(8,128)S(1)} %get-tuple-element.26), channel_id=1, source_target_pairs={{1,0},{2,1},{3,2},{4,3},{5,4},{6,5},{7,6},{9,8},{10,9},{11,10},{12... | collective-permute-start | bytes 417800 | tf_op jit(solution)/shard_map/ppermute | solution.py:534
  34.5 5.5 %copy-start.28 = (f32[256,128]{1,0:T(8,128)S(1)}, f32[256,128]{1,0:T(8,128)}, u32[]{:S(2)}) copy-start(f32[256,128]{1,0:T(8,128)} %copy-done.27) | copy-start | bytes 393220
  34.8 4.8 %copy-start.31 = (f32[272,128]{1,0:T(8,128)}, f32[272,128]{1,0:T(8,128)S(1)}, u32[]{:S(2)}) copy-start(f32[272,128]{1,0:T(8,128)S(1)} %collective-permute-done.2.below_ref) | copy-start | bytes 417796
  55.4 1.2 copy-start.1
  56.6 1.1 copy-start.5
  57.8 1.1 copy-start.25
  61.6 1.1 copy-start.42
  67.6 25.7 %all-to-all-start.1 = ((f32[256,1,128]{2,1,0:T(1,128)}), f32[256,1,128]{2,1,0:T(1,128)}, u32[]{:S(2)}, u32[]{:S(2)}) async-start(f32[256,1,128]{2,1,0:T(1,128)} %bitcast.15), calls=%async_computation.1 | async-start | bytes 262144 | tf_op jit(solution)/shard_map/all_to_all | solution.py:501
  81.2 1.2 copy-start.2
  82.3 1.1 copy-start.6
  93.3 1.2 copy-start.3
  (26 other events, 24.5 us)

commit v2 on v1

--- a/solution.py
+++ b/solution.py
@@ -22,7 +22,8 @@
 LANES = 128
 BLK = 3
 BAND = NY // AGG_LAT
-STEP = 32
+STEP = 16
+SWEEP = 24
 SLOTS = LANES // 8
 AXES = ("lon", "lat")
 F32 = jnp.float32
@@ -67,14 +68,13 @@
 
 
 def for_strips(fn):
-    fn(HY - 8, 8)
-
-    def step(i, carry):
-        fn(pl.multiple_of(HY + i * STEP, 8), STEP)
-        return carry
-
-    lax.fori_loop(0, NY // STEP, step, 0)
-    fn(HY + NY, 8)
+    for start in range(8, ROWS - 8, SWEEP):
+        fn(start, min(SWEEP, ROWS - 8 - start))
+
+
+def for_own(fn):
+    for start in range(0, NY, STEP):
+        fn(start // BAND, start)
 
 
 def clear_ends(ref):
@@ -135,16 +135,31 @@
     ref[...] = jnp.broadcast_to(row, ref.shape)
 
 
-def pack_kernel(tile_ref, rhs_ref, depth_ref, mask_ref, basis_ref, inverse_ref, gather_ref, west_ref, east_ref):
+def pack_kernel(
+    tile_ref, rhs_hbm, depth_hbm, mask_hbm, basis_hbm, inverse_hbm,
+    gather_ref, west_ref, east_ref, wet_ref, res_ref, weight_ref,
+    rhs_ref, depth_ref, mask_ref, basis_ref, inverse_ref, sems,
+):
+    pairs = ((rhs_hbm, rhs_ref), (mask_hbm, mask_ref), (basis_hbm, basis_ref), (depth_hbm, depth_ref))
+    copies = []
+    for g in range(AGG_LAT):
+        at = pl.ds(g * BAND, BAND)
+        copies.append(
+            [pltpu.make_async_copy(src.at[at], dst.at[at], sems.at[4 * g + k]) for k, (src, dst) in enumerate(pairs)]
+        )
+    last = pltpu.make_async_copy(inverse_hbm, inverse_ref, sems.at[4 * AGG_LAT])
+    for copy in sum(copies, []) + [last]:
+        copy.start()
     groups = inverse_ref.shape[1] // LANES
     lane = lane_ids(STEP)
     sums = []
+    zero = jnp.zeros((8, LANES), F32)
     for g in range(AGG_LAT):
-
-        def step(i, carry, g=g):
-            start = pl.multiple_of(g * BAND + i * STEP, 8)
-            out_row = pl.multiple_of(i * STEP, 8)
-            accs = []
+        for copy in copies[g]:
+            copy.wait()
+        accs = [zero] * AGG_LON
+        for start in range(g * BAND, (g + 1) * BAND, STEP):
+            out_row = start - g * BAND
             fields = []
             for b in range(AGG_LON):
                 at = (pl.ds(start, STEP), pl.ds(b * LANES, LANES))
@@ -152,24 +167,20 @@
                 wet = depth_ref[at] * mask
                 res = rhs_ref[at] * mask
                 weight = basis_ref[at] * mask
-                accs.append(carry[b] + fold(weight * res))
+                accs[b] = accs[b] + fold(weight * res)
                 fields.append((wet, res, weight))
+                for ref, value in zip((wet_ref, res_ref, weight_ref), fields[b]):
+                    ref[b, HY + start : HY + start + STEP, :] = value
             for ref, b, extra in ((west_ref, 0, 0), (east_ref, 1, WX)):
-                if g == 0:
-                    packed = jnp.zeros((STEP, LANES), F32)
-                else:
-                    packed = ref[pl.ds(out_row, STEP), :]
+                packed = jnp.zeros((STEP, LANES), F32) if g == 0 else ref[out_row : out_row + STEP, :]
                 for f in range(3):
                     lo = 32 * g + WX * f
                     moved = pltpu.roll(fields[b][f], (lo + extra) % LANES, 1)
                     packed = jnp.where((lane >= lo) & (lane < lo + WX), moved, packed)
-                ref[pl.ds(out_row, STEP), :] = packed
-            return tuple(accs)
-
-        zero = jnp.zeros((8, LANES), F32)
-        for acc in lax.fori_loop(0, BAND // STEP, step, (zero,) * AGG_LON):
-            sums.append(total(acc))
+                ref[out_row : out_row + STEP, :] = packed
+        sums += [total(acc) for acc in accs]
     fill_rows(gather_ref, own_row(tile_ref, sums))
+    last.wait()
     for g in range(groups):
         part = inverse_ref[:, g * LANES : (g + 1) * LANES]
         west_ref[BAND + 8 * g : BAND + 8 * g + 8, :] = part
@@ -188,22 +199,15 @@
     return out
 
 
-def own_fields(rhs_ref, depth_ref, mask_ref, basis_ref, start, rows, b):
-    at = (pl.ds(start, rows), pl.ds(b * LANES, LANES))
-    mask = mask_ref[at].astype(F32)
-    return depth_ref[at] * mask, rhs_ref[at] * mask, basis_ref[at] * mask
-
-
-def edge_kernel(rhs_ref, depth_ref, mask_ref, basis_ref, inverse_ref, left_ref, right_ref, south_ref, north_ref):
+def edge_kernel(wet_ref, res_ref, weight_ref, inverse_ref, left_ref, right_ref, south_ref, north_ref):
     groups = inverse_ref.shape[1] // LANES
     sub = lax.broadcasted_iota(jnp.int32, (8, LANES), 0)
     for ref, start, g, band in ((south_ref, 0, 0, 0), (north_ref, NY - HY, AGG_LAT - 1, AGG_LAT - 1)):
-        blocks = [own_fields(rhs_ref, depth_ref, mask_ref, basis_ref, start, HY, b) for b in range(2)]
-        blocks.append(unpack_columns(left_ref, right_ref, g, start % BAND, HY))
-        for f in range(3):
+        halo = unpack_columns(left_ref, right_ref, g, start % BAND, HY)
+        for f, field in enumerate((wet_ref, res_ref, weight_ref)):
             for b in range(BLK):
                 at = (f * BLK + b) * HY
-                ref[at : at + HY, :] = blocks[b][f]
+                ref[at : at + HY, :] = field[b, HY + start : 2 * HY + start, :] if b < 2 else halo[f]
         base = 3 * BLK * HY
         for i in range(groups):
             own = inverse_ref[:, i * LANES : (i + 1) * LANES]
@@ -244,29 +248,22 @@
 
 
 def setup_kernel(
-    rhs_ref, depth_ref, mask_ref, basis_ref, left_ref, right_ref, below_ref, above_ref, geo_ref,
-    east_ref, west_ref, north_ref, inv_ref, basis_out, res_ref, smooth_ref,
-    wet_ref, est_a, est_b, step_ref,
+    wet_in, res_in, weight_in, left_ref, right_ref, below_ref, above_ref, geo_ref,
+    wet_ref, res_ref, weight_ref, east_ref, west_ref, north_ref, inv_ref, smooth_ref,
+    est_a, est_b, step_ref,
 ):
-    outs = (wet_ref, res_ref, basis_out)
+    outs = (wet_ref, res_ref, weight_ref)
     for f, ref in enumerate(outs):
         for b in range(BLK):
             at = (f * BLK + b) * HY
             ref[b, 0:HY, :] = below_ref[at : at + HY, :]
             ref[b, HY + NY : ROWS, :] = above_ref[at : at + HY, :]
-    for g in range(AGG_LAT):
-
-        def fill(i, carry, g=g):
-            start = pl.multiple_of(g * BAND + i * STEP, 8)
-            for b in range(2):
-                for f, value in enumerate(own_fields(rhs_ref, depth_ref, mask_ref, basis_ref, start, STEP, b)):
-                    outs[f][b, pl.ds(HY + start, STEP), :] = value
-            part = pl.multiple_of(i * STEP, 8)
-            for f, value in enumerate(unpack_columns(left_ref, right_ref, g, part, STEP)):
-                outs[f][2, pl.ds(HY + start, STEP), :] = value
-            return carry
-
-        lax.fori_loop(0, BAND // STEP, fill, 0)
+
+    def fill(g, start):
+        for f, value in enumerate(unpack_columns(left_ref, right_ref, g, start - g * BAND, STEP)):
+            outs[f][2, HY + start : HY + start + STEP, :] = value
+
+    for_own(fill)
 
     def east_west(start, rows):
         wet = load(wet_ref, start, rows)
@@ -339,17 +336,10 @@
     return rows
 
 
-def for_bands(fn, carry_of=None):
-    out = []
-    fn(0, HY, 0, None)
-    for a in range(AGG_LAT):
-
-        def step(i, carry, a=a):
-            return fn(pl.multiple_of(HY + a * BAND + i * STEP, 8), STEP, a + 1, carry)
-
-        out.append(lax.fori_loop(0, BAND // STEP, step, carry_of))
-    fn(HY + NY, HY, AGG_LAT + 1, None)
-    return out
+def for_bands(fn):
+    fn(0, HY, 0)
+    for_own(lambda a, start: fn(HY + start, STEP, a + 1))
+    fn(HY + NY, HY, AGG_LAT + 1)
 
 
 def search_kernel(
@@ -359,12 +349,11 @@
 ):
     coarse = coarse_solve(got_ref, inverse_ref, left_ref, right_ref, below_ref, above_ref)
 
-    def direction(start, rows, band, carry):
+    def direction(start, rows, band):
         part, weight = load(smooth_ref, start, rows), load(basis_ref, start, rows)
         store(search_ref, start, rows, [part[b] + weight[b] * coarse[band][b] for b in range(BLK)])
-        return 0
-
-    for_bands(direction, 0)
+
+    for_bands(direction)
     ops = (east_ref, west_ref, north_ref, geo_ref.at[2])
     clear_ends(applied_ref)
 
@@ -374,27 +363,22 @@
         return here, out
 
     apply(HY - 8, 8)
-    sums = []
     zero = jnp.zeros((8, LANES), F32)
-    curvature, projection = zero, zero
-    for a in range(AGG_LAT):
-
-        def step(i, carry, a=a):
-            start = pl.multiple_of(HY + a * BAND + i * STEP, 8)
-            here, out = apply(start, STEP)
-            accs = [carry[b] + fold(basis_ref[b, pl.ds(start, STEP), :] * out[b]) for b in range(AGG_LON)]
-            curvature, projection = carry[AGG_LON:]
-            for b in range(AGG_LON):
-                curvature = curvature + fold(here[b] * out[b])
-                projection = projection + fold(here[b] * res_ref[b, pl.ds(start, STEP), :])
-            return (*accs, curvature, projection)
-
-        *accs, curvature, projection = lax.fori_loop(
-            0, BAND // STEP, step, (zero,) * AGG_LON + (curvature, projection)
-        )
-        sums += [total(x) for x in accs]
+    sums = [zero] * (AGG_LAT * AGG_LON + 2)
+
+    def own(a, start):
+        start = HY + start
+        here, out = apply(start, STEP)
+        for b in range(AGG_LON):
+            k, weight = a * AGG_LON + b, basis_ref[b, start : start + STEP, :]
+            sums[k] = sums[k] + fold(weight * out[b])
+            sums[-2] = sums[-2] + fold(here[b] * out[b])
+            sums[-1] = sums[-1] + fold(here[b] * res_ref[b, start : start + STEP, :])
+
+    for_own(own)
     apply(HY + NY, 8)
-    fill_rows(send_ref, own_row(tile_ref, sums, (total(curvature), total(projection))))
+    sums = [total(x) for x in sums]
+    fill_rows(send_ref, own_row(tile_ref, sums[:-2], sums[-2:]))
 
 
 def second_kernel(
@@ -422,35 +406,33 @@
     alpha = jnp.broadcast_to(projection, (1, LANES)) / jnp.broadcast_to(curvature, (1, LANES))
     known_ref[...] = jnp.broadcast_to(jnp.where(lane == 0, curvature, alpha), (8, LANES))
 
-    def build(start, rows, band, carry):
+    def build(start, rows, band):
         part, weight = load(smooth_ref, start, rows), load(basis_ref, start, rows)
         search = load(search_ref, start, rows)
         store(
             full_ref, start, rows,
             [search[b] - alpha * (part[b] + weight[b] * coarse[band][b]) for b in range(BLK)],
         )
-        return 0
-
-    for_bands(build, 0)
+
+    for_bands(build)
     ops = (east_ref, west_ref, north_ref, geo_ref.at[2])
 
-    def step(i, carry):
-        start = pl.multiple_of(HY + i * STEP, 8)
-        own = pl.ds(pl.multiple_of(i * STEP, 8), STEP)
+    accs = [jnp.zeros((8, LANES), F32)] * 4
+
+    def own(a, start):
+        at, start = slice(start, start + STEP), HY + start
         here, out = operate(full_ref, *ops, start, STEP)
         search, applied, res = load(search_ref, start, STEP), load(applied_ref, start, STEP), load(res_ref, start, STEP)
-        carry = list(carry)
         for b in range(AGG_LON):
             rest = res[b] - alpha * applied[b]
-            update_ref[b, own, :] = here[b]
-            operated_ref[b, own, :] = out[b]
-            rest_ref[b, own, :] = rest
+            update_ref[b, at, :] = here[b]
+            operated_ref[b, at, :] = out[b]
+            rest_ref[b, at, :] = rest
             pairs = ((here[b], applied[b]), (here[b], out[b]), (here[b], rest), (search[b], rest))
-            carry = [acc + fold(x * y) for acc, (x, y) in zip(carry, pairs)]
-        return tuple(carry)
-
-    zero = jnp.zeros((8, LANES), F32)
-    accs = lax.fori_loop(0, NY // STEP, step, (zero,) * 4)
+            for k, (x, y) in enumerate(pairs):
+                accs[k] = accs[k] + fold(x * y)
+
+    for_own(own)
     row = jnp.zeros((1, LANES), F32)
     for k, acc in enumerate(accs):
         row = jnp.where(lane == k, total(acc), row)
@@ -472,27 +454,26 @@
     along = alpha + step_size * beta
     back = step_size * beta
 
-    def step(i, carry):
-        start = pl.multiple_of(i * STEP, 8)
-        own, halo = pl.ds(start, STEP), pl.ds(pl.multiple_of(HY + i * STEP, 8), STEP)
+    def own(a, start):
+        at, halo = slice(start, start + STEP), slice(HY + start, HY + start + STEP)
         for b in range(AGG_LON):
-            at = (own, pl.ds(b * LANES, LANES))
-            field_ref[at] = along * search_ref[b, halo, :] + step_size * update_ref[b, own, :]
-            out_ref[at] = rest_ref[b, own, :] - step_size * operated_ref[b, own, :] - back * applied_ref[b, halo, :]
-        return carry
-
-    lax.fori_loop(0, NY // STEP, step, 0)
-
-
-def call(kernel, outs, scratch=(), scalars=0, ins=0, flops=0):
-    specs = [pl.BlockSpec(memory_space=pltpu.SMEM)] * scalars + [pl.BlockSpec(memory_space=pltpu.VMEM)] * ins
+            out = (at, slice(b * LANES, (b + 1) * LANES))
+            field_ref[out] = along * search_ref[b, halo, :] + step_size * update_ref[b, at, :]
+            out_ref[out] = rest_ref[b, at, :] - step_size * operated_ref[b, at, :] - back * applied_ref[b, halo, :]
+
+    for_own(own)
+
+
+def call(kernel, outs, scratch=(), scalars=0, hbm=0, ins=0, flops=0, grant=6, aliases=None):
+    spaces = [pltpu.SMEM] * scalars + [pltpu.HBM] * hbm + [pltpu.VMEM] * ins
     return pl.pallas_call(
         kernel,
         out_shape=[jax.ShapeDtypeStruct(s, F32) for s in outs],
-        in_specs=specs,
+        in_specs=[pl.BlockSpec(memory_space=space) for space in spaces],
         out_specs=[pl.BlockSpec(memory_space=pltpu.VMEM)] * len(outs),
-        scratch_shapes=[pltpu.VMEM(s, F32) for s in scratch],
-        compiler_params=pltpu.CompilerParams(vmem_limit_bytes=40 * 1024 * 1024),
+        scratch_shapes=[pltpu.VMEM(s, F32) if isinstance(s, tuple) else s for s in scratch],
+        input_output_aliases=aliases or {},
+        compiler_params=pltpu.CompilerParams(vmem_limit_bytes=grant * 1024 * 1024),
         cost_estimate=pl.CostEstimate(flops=flops, bytes_accessed=4 * 1024 * 1024, transcendentals=0),
     )
 
@@ -520,22 +501,25 @@
     )
     geo = jnp.broadcast_to(geo[:, :, None], (3, ROWS, LANES))
 
-    gather, to_west, to_east = call(
-        pack_kernel, [(devices, LANES), (BAND + rows8, LANES), (BAND + rows8, LANES)], scalars=1, ins=5
+    loads = [(NY, NX), (NY, NX), pltpu.VMEM((NY, NX), jnp.int32), (NY, NX), inverse.shape]
+    gather, to_west, to_east, *fields = call(
+        pack_kernel,
+        [(devices, LANES), (BAND + rows8, LANES), (BAND + rows8, LANES), full, full, full],
+        scratch=[*loads, pltpu.SemaphoreType.DMA((4 * AGG_LAT + 1,))], scalars=1, hbm=5,
     )(tile, *own, inverse)
     ring = [(i, (i + 1) % n_lon) for i in range(n_lon)]
     left = lax.ppermute(to_east, "lon", ring)
     right = lax.ppermute(to_west, "lon", [(j, i) for i, j in ring])
     got = exchange(gather)
     edge_rows = 3 * BLK * HY + rows8
-    to_south, to_north = call(edge_kernel, [(edge_rows, LANES)] * 2, ins=7)(*own, inverse, left, right)
+    to_south, to_north = call(edge_kernel, [(edge_rows, LANES)] * 2, ins=6)(*fields, inverse, left, right)
     line = [(i, i + 1) for i in range(n_lat - 1)]
     below = lax.ppermute(to_north, "lat", line)
     above = lax.ppermute(to_south, "lat", [(j, i) for i, j in line])
 
-    east, west, north, inv, weight, res, smoothed = call(
-        setup_kernel, [full] * 7, scratch=[full] * 4, ins=9, flops=40000000
-    )(*own, left, right, below, above, geo)
+    _, res, weight, east, west, north, inv, smoothed = call(
+        setup_kernel, [full] * 8, scratch=[full] * 3, ins=8, flops=40000000, aliases={0: 0, 1: 1, 2: 2}
+    )(*fields, left, right, below, above, geo)
     solver = (inverse, left, right, below, above)
     faces = (east, west, north, weight)
     send, search, applied = call(search_kernel, [(devices, LANES), full, full], scalars=1, ins=13, flops=8000000)(

time: 132 us -> 122 us (0.924)
  Pallas kernels: 27.2 us -> 15.9 us
  blocking collectives: 24.8 us -> 21.9 us
  waiting for transfers between devices: 6.44 us -> 9.28 us
    pallas_call x2, Pallas kernels: 11 us -> 4.51 us  [the longest x1 4.42 us: body(): call(setup_kernel, [full] * 8, scratch=[full] * 3, ins=8, flops=40000000,...]
    pallas_call x1, Pallas kernels: 6.15 us -> 2.15 us  [body(): call(second_kernel, [full], scratch=[full] * 3, ins=7, flops=20000000)]
    all_to_all x1, blocking collectives: 24.8 us -> 21.9 us  [exchange(): return lax.all_to_all(x, AXES, 0, 0, tiled=True)]
    all_to_all x2, waiting for transfers between devices: 1.62 us -> 4.45 us  [exchange(): return lax.all_to_all(x, AXES, 0, 0, tiled=True)]
    pallas_call x1, Pallas kernels: 2.35 us -> 4.36 us  [body(): call(pack_kernel, [(devices, LANES), (BAND + rows8, LANES), (BAND + rows8...]
    pallas_call x1, Pallas kernels: 3.29 us -> 1.82 us  [body(): call(search_kernel, [(devices, LANES), full, full], scalars=1, ins=13, fl...]
    unnamed x88 -> x76, local copies, waits for them, and re-layouts: 32.1 us -> 33.3 us
  transfers between devices with their start and end apart: 6 -> 6, of which waited for: 3 -> 3; matrix products, arithmetic and copies ran while one was open for 0% -> 0% of each run, Pallas kernels for 13% -> 6%
where the time goes in v2:
time: 122 us; the launch traced here: 121 us
  starting transfers between devices  39 us (32%)
  local copies, waits for them, and re-layouts  33.5 us (27%)
  blocking collectives  21.9 us (18%)
  Pallas kernels  15.9 us (13%)
  waiting for transfers between devices  9.28 us (8%)
    unnamed x76, local copies, waits for them, and re-layouts  33.3 us
    all_to_all x2, starting transfers between devices, exchange(): return lax.all_to_all(x, AXES, 0, 0, tiled=True)  24.7 us
    all_to_all x1, blocking collectives, exchange(): return lax.all_to_all(x, AXES, 0, 0, tiled=True)  21.9 us
    ppermute x1, starting transfers between devices, body(): right = lax.ppermute(to_west, 'lon', [(j, i) for i, j in ring])  6.22 us
    ppermute x1, waiting for transfers between devices, body(): above = lax.ppermute(to_south, 'lat', [(j, i) for i, j in line])  4.54 us
    all_to_all x2, waiting for transfers between devices, exchange(): return lax.all_to_all(x, AXES, 0, 0, tiled=True)  4.45 us
    pallas_call x1, Pallas kernels, body(): call(setup_kernel, [full] * 8, scratch=[full] * 3, ins=8, flops=40000000,...  4.42 us
    pallas_call x1, Pallas kernels, body(): call(pack_kernel, [(devices, LANES), (BAND + rows8, LANES), (BAND + rows8...  4.36 us
  transfers between devices with their start and end apart: 6, of which 3 were waited for; matrix products, arithmetic and copies ran while one was open for 0% of the time, Pallas kernels for 6%

profile of v2, /device:TPU:1, one launch (start us, length us, event | category | flops | bytes accessed | tf_op | source)
XLA Modules:
  0.0 120.8 jit_solution(12425860421964314077)
XLA Ops:
  5.6 4.4 %shard_map.68 = (f32[256,128]{1,0:T(8,128)}, f32[256,128]{1,0:T(8,128)S(1)}, f32[256,128]{1,0:T(8,128)S(1)}, f32[3,544,128]{2,1,0:T(8,128)S(1)}, f32[3,544,128]{2,1,0:T(8,128)S(1)}, /*index=5*/f32[3,544,128]{2,1,0:T(8,128)S(1)}) custom-call(s32[1]{0:T(128)} %bitcast.tile_ref, f32[512,256]{1,0:T(8,128)S(1)} %copy-done.33, f32[512,256]{1,0:T(8,128)S(1)} %copy-done.34, ...), custom_call_target="tpu_custom_call" | custom-call | bytes 4194304 | tf_op jit(solution)/shard_map/pallas_call | solution.py:505
  10.0 2.5 %collective-permute-start = (f32[256,128]{1,0:T(8,128)S(1)}, f32[256,128]{1,0:T(8,128)S(1)}, u32[]{:S(2)}, u32[]{:S(2)}) collective-permute-start(f32[256,128]{1,0:T(8,128)S(1)} %get-tuple-element.26), channel_id=1, source_target_pairs={{0,8},{8,16},{16,24},{24,32},{32,40},{40,48},{48,56},{56,64},{64,7... | collective-permute-start | bytes 393224 | tf_op jit(solution)/shard_map/ppermute | solution.py:511
  12.6 6.2 %collective-permute-start.1 = (f32[256,128]{1,0:T(8,128)S(1)}, f32[256,128]{1,0:T(8,128)S(1)}, u32[]{:S(2)}, u32[]{:S(2)}) collective-permute-start(f32[256,128]{1,0:T(8,128)S(1)} %get-tuple-element.27), channel_id=1, source_target_pairs={{8,0},{16,8},{24,16},{32,24},{40,32},{48,40},{56,48},{64,56},{72,6... | collective-permute-start | bytes 393224 | tf_op jit(solution)/shard_map/ppermute | solution.py:512
  18.8 11.2 %all-to-all-start = ((f32[256,1,128]{2,1,0:T(1,128)}), f32[256,1,128]{2,1,0:T(1,128)}, u32[]{:S(2)}, u32[]{:S(2)}) async-start(f32[256,1,128]{2,1,0:T(1,128)} %bitcast.2), calls=%async_computation | async-start | bytes 262144 | tf_op jit(solution)/shard_map/all_to_all | solution.py:482
  30.8 3.5 %collective-permute-start.2 = (f32[272,128]{1,0:T(8,128)S(1)}, f32[272,128]{1,0:T(8,128)S(1)}, u32[]{:S(2)}, u32[]{:S(2)}) collective-permute-start(f32[272,128]{1,0:T(8,128)S(1)} %get-tuple-element.31), channel_id=1, source_target_pairs={{0,1},{1,2},{2,3},{3,4},{4,5},{5,6},{6,7},{8,9},{9,10},{10,11},{11... | collective-permute-start | bytes 417800 | tf_op jit(solution)/shard_map/ppermute | solution.py:517
  34.4 1.9 %collective-permute-start.3 = (f32[272,128]{1,0:T(8,128)S(1)}, f32[272,128]{1,0:T(8,128)S(1)}, u32[]{:S(2)}, u32[]{:S(2)}) collective-permute-start(f32[272,128]{1,0:T(8,128)S(1)} %get-tuple-element.32), channel_id=1, source_target_pairs={{1,0},{2,1},{3,2},{4,3},{5,4},{6,5},{7,6},{9,8},{10,9},{11,10},{12... | collective-permute-start | bytes 417800 | tf_op jit(solution)/shard_map/ppermute | solution.py:518
  36.7 4.5 %collective-permute-done.3.above_ref = f32[272,128]{1,0:T(8,128)S(1)} collective-permute-done((f32[272,128]{1,0:T(8,128)S(1)}, f32[272,128]{1,0:T(8,128)S(1)}, u32[]{:S(2)}, u32[]{:S(2)}) %collective-permute-start.3) | collective-permute-done | bytes 139296 | tf_op jit(solution)/shard_map/ppermute | solution.py:518
  41.9 4.4 %shard_map.70 = (f32[3,544,128]{2,1,0:T(8,128)S(1)}, f32[3,544,128]{2,1,0:T(8,128)S(1)}, f32[3,544,128]{2,1,0:T(8,128)S(1)}, f32[3,544,128]{2,1,0:T(8,128)S(1)},...) custom-call(f32[3,544,128]{2,1,0:T(8,128)S(1)} %get-tuple-element.28, ...), custom_call_target="tpu_custom_call", output_to_operand_aliasing={{0}: (0, {}), {1}: (1, {}), {2}: (2, {})} | custom-call | flops 40000000 | bytes 4194304 | tf_op jit(solution)/shard_map/pallas_call | solution.py:520
  50.9 1.1 copy-done.1
  52.0 1.1 copy-done.5
  53.2 1.1 copy-done.9
  58.2 1.8 %shard_map.71 = (f32[256,128]{1,0:T(8,128)S(1)}, f32[3,544,128]{2,1,0:T(8,128)S(1)}, f32[3,544,128]{2,1,0:T(8,128)S(1)}) custom-call(s32[1]{0:T(128)} %bitcast.tile_ref, f32[256,128]{1,0:T(8,128)} %bitcast.3.got_ref, f32[8,2048]{1,0:T(8,128)S(1)} %copy-done.28, f32[256,128]{1,0:T(8,128)S(1)} %collective-permute-done.left_ref, f32[256,128]{1,0:T(8,128)S(1)} %copy-done.19, ...), custom_call_target="tpu_custom_call" | custom-call | flops 8000000 | bytes 4194304 | tf_op jit(solution)/shard_map/pallas_call | solution.py:525
  61.6 13.5 %all-to-all-start.1 = ((f32[256,1,128]{2,1,0:T(1,128)}), f32[256,1,128]{2,1,0:T(1,128)}, u32[]{:S(2)}, u32[]{:S(2)}) async-start(f32[256,1,128]{2,1,0:T(1,128)} %bitcast.15), calls=%async_computation.1 | async-start | bytes 262144 | tf_op jit(solution)/shard_map/all_to_all | solution.py:482
  76.3 1.1 copy-done.6
  78.6 1.1 copy-done.30
  79.7 2.1 %shard_map.72.smooth_ref = f32[3,544,128]{2,1,0:T(8,128)S(1)} custom-call(f32[3,544,128]{2,1,0:T(8,128)S(1)} %get-tuple-element.40.applied_ref, f32[3,544,128]{2,1,0:T(8,128)S(1)} %copy-done.30, f32[3,544,128]{2,1,0:T(8,128)S(1)} %copy-done.2, f32[3,544,128]{2,1,0:T(8,128)S(1)} %copy-done.6, f32[3,544,128]{2,1,0:T(8,128)S(1)} %copy-done.10, ...), custom_call_target="tpu_custom_call" | custom-call | flops 20000000 | bytes 4194304 | tf_op jit(solution)/shard_map/pallas_call | solution.py:529
  82.8 4.4 %all-to-all-done.1 = f32[256,1,128]{2,1,0:T(1,128)} async-done(((f32[256,1,128]{2,1,0:T(1,128)}), f32[256,1,128]{2,1,0:T(1,128)}, u32[]{:S(2)}, u32[]{:S(2)}) %all-to-all-start.1) | async-done | bytes 131104 | tf_op jit(solution)/shard_map/all_to_all | solution.py:482
  87.3 1.1 copy-done.3
  88.4 1.1 copy-done.7
  90.7 1.1 copy-done.13
  91.9 1.1 copy-done.15
  95.7 1.9 %shard_map.73 = (f32[256,128]{1,0:T(8,128)S(1)}, f32[8,128]{1,0:T(8,128)S(1)}, f32[2,512,128]{2,1,0:T(8,128)S(1)}, f32[2,512,128]{2,1,0:T(8,128)S(1)}, f32[2,512,128]{2,1,0:T(8,128)S(1)}) custom-call(f32[256,128]{1,0:T(8,128)} %bitcast.6.got_ref, f32[8,2048]{1,0:T(8,128)S(1)} %copy-done.28, f32[256,128]{1,0:T(8,128)S(1)} %collective-permute-done.left_ref, ...), custom_call_target="tpu_custom_call" | custom-call | flops 8000000 | bytes 4194304 | tf_op jit(solution)/shard_map/pallas_call | solution.py:530
  97.6 21.9 %all_to_all.33 = f32[256,1,128]{2,1,0:T(1,128)S(1)} all-to-all(f32[256,1,128]{2,1,0:T(1,128)S(1)} %bitcast.14), channel_id=1, replica_groups=mesh['lon'=32,'lat'=8] {'lon','lat'}, dimensions={0} | all-to-all | bytes 262144 | tf_op jit(solution)/shard_map/all_to_all | solution.py:482
  119.5 1.2 %shard_map.74 = (f32[512,256]{1,0:T(8,128)}, f32[512,256]{1,0:T(8,128)}) custom-call(f32[256,128]{1,0:T(8,128)S(1)} %bitcast.13, f32[8,128]{1,0:T(8,128)S(1)} %get-tuple-element.44.known_ref, f32[3,544,128]{2,1,0:T(8,128)S(1)} %copy-done.16, f32[3,544,128]{2,1,0:T(8,128)S(1)} %get-tuple-element.40.applied_ref, ...), custom_call_target="tpu_custom_call" | custom-call | flops 1000000 | bytes 4194304 | tf_op jit(solution)/shard_map/pallas_call | solution.py:534
  (76 shorter events, 23.8 us)
Async XLA Ops:
  1.5 1.0 copy-start.33
  10.0 20.2 %collective-permute-start = (f32[256,128]{1,0:T(8,128)S(1)}, f32[256,128]{1,0:T(8,128)S(1)}, u32[]{:S(2)}, u32[]{:S(2)}) collective-permute-start(f32[256,128]{1,0:T(8,128)S(1)} %get-tuple-element.26), channel_id=1, source_target_pairs={{0,8},{8,16},{16,24},{24,32},{32,40},{40,48},{48,56},{56,64},{64,7... | collective-permute-start | bytes 393224 | tf_op jit(solution)/shard_map/ppermute | solution.py:511
  12.6 17.6 %collective-permute-start.1 = (f32[256,128]{1,0:T(8,128)S(1)}, f32[256,128]{1,0:T(8,128)S(1)}, u32[]{:S(2)}, u32[]{:S(2)}) collective-permute-start(f32[256,128]{1,0:T(8,128)S(1)} %get-tuple-element.27), channel_id=1, source_target_pairs={{8,0},{16,8},{24,16},{32,24},{40,32},{48,40},{56,48},{64,56},{72,6... | collective-permute-start | bytes 393224 | tf_op jit(solution)/shard_map/ppermute | solution.py:512
  18.8 11.4 %copy-start.28 = (f32[8,2048]{1,0:T(8,128)S(1)}, f32[8,2048]{1,0:T(8,128)}, u32[]{:S(2)}) copy-start(f32[8,2048]{1,0:T(8,128)} %inverse_ref.5) | copy-start | bytes 196612
  18.8 32.1 %all-to-all-start = ((f32[256,1,128]{2,1,0:T(1,128)}), f32[256,1,128]{2,1,0:T(1,128)}, u32[]{:S(2)}, u32[]{:S(2)}) async-start(f32[256,1,128]{2,1,0:T(1,128)} %bitcast.2), calls=%async_computation | async-start | bytes 262144 | tf_op jit(solution)/shard_map/all_to_all | solution.py:482
  30.8 5.9 %collective-permute-start.2 = (f32[272,128]{1,0:T(8,128)S(1)}, f32[272,128]{1,0:T(8,128)S(1)}, u32[]{:S(2)}, u32[]{:S(2)}) collective-permute-start(f32[272,128]{1,0:T(8,128)S(1)} %get-tuple-element.31), channel_id=1, source_target_pairs={{0,1},{1,2},{2,3},{3,4},{4,5},{5,6},{6,7},{8,9},{9,10},{10,11},{11... | collective-permute-start | bytes 417800 | tf_op jit(solution)/shard_map/ppermute | solution.py:517
  34.4 6.9 %collective-permute-start.3 = (f32[272,128]{1,0:T(8,128)S(1)}, f32[272,128]{1,0:T(8,128)S(1)}, u32[]{:S(2)}, u32[]{:S(2)}) collective-permute-start(f32[272,128]{1,0:T(8,128)S(1)} %get-tuple-element.32), channel_id=1, source_target_pairs={{1,0},{2,1},{3,2},{4,3},{5,4},{6,5},{7,6},{9,8},{10,9},{11,10},{12... | collective-permute-start | bytes 417800 | tf_op jit(solution)/shard_map/ppermute | solution.py:518
  36.4 5.5 %copy-start.18 = (f32[256,128]{1,0:T(8,128)S(1)}, f32[256,128]{1,0:T(8,128)}, u32[]{:S(2)}) copy-start(f32[256,128]{1,0:T(8,128)} %copy-done.17) | copy-start | bytes 393220
  36.7 4.8 %copy-start.21 = (f32[272,128]{1,0:T(8,128)}, f32[272,128]{1,0:T(8,128)S(1)}, u32[]{:S(2)}) copy-start(f32[272,128]{1,0:T(8,128)S(1)} %collective-permute-done.2.below_ref) | copy-start | bytes 417796
  50.9 1.2 copy-start.1
  52.0 1.1 copy-start.5
  53.2 1.1 copy-start.9
  57.0 1.1 copy-start.32
  61.6 25.7 %all-to-all-start.1 = ((f32[256,1,128]{2,1,0:T(1,128)}), f32[256,1,128]{2,1,0:T(1,128)}, u32[]{:S(2)}, u32[]{:S(2)}) async-start(f32[256,1,128]{2,1,0:T(1,128)} %bitcast.15), calls=%async_computation.1 | async-start | bytes 262144 | tf_op jit(solution)/shard_map/all_to_all | solution.py:482
  75.1 1.2 copy-start.2
  76.3 1.1 copy-start.6
  77.4 1.1 copy-start.10
  78.6 1.1 copy-start.30
  87.3 1.2 copy-start.3
  88.4 1.1 copy-start.7
  89.6 1.1 copy-start.11
  90.7 1.1 copy-start.13
  91.9 1.1 copy-start.15
  95.7 23.8 %copy-start.16 = (f32[3,544,128]{2,1,0:T(8,128)S(1)}, f32[3,544,128]{2,1,0:T(8,128)}, u32[]{:S(2)}) copy-start(f32[3,544,128]{2,1,0:T(8,128)} %copy-done.14) | copy-start | bytes 2506756
  (20 other events, 17.7 us)

commit v3 on v2

v3 whole, which is shorter than its diff:
```python
import functools

import jax
import jax.numpy as jnp
from jax import lax
from jax.experimental import pallas as pl
from jax.experimental.pallas import tpu as pltpu
from jax.sharding import PartitionSpec as P

SWEEPS = 4
AGG_LAT = 4
AGG_LON = 2
LOW_EDGE = 0.1
HIGH_EDGE = 2.0
SHIFT_SCALE = 1.0e-5

NY = 512
NX = 256
HY = 16
WX = 9
ROWS = NY + 2 * HY
LANES = 128
BLK = 3
BAND = NY // AGG_LAT
STEP = 16
SWEEP = 24
CHUNKS = ((0, 152), (152, 128), (280, 128), (408, 136))
SLOTS = LANES // 8
AXES = ("lon", "lat")
F32 = jnp.float32


def chebyshev_plan(sweep_total):
    interval_mid = (HIGH_EDGE + LOW_EDGE) / 2.0
    interval_half = (HIGH_EDGE - LOW_EDGE) / 2.0
    mid_ratio = interval_mid / interval_half
    previous = 1.0 / mid_ratio
    pairs = []
    for _ in range(sweep_total - 1):
        fresh = 1.0 / (2.0 * mid_ratio - previous)
        pairs.append((fresh * previous, 2.0 * fresh / interval_half))
        previous = fresh
    return 1.0 / interval_mid, pairs


def lane_ids(rows):
    return lax.broadcasted_iota(jnp.int32, (rows, LANES), 1)


def east_of(blocks):
    lane = lane_ids(blocks[0].shape[0])
    rolled = [pltpu.roll(v, LANES - 1, 1) for v in blocks]
    return [jnp.where(lane == LANES - 1, rolled[(b + 1) % BLK], rolled[b]) for b in range(BLK)]


def west_of(blocks):
    lane = lane_ids(blocks[0].shape[0])
    rolled = [pltpu.roll(v, 1, 1) for v in blocks]
    return [jnp.where(lane == 0, rolled[(b + BLK - 1) % BLK], rolled[b]) for b in range(BLK)]


def load(ref, start, rows):
    return [ref[b, pl.ds(start, rows), :] for b in range(BLK)]


def store(ref, start, rows, blocks):
    for b in range(BLK):
        ref[b, pl.ds(start, rows), :] = blocks[b]


def for_strips(fn):
    for start in range(8, ROWS - 8, SWEEP):
        fn(start, min(SWEEP, ROWS - 8 - start))


def for_own(fn):
    for start in range(0, NY, STEP):
        fn(start // BAND, start)


def clear_ends(ref):
    zero = jnp.zeros((8, LANES), F32)
    for b in range(BLK):
        ref[b, 0:8, :] = zero
        ref[b, ROWS - 8 : ROWS, :] = zero


def operate(v_ref, east_ref, west_ref, north_ref, shift_ref, start, rows):
    here = load(v_ref, start, rows)
    up, down = load(v_ref, start + 1, rows), load(v_ref, start - 1, rows)
    right, left = east_of(here), west_of(here)
    ef, wf = load(east_ref, start, rows), load(west_ref, start, rows)
    nf, sf = load(north_ref, start, rows), load(north_ref, start - 1, rows)
    shift = shift_ref[pl.ds(start, rows), :]
    out = [
        shift * here[b]
        + ef[b] * (here[b] - right[b])
        + wf[b] * (here[b] - left[b])
        + nf[b] * (here[b] - up[b])
        + sf[b] * (here[b] - down[b])
        for b in range(BLK)
    ]
    return here, out


def fold(x):
    return jnp.sum(x.reshape(-1, 8, LANES), axis=0)


def total(x):
    return jnp.sum(jnp.sum(x, axis=1, keepdims=True), axis=0, keepdims=True)


def own_row(tile_ref, values, scalars=()):
    lane = lane_ids(1)
    base = (tile_ref[0] % SLOTS) * 8
    other = ((tile_ref[0] + SLOTS // 2) % SLOTS) * 8
    row = jnp.zeros((1, LANES), F32)
    for k, value in enumerate(values):
        row = jnp.where(lane == base + k, value, row)
    for k, value in enumerate(scalars):
        row = jnp.where(lane == other + k, value, row)
    return row


def own_row_sums(got_ref, count):
    rows = got_ref.shape[0]
    lane = lane_ids(rows)
    slot = lax.broadcasted_iota(jnp.int32, (rows, LANES), 0) % SLOTS
    other = ((slot + SLOTS // 2) % SLOTS) * 8
    got = got_ref[...]
    return [total(fold(jnp.where(lane == other + k, got, 0.0))) for k in range(count)]


def fill_rows(ref, row):
    ref[...] = jnp.broadcast_to(row, ref.shape)


def pack_kernel(
    tile_ref, rhs_hbm, depth_hbm, mask_hbm, basis_hbm, inverse_hbm,
    gather_ref, west_ref, east_ref, edge_ref, wet_ref, res_ref, weight_ref,
    rhs_ref, depth_ref, mask_ref, basis_ref, inverse_ref, sems,
):
    pairs = ((rhs_hbm, rhs_ref), (mask_hbm, mask_ref), (basis_hbm, basis_ref), (depth_hbm, depth_ref))
    copies = []
    for g in range(AGG_LAT):
        at = pl.ds(g * BAND, BAND)
        copies.append(
            [pltpu.make_async_copy(src.at[at], dst.at[at], sems.at[4 * g + k]) for k, (src, dst) in enumerate(pairs)]
        )
    last = pltpu.make_async_copy(inverse_hbm, inverse_ref, sems.at[4 * AGG_LAT])
    for copy in sum(copies, []) + [last]:
        copy.start()
    groups = inverse_ref.shape[1] // LANES
    lane = lane_ids(STEP)
    sums = []
    zero = jnp.zeros((8, LANES), F32)
    for g in range(AGG_LAT):
        for copy in copies[g]:
            copy.wait()
        accs = [zero] * AGG_LON
        for start in range(g * BAND, (g + 1) * BAND, STEP):
            out_row = start - g * BAND
            fields = []
            for b in range(AGG_LON):
                at = (pl.ds(start, STEP), pl.ds(b * LANES, LANES))
                mask = mask_ref[at].astype(F32)
                wet = depth_ref[at] * mask
                res = rhs_ref[at] * mask
                weight = basis_ref[at] * mask
                accs[b] = accs[b] + fold(weight * res)
                fields.append((wet, res, weight))
                for f, (ref, value) in enumerate(zip((wet_ref, res_ref, weight_ref), fields[b])):
                    ref[b, start : start + STEP, :] = value
                    for side, first in ((0, 0), (1, NY - HY)):
                        if start == first:
                            edge_ref[side, f, b] = value
            for ref, b, extra in ((west_ref, 0, 0), (east_ref, 1, WX)):
                packed = jnp.zeros((STEP, LANES), F32) if g == 0 else ref[out_row : out_row + STEP, :]
                for f in range(3):
                    lo = 32 * g + WX * f
                    moved = pltpu.roll(fields[b][f], (lo + extra) % LANES, 1)
                    packed = jnp.where((lane >= lo) & (lane < lo + WX), moved, packed)
                ref[out_row : out_row + STEP, :] = packed
        sums += [total(acc) for acc in accs]
    fill_rows(gather_ref, own_row(tile_ref, sums))
    last.wait()
    for g in range(groups):
        part = inverse_ref[:, g * LANES : (g + 1) * LANES]
        west_ref[BAND + 8 * g : BAND + 8 * g + 8, :] = part
        east_ref[BAND + 8 * g : BAND + 8 * g + 8, :] = part


def unpack_columns(left_ref, right_ref, g, start, rows):
    lane = lane_ids(rows)
    left, right = left_ref[pl.ds(start, rows), :], right_ref[pl.ds(start, rows), :]
    out = []
    for f in range(3):
        lo = 32 * g + WX * f
        from_right = pltpu.roll(right, (LANES - lo) % LANES, 1)
        from_left = pltpu.roll(left, (2 * LANES - lo - WX) % LANES, 1)
        out.append(jnp.where(lane < WX, from_right, jnp.where(lane >= LANES - WX, from_left, 0.0)))
    return out


def edge_kernel(edge_ref, inverse_ref, left_ref, right_ref, south_ref, north_ref):
    groups = inverse_ref.shape[1] // LANES
    sub = lax.broadcasted_iota(jnp.int32, (8, LANES), 0)
    for side, (ref, start, band) in enumerate(((south_ref, 0, 0), (north_ref, BAND - HY, AGG_LAT - 1))):
        halo = unpack_columns(left_ref, right_ref, band, start, HY)
        for f in range(3):
            for b in range(BLK):
                at = (f * BLK + b) * HY
                ref[at : at + HY, :] = edge_ref[side, f, b] if b < 2 else halo[f]
        base = 3 * BLK * HY
        for i in range(groups):
            own = inverse_ref[:, i * LANES : (i + 1) * LANES]
            left = left_ref[BAND + 8 * i : BAND + 8 * i + 8, :]
            right = right_ref[BAND + 8 * i : BAND + 8 * i + 8, :]
            own = pltpu.roll(own, (8 - 2 * band) % 8, 0) if band else own
            left = pltpu.roll(left, (2 - 2 * band - 1 + 16) % 8, 0)
            right = pltpu.roll(right, (3 - 2 * band + 16) % 8, 0)
            picked = jnp.where(sub < 2, own, jnp.where(sub == 2, left, right))
            ref[base + 8 * i : base + 8 * i + 8, :] = picked


def west_of_faces(east_ref, west_ref, start, rows):
    store(west_ref, start, rows, west_of(load(east_ref, start, rows)))


def first_step(res_ref, inv_ref, faces, est_ref, step_ref, start, rows):
    east_ref, west_ref, north_ref, shift_ref = faces
    ef, wf = load(east_ref, start, rows), load(west_ref, start, rows)
    nf, sf = load(north_ref, start, rows), load(north_ref, start - 1, rows)
    shift = shift_ref[pl.ds(start, rows), :]
    inv = [1.0 / (shift + ef[b] + wf[b] + nf[b] + sf[b]) for b in range(BLK)]
    store(inv_ref, start, rows, inv)
    res = load(res_ref, start, rows)
    value = [chebyshev_plan(SWEEPS)[0] * (inv[b] * res[b]) for b in range(BLK)]
    store(step_ref, start, rows, value)
    store(est_ref, start, rows, value)


def smooth(res_ref, inv_ref, faces, est_refs, step_ref, finish):
    _, pairs = chebyshev_plan(SWEEPS)
    for k, (c1, c2) in enumerate(pairs):
        src, dst = est_refs[k % 2], est_refs[(k + 1) % 2]
        last = k == len(pairs) - 1

        def strip(start, rows, band=None):
            here, applied = operate(src, *faces, start, rows)
            inv, res, step = load(inv_ref, start, rows), load(res_ref, start, rows), load(step_ref, start, rows)
            step = [c1 * step[b] + c2 * (inv[b] * (res[b] - applied[b])) for b in range(BLK)]
            value = [here[b] + step[b] for b in range(BLK)]
            if last:
                finish(start, rows, band, value)
            else:
                store(step_ref, start, rows, step)
                store(dst, start, rows, value)

        if last:
            for_bands(strip)
        else:
            for_strips(strip)


def coarse_solve(got_ref, inverse_ref, left_ref, right_ref, below_ref, above_ref):
    groups = inverse_ref.shape[1] // LANES
    count = got_ref.shape[0] // groups
    base = 3 * BLK * HY
    accs = [jnp.zeros((8, LANES), F32) for _ in range(5)]
    mine = lane_ids(count) // 8 == lax.broadcasted_iota(jnp.int32, (count, LANES), 0)
    for i in range(groups):
        vec = jnp.sum(jnp.where(mine, got_ref[i * count : (i + 1) * count, :], 0.0), axis=0, keepdims=True)
        at = slice(BAND + 8 * i, BAND + 8 * i + 8)
        band = slice(base + 8 * i, base + 8 * i + 8)
        parts = (
            inverse_ref[:, i * LANES : (i + 1) * LANES],
            left_ref[at, :],
            right_ref[at, :],
            below_ref[band, :],
            above_ref[band, :],
        )
        accs = [acc + part * vec for acc, part in zip(accs, parts)]
    own, left, right, below, above = [jnp.sum(acc, axis=1, keepdims=True) for acc in accs]
    low = lane_ids(1) < LANES // 2

    def spread(value):
        return jnp.broadcast_to(value, (1, LANES))

    def edge(x):
        halo = jnp.where(low, spread(x[3:4]), spread(x[2:3]))
        return [spread(x[0:1]), spread(x[1:2]), halo]

    rows = [edge(below)]
    for a in range(AGG_LAT):
        halo = jnp.where(low, spread(right[2 * a : 2 * a + 1]), spread(left[2 * a + 1 : 2 * a + 2]))
        rows.append([spread(own[2 * a : 2 * a + 1]), spread(own[2 * a + 1 : 2 * a + 2]), halo])
    rows.append(edge(above))
    return rows


def for_bands(fn):
    fn(HY - 8, 8, 0)
    for_own(lambda a, start: fn(HY + start, STEP, a + 1))
    fn(HY + NY, 8, AGG_LAT + 1)


class Stream:
    def __init__(self, pairs, sems, first=0):
        self.chunks, self.done, self.rows = [], 0, 0
        for start, rows in CHUNKS:
            chunk = []
            for src, dst in pairs:
                lo, hi = start, start + rows
                if src.shape[1] == NY:
                    lo, hi = min(max(lo - HY, 0), NY), min(max(hi - HY, 0), NY)
                at = (slice(None), pl.ds(lo, hi - lo), slice(None))
                chunk.append(pltpu.make_async_copy(src.at[at], dst.at[at], sems.at[first]))
                first += 1
            for copy in chunk:
                copy.start()
            self.chunks.append(chunk)

    def need(self, row):
        while self.rows < min(row, ROWS):
            for copy in self.chunks[self.done]:
                copy.wait()
            self.rows = sum(CHUNKS[self.done])
            self.done += 1


def send_out(src, dst, sem):
    copy = pltpu.make_async_copy(src, dst, sem)
    copy.start()
    return copy


def search_kernel(
    tile_ref, got_ref, inverse_ref, left_ref, right_ref, below_ref, above_ref,
    wet_in, res_in, weight_in, geo_ref, shift_ref,
    send_ref, east_out, north_out, weight_out, search_out, applied_out,
    wet_ref, res_ref, weight_ref, east_ref, west_ref, north_ref, inv_ref,
    est_a, est_b, step_ref, search_ref, applied_ref, sems,
):
    fields = (wet_ref, res_ref, weight_ref)
    for f, (src, ref) in enumerate(zip((wet_in, res_in, weight_in), fields)):
        for b in range(BLK):
            at = (f * BLK + b) * HY
            ref[b, 0:HY, :] = below_ref[at : at + HY, :]
            ref[b, HY + NY : ROWS, :] = above_ref[at : at + HY, :]

    def fill(g, start):
        at = slice(HY + start, HY + start + STEP)
        halo = unpack_columns(left_ref, right_ref, g, start - g * BAND, STEP)
        for f, (src, ref) in enumerate(zip((wet_in, res_in, weight_in), fields)):
            for b in range(2):
                ref[b, at, :] = src[b, start : start + STEP, :]
            ref[2, at, :] = halo[f]

    for_own(fill)
    outs = [send_out(weight_ref, weight_out, sems.at[0])]

    def east_west(start, rows):
        wet = load(wet_ref, start, rows)
        over = geo_ref[0, pl.ds(start, rows), :]
        nxt = east_of(wet)
        face = [jnp.minimum(wet[b], nxt[b]) * over for b in range(BLK)]
        store(east_ref, start, rows, face)
        store(west_ref, start, rows, west_of(face))

    def north(start, rows):
        wet, nxt = load(wet_ref, start, rows), load(wet_ref, start + 1, rows)
        cosine = geo_ref[1, pl.ds(start, rows), :]
        store(north_ref, start, rows, [jnp.minimum(wet[b], nxt[b]) * cosine for b in range(BLK)])

    north(0, 8)
    for ref in (est_a, est_b, search_ref, applied_ref, east_ref):
        clear_ends(ref)
    for b in range(BLK):
        north_ref[b, ROWS - 8 : ROWS, :] = jnp.zeros((8, LANES), F32)
    faces = (east_ref, west_ref, north_ref, shift_ref)

    def prepare(start, rows):
        east_west(start, rows)
        north(start, rows)
        first_step(res_ref, inv_ref, faces, est_a, step_ref, start, rows)

    for_strips(prepare)
    outs += [send_out(east_ref, east_out, sems.at[1]), send_out(north_ref, north_out, sems.at[2])]
    coarse = coarse_solve(got_ref, inverse_ref, left_ref, right_ref, below_ref, above_ref)

    def finish(start, rows, band, value):
        wet, weight = load(wet_ref, start, rows), load(weight_ref, start, rows)
        part = [jnp.where(wet[b] > 0.0, value[b], 0.0) for b in range(BLK)]
        store(search_ref, start, rows, [part[b] + weight[b] * coarse[band][b] for b in range(BLK)])

    smooth(res_ref, inv_ref, faces, (est_a, est_b), step_ref, finish)
    outs.append(send_out(search_ref, search_out, sems.at[3]))
    sums = [jnp.zeros((8, LANES), F32)] * (AGG_LAT * AGG_LON + 2)

    def apply(start, rows, band):
        here, out = operate(search_ref, *faces, start, rows)
        store(applied_ref, start, rows, out)
        if 0 < band <= AGG_LAT:
            for b in range(AGG_LON):
                k, at = (band - 1) * AGG_LON + b, (b, slice(start, start + rows))
                sums[k] = sums[k] + fold(weight_ref[at] * out[b])
                sums[-2] = sums[-2] + fold(here[b] * out[b])
                sums[-1] = sums[-1] + fold(here[b] * res_ref[at])

    for_bands(apply)
    outs.append(send_out(applied_ref, applied_out, sems.at[4]))
    values = [total(x) for x in sums]
    fill_rows(send_ref, own_row(tile_ref, values[:-2], values[-2:]))
    for copy in outs:
        copy.wait()


def second_kernel(
    applied_hbm, east_hbm, north_hbm, weight_hbm, shift_ref,
    out_ref,
    applied_ref, east_ref, north_ref, weight_ref, west_ref, inv_ref, est_a, est_b, step_ref, sems,
):
    stream = Stream(
        ((applied_hbm, applied_ref), (east_hbm, east_ref), (north_hbm, north_ref), (weight_hbm, weight_ref)), sems
    )
    for ref in (est_a, est_b, out_ref):
        clear_ends(ref)
    faces = (east_ref, west_ref, north_ref, shift_ref)

    def prepare(start, rows):
        stream.need(start + rows)
        west_of_faces(east_ref, west_ref, start, rows)
        first_step(applied_ref, inv_ref, faces, est_a, step_ref, start, rows)

    for_strips(prepare)
    stream.need(ROWS)

    def finish(start, rows, band, value):
        weight = load(weight_ref, start, rows)
        store(out_ref, start, rows, [jnp.where(weight[b] > 0.0, value[b], 0.0) for b in range(BLK)])

    smooth(applied_ref, inv_ref, faces, (est_a, est_b), step_ref, finish)


def sums_kernel(
    got_ref, inverse_ref, left_ref, right_ref, below_ref, above_ref, smooth_ref, shift_ref,
    east_hbm, north_hbm, weight_hbm, search_hbm, applied_hbm, res_hbm,
    send_ref, known_ref, search_out, applied_out, update_ref, operated_ref, rest_ref,
    east_ref, north_ref, weight_ref, search_ref, applied_ref, res_ref, full_ref, sems,
):
    stream = Stream(
        (
            (weight_hbm, weight_ref), (search_hbm, search_ref), (east_hbm, east_ref),
            (north_hbm, north_ref), (applied_hbm, applied_ref), (res_hbm, res_ref),
        ),
        sems,
    )
    coarse = coarse_solve(got_ref, inverse_ref, left_ref, right_ref, below_ref, above_ref)
    curvature, projection = own_row_sums(got_ref, 2)
    lane = lane_ids(1)
    alpha = jnp.broadcast_to(projection, (1, LANES)) / jnp.broadcast_to(curvature, (1, LANES))
    known_ref[...] = jnp.broadcast_to(jnp.where(lane == 0, curvature, alpha), (8, LANES))

    def build(start, rows, band):
        stream.need(start + rows)
        part, weight, search = [load(ref, start, rows) for ref in (smooth_ref, weight_ref, search_ref)]
        store(
            full_ref, start, rows,
            [search[b] - alpha * (part[b] + weight[b] * coarse[band][b]) for b in range(BLK)],
        )

    accs = [jnp.zeros((8, LANES), F32)] * 4

    def apply(start):
        at, start = slice(start, start + STEP), HY + start
        here = load(full_ref, start, STEP)
        up, down = load(full_ref, start + 1, STEP), load(full_ref, start - 1, STEP)
        right, left = east_of(here), west_of(here)
        ef = load(east_ref, start, STEP)
        wf = west_of(ef)
        nf, sf = load(north_ref, start, STEP), load(north_ref, start - 1, STEP)
        shift = shift_ref[pl.ds(start, STEP), :]
        for b in range(AGG_LON):
            out = (
                shift * here[b]
                + ef[b] * (here[b] - right[b])
                + wf[b] * (here[b] - left[b])
                + nf[b] * (here[b] - up[b])
                + sf[b] * (here[b] - down[b])
            )
            search, applied = search_ref[b, start : start + STEP, :], applied_ref[b, start : start + STEP, :]
            rest = res_ref[b, at, :] - alpha * applied
            search_out[b, at, :] = search
            applied_out[b, at, :] = applied
            update_ref[b, at, :] = here[b]
            operated_ref[b, at, :] = out
            rest_ref[b, at, :] = rest
            pairs = ((here[b], applied), (here[b], out), (here[b], rest), (search, rest))
            for k, (x, y) in enumerate(pairs):
                accs[k] = accs[k] + fold(x * y)

    waiting = []

    def step(start, rows, band):
        build(start, rows, band)
        for ready in waiting:
            apply(ready)
        waiting.clear()
        if 0 < band <= AGG_LAT:
            waiting.append(start - HY)

    for_bands(step)
    stream.need(ROWS)
    row = jnp.zeros((1, LANES), F32)
    for k, acc in enumerate(accs):
        row = jnp.where(lane == k, total(acc), row)
    fill_rows(send_ref, row)


def final_kernel(
    got_ref, known_ref, search_ref, applied_ref, update_ref, operated_ref, rest_ref,
    field_out, residual_out, field_ref, residual_ref, sems,
):
    sums = jnp.sum(got_ref[...], axis=0, keepdims=True)
    lane = lane_ids(1)

    def pick(row, k):
        return jnp.broadcast_to(jnp.sum(jnp.where(lane == k, row, 0.0), axis=1, keepdims=True), (1, LANES))

    u_ap, u_au, u_r, p_r = [pick(sums, k) for k in range(4)]
    p_ap, alpha = pick(known_ref[0:1, :], 0), pick(known_ref[0:1, :], 1)
    beta = -u_ap / p_ap
    curvature = u_au + 2.0 * beta * u_ap + beta * beta * p_ap
    step_size = (u_r + beta * p_r) / curvature
    along = alpha + step_size * beta
    back = step_size * beta
    copies = []

    def own(a, start):
        at = slice(start, start + STEP)
        for b in range(AGG_LON):
            out = (at, slice(b * LANES, (b + 1) * LANES))
            field_ref[out] = along * search_ref[b, at, :] + step_size * update_ref[b, at, :]
            residual_ref[out] = rest_ref[b, at, :] - step_size * operated_ref[b, at, :] - back * applied_ref[b, at, :]
        if (start + STEP) % BAND == 0:
            rows = pl.ds(a * BAND, BAND)
            copies.append(send_out(field_ref.at[rows], field_out.at[rows], sems.at[2 * a]))
            copies.append(send_out(residual_ref.at[rows], residual_out.at[rows], sems.at[2 * a + 1]))

    for_own(own)
    for copy in copies:
        copy.wait()


def call(kernel, args, outs, scratch=(), hbm_outs=(), sems=0, flops=0, grant=6, scalars=0, hbm=()):
    def spec(i, inside):
        space = pltpu.SMEM if inside and i < scalars else pl.ANY if i in (hbm if inside else hbm_outs) else pltpu.VMEM
        return pl.BlockSpec(memory_space=space)

    return pl.pallas_call(
        kernel,
        out_shape=[jax.ShapeDtypeStruct(s, F32) for s in outs],
        in_specs=[spec(i, True) for i in range(len(args))],
        out_specs=[spec(i, False) for i in range(len(outs))],
        scratch_shapes=[pltpu.VMEM(s, F32) if isinstance(s, tuple) else s for s in scratch]
        + ([pltpu.SemaphoreType.DMA((sems,))] if sems else []),
        compiler_params=pltpu.CompilerParams(vmem_limit_bytes=grant * 1024 * 1024),
        cost_estimate=pl.CostEstimate(flops=flops, bytes_accessed=4 * 1024 * 1024, transcendentals=0),
    )(*args)


def exchange(x):
    return lax.all_to_all(x, AXES, 0, 0, tiled=True)


def body(rhs, depth, mask, basis, inverse):
    n_lon, n_lat = lax.axis_size("lon"), lax.axis_size("lat")
    devices = n_lon * n_lat
    total_rows = NY * n_lat
    lat = lax.axis_index("lat")
    tile = (lax.axis_index("lon") * n_lat + lat).astype(jnp.int32).reshape(1)
    full = (BLK, ROWS, LANES)
    half = (AGG_LON, NY, LANES)
    rows8 = 8 * (inverse.shape[1] // LANES)
    row = (devices, LANES)

    row_index = lat * NY - HY + jnp.arange(ROWS, dtype=jnp.int32)
    latitude = (row_index.astype(F32) + 0.5) * (2.6 / total_rows) - 1.3
    inside = ((row_index >= 0) & (row_index <= total_rows - 2)).astype(F32)
    geo = jnp.stack([1.0 / jnp.cos(latitude), jnp.cos(latitude + 1.3 / total_rows) * inside])
    geo = jnp.broadcast_to(geo[:, :, None], (2, ROWS, LANES))
    shift = jnp.broadcast_to((SHIFT_SCALE * jnp.cos(latitude))[:, None], (ROWS, LANES))

    loads = [(NY, NX), (NY, NX), pltpu.VMEM((NY, NX), jnp.int32), (NY, NX), inverse.shape]
    pack = (BAND + rows8, LANES)
    gather, to_west, to_east, edges, *fields = call(
        pack_kernel, [tile, rhs, depth, mask, basis, inverse], [row, pack, pack, (2, 3, 2, HY, LANES), half, half, half],
        scratch=loads, sems=4 * AGG_LAT + 1, scalars=1, hbm=range(1, 6), grant=60,
    )
    ring = [(i, (i + 1) % n_lon) for i in range(n_lon)]
    left = lax.ppermute(to_east, "lon", ring)
    right = lax.ppermute(to_west, "lon", [(j, i) for i, j in ring])
    got = exchange(gather)
    edge = (3 * BLK * HY + rows8, LANES)
    to_south, to_north = call(edge_kernel, [edges, inverse, left, right], [edge, edge], grant=4)
    line = [(i, i + 1) for i in range(n_lat - 1)]
    below = lax.ppermute(to_north, "lat", line)
    above = lax.ppermute(to_south, "lat", [(j, i) for i, j in line])
    solver = (inverse, left, right, below, above)

    send, east, north, weight, search, applied = call(
        search_kernel, [tile, got, *solver, *fields, geo, shift], [row] + [full] * 5, hbm_outs=range(1, 6),
        scratch=[full] * 12, sems=5, scalars=1, flops=40000000, grant=59,
    )
    got = exchange(send)
    (smoothed,) = call(
        second_kernel, [applied, east, north, weight, shift], [full], hbm=range(4),
        scratch=[full] * 9, sems=4 * len(CHUNKS), flops=20000000, grant=60,
    )
    send, known, *state = call(
        sums_kernel,
        [got, *solver, smoothed, shift, east, north, weight, search, applied, fields[1]],
        [row, (8, LANES)] + [half] * 5, hbm=range(8, 14),
        scratch=[full] * 5 + [half, full], sems=6 * len(CHUNKS), flops=8000000, grant=58,
    )
    got = exchange(send)
    field, out = call(
        final_kernel, [got, known, *state], [(NY, NX)] * 2, hbm_outs=range(2), scratch=[(NY, NX)] * 2,
        sems=2 * AGG_LAT, flops=1000000, grant=4,
    )
    return field, out


def solution(mesh):
    tile = P("lat", "lon")
    return jax.shard_map(
        body,
        mesh=mesh,
        in_specs=(tile, tile, tile, tile, P(AXES, None)),
        out_specs=(tile, tile),
        check_vma=False,
    )
```

time: 122 us -> 105 us (0.86)
  local copies, waits for them, and re-layouts: 33.5 us -> 8.99 us
  Pallas kernels: 15.9 us -> 26.1 us
  waiting for transfers between devices: 9.28 us -> 13.1 us
  starting transfers between devices: 39 us -> 35.4 us
  blocking collectives: 21.9 us -> 19.9 us
    unnamed x76 -> x28, local copies, waits for them, and re-layouts: 33.3 us -> 7.13 us
    pallas_call x7 -> x6, Pallas kernels: 15.9 us -> 26.1 us  [call(): pl.pallas_call(kernel, out_shape=[jax.ShapeDtypeStruct(s, F32) for s in o...]
    all_to_all x2, waiting for transfers between devices: 4.45 us -> 13.1 us  [exchange(): return lax.all_to_all(x, AXES, 0, 0, tiled=True)]
    ppermute x1, waiting for transfers between devices: 4.54 us -> 0.01 us  [body(): above = lax.ppermute(to_south, 'lat', [(j, i) for i, j in line])]
    all_to_all x2, starting transfers between devices: 24.7 us -> 21.2 us  [exchange(): return lax.all_to_all(x, AXES, 0, 0, tiled=True)]
    all_to_all x1, blocking collectives: 21.9 us -> 19.9 us  [exchange(): return lax.all_to_all(x, AXES, 0, 0, tiled=True)]
    broadcast_in_dim x1 -> x2, local copies, waits for them, and re-layouts: 0.27 us -> 1.85 us  [the longest x1 1.02 us: body(): geo = jnp.broadcast_to(geo[:, :, None], (2, ROWS, LANES))]
  transfers between devices with their start and end apart: 6 -> 6, of which waited for: 3 -> 2; matrix products, arithmetic and copies ran while one was open for 0% -> 0% of each run, Pallas kernels for 6% -> 6%
where the time goes in v3:
time: 105 us
  starting transfers between devices  35.4 us (34%)
  Pallas kernels  26.1 us (25%)
  blocking collectives  19.9 us (19%)
  waiting for transfers between devices  13.1 us (12%)
  local copies, waits for them, and re-layouts  8.99 us (9%)
    pallas_call x6, Pallas kernels, call(): pl.pallas_call(kernel, out_shape=[jax.ShapeDtypeStruct(s, F32) for s in o...  26.1 us
    all_to_all x2, starting transfers between devices, exchange(): return lax.all_to_all(x, AXES, 0, 0, tiled=True)  21.2 us
    all_to_all x1, blocking collectives, exchange(): return lax.all_to_all(x, AXES, 0, 0, tiled=True)  19.9 us
    all_to_all x2, waiting for transfers between devices, exchange(): return lax.all_to_all(x, AXES, 0, 0, tiled=True)  13.1 us
    unnamed x28, local copies, waits for them, and re-layouts  7.13 us
    ppermute x1, starting transfers between devices, body(): right = lax.ppermute(to_west, 'lon', [(j, i) for i, j in ring])  6.22 us
    ppermute x1, starting transfers between devices, body(): below = lax.ppermute(to_north, 'lat', line)  3.53 us
    ppermute x1, starting transfers between devices, body(): left = lax.ppermute(to_east, 'lon', ring)  2.54 us
  transfers between devices with their start and end apart: 6, of which 2 were waited for; matrix products, arithmetic and copies ran while one was open for 0% of the time, Pallas kernels for 6%

profile of v3, /device:TPU:1, one launch (start us, length us, event | category | flops | bytes accessed | tf_op | source)
XLA Modules:
  0.0 104.7 jit_solution(4036627497082650249)
XLA Ops:
  0.6 3.3 %shard_map.68 = (f32[256,128]{1,0:T(8,128)}, f32[256,128]{1,0:T(8,128)}, f32[256,128]{1,0:T(8,128)}, f32[2,3,2,16,128]{4,3,2,1,0:T(8,128)}, f32[2,512,128]{2,1,0...) custom-call(s32[1]{0:T(128)} %bitcast.tile_ref, f32[512,256]{1,0:T(8,128)} %rhs_hbm.1, f32[512,256]{1,0:T(8,128)} %depth_hbm.1, ...), custom_call_target="tpu_custom_call" | custom-call | bytes 4194304 | tf_op jit(solution)/shard_map/pallas_call | solution.py:562
  4.0 2.5 %collective-permute-start = (f32[256,128]{1,0:T(8,128)}, f32[256,128]{1,0:T(8,128)S(1)}, u32[]{:S(2)}, u32[]{:S(2)}) collective-permute-start(f32[256,128]{1,0:T(8,128)} %get-tuple-element.25), channel_id=1, source_target_pairs={{0,8},{8,16},{16,24},{24,32},{32,40},{40,48},{48,56},{56,64},{64,7... | collective-permute-start | bytes 393224 | tf_op jit(solution)/shard_map/ppermute | solution.py:603
  6.5 6.2 %collective-permute-start.1 = (f32[256,128]{1,0:T(8,128)}, f32[256,128]{1,0:T(8,128)S(1)}, u32[]{:S(2)}, u32[]{:S(2)}) collective-permute-start(f32[256,128]{1,0:T(8,128)} %get-tuple-element.26), channel_id=1, source_target_pairs={{8,0},{16,8},{24,16},{32,24},{40,32},{48,40},{56,48},{64,56},{72,6... | collective-permute-start | bytes 393224 | tf_op jit(solution)/shard_map/ppermute | solution.py:604
  12.7 10.2 %all-to-all-start = ((f32[256,1,128]{2,1,0:T(1,128)}), f32[256,1,128]{2,1,0:T(1,128)S(1)}, u32[]{:S(2)}, u32[]{:S(2)}) async-start(f32[256,1,128]{2,1,0:T(1,128)} %bitcast.16), calls=%async_computation | async-start | bytes 262144 | tf_op jit(solution)/shard_map/all_to_all | solution.py:575
  23.3 0.5 copy-done
  23.9 3.5 %collective-permute-start.2 = (f32[272,128]{1,0:T(8,128)S(1)}, f32[272,128]{1,0:T(8,128)S(1)}, u32[]{:S(2)}, u32[]{:S(2)}) collective-permute-start(f32[272,128]{1,0:T(8,128)S(1)} %get-tuple-element.28), channel_id=1, source_target_pairs={{0,1},{1,2},{2,3},{3,4},{4,5},{5,6},{6,7},{8,9},{9,10},{10,11},{11... | collective-permute-start | bytes 417800 | tf_op jit(solution)/shard_map/ppermute | solution.py:609
  27.4 1.9 %collective-permute-start.3 = (f32[272,128]{1,0:T(8,128)S(1)}, f32[272,128]{1,0:T(8,128)S(1)}, u32[]{:S(2)}, u32[]{:S(2)}) collective-permute-start(f32[272,128]{1,0:T(8,128)S(1)} %get-tuple-element.29), channel_id=1, source_target_pairs={{1,0},{2,1},{3,2},{4,3},{5,4},{6,5},{7,6},{9,8},{10,9},{11,10},{12... | collective-permute-start | bytes 417800 | tf_op jit(solution)/shard_map/ppermute | solution.py:610
  29.4 6.4 %all-to-all-done = f32[256,1,128]{2,1,0:T(1,128)S(1)} async-done(((f32[256,1,128]{2,1,0:T(1,128)}), f32[256,1,128]{2,1,0:T(1,128)S(1)}, u32[]{:S(2)}, u32[]{:S(2)}) %all-to-all-start) | async-done | bytes 131104 | tf_op jit(solution)/shard_map/all_to_all | solution.py:575
  35.8 0.8 broadcast_in_dim.5.shift_ref
  36.7 1.0 broadcast_in_dim.4.geo_ref
  37.7 9.5 %shard_map.70 = (f32[256,128]{1,0:T(8,128)}, f32[3,544,128]{2,1,0:T(8,128)}, f32[3,544,128]{2,1,0:T(8,128)}, f32[3,544,128]{2,1,0:T(8,128)}, f32[3,544,128]{2,1,0:T(8,128)}, /*index=5*/f32[3,544,128]{2,1,0:T(8,128)}) custom-call(s32[1]{0:T(128)} %bitcast.tile_ref, f32[256,128]{1,0:T(8,128)} %bitcast.15, f32[8,2048]{1,0:T(8,128)} %inverse_ref.5, ...), custom_call_target="tpu_custom_call" | custom-call | flops 40000000 | bytes 4194304 | tf_op jit(solution)/shard_map/pallas_call | solution.py:562
  47.2 11.0 %all-to-all-start.1 = ((f32[256,1,128]{2,1,0:T(1,128)}), f32[256,1,128]{2,1,0:T(1,128)S(1)}, u32[]{:S(2)}, u32[]{:S(2)}) async-start(f32[256,1,128]{2,1,0:T(1,128)} %bitcast.18), calls=%async_computation.1 | async-start | bytes 262144 | tf_op jit(solution)/shard_map/all_to_all | solution.py:575
  58.2 6.2 %shard_map.71.smooth_ref = f32[3,544,128]{2,1,0:T(8,128)} custom-call(f32[3,544,128]{2,1,0:T(8,128)} %get-tuple-element.34.applied_hbm, f32[3,544,128]{2,1,0:T(8,128)} %get-tuple-element.35.east_hbm, f32[3,544,128]{2,1,0:T(8,128)} %get-tuple-element.36.north_hbm, f32[3,544,128]{2,1,0:T(8,128)} %get-tuple-element.37.weight_hbm, ...), custom_call_target="tpu_custom_call" | custom-call | flops 20000000 | bytes 4194304 | tf_op jit(solution)/shard_map/pallas_call | solution.py:562
  64.4 6.7 %all-to-all-done.1 = f32[256,1,128]{2,1,0:T(1,128)S(1)} async-done(((f32[256,1,128]{2,1,0:T(1,128)}), f32[256,1,128]{2,1,0:T(1,128)S(1)}, u32[]{:S(2)}, u32[]{:S(2)}) %all-to-all-start.1) | async-done | bytes 131104 | tf_op jit(solution)/shard_map/all_to_all | solution.py:575
  71.1 0.7 copy-done.12
  71.7 5.8 %shard_map.72 = (f32[256,128]{1,0:T(8,128)}, f32[8,128]{1,0:T(8,128)}, f32[2,512,128]{2,1,0:T(8,128)}, f32[2,512,128]{2,1,0:T(8,128)}, f32[2,512,128]{2,1,0:T(8,...) custom-call(f32[256,128]{1,0:T(8,128)} %bitcast.14, f32[8,2048]{1,0:T(8,128)} %inverse_ref.5, f32[256,128]{1,0:T(8,128)} %copy-done, ...), custom_call_target="tpu_custom_call" | custom-call | flops 8000000 | bytes 4194304 | tf_op jit(solution)/shard_map/pallas_call | solution.py:562
  77.5 19.9 %all_to_all.33 = f32[256,1,128]{2,1,0:T(1,128)S(1)} all-to-all(f32[256,1,128]{2,1,0:T(1,128)} %bitcast.17), channel_id=1, replica_groups=mesh['lon'=32,'lat'=8] {'lon','lat'}, dimensions={0} | all-to-all | bytes 262144 | tf_op jit(solution)/shard_map/all_to_all | solution.py:575
  97.5 0.7 copy-done.9
  98.1 1.0 copy-done.3
  99.2 1.0 copy-done.4
  100.2 1.0 copy-done.5
  101.3 1.0 copy-done.6
  102.3 1.0 copy-done.7
  103.3 1.2 %shard_map.73 = (f32[512,256]{1,0:T(8,128)}, f32[512,256]{1,0:T(8,128)}) custom-call(f32[256,128]{1,0:T(8,128)S(1)} %bitcast.13, f32[8,128]{1,0:T(8,128)S(1)} %copy-done.9, f32[2,512,128]{2,1,0:T(8,128)S(1)} %copy-done.3, f32[2,512,128]{2,1,0:T(8,128)S(1)} %copy-done.4, f32[2,512,128]{2,1,0:T(8,128)S(1)} %copy-done.5, f32[2,512,128]{2,1,0:T(8,128)S(1)} %copy-done.6, ...), custom_call_target="tpu_custom_call" | custom-call | flops 1000000 | bytes 4194304 | tf_op jit(solution)/shard_map/pallas_call | solution.py:562
  (28 shorter events, 0.4 us)
Async XLA Ops:
  4.0 19.2 %collective-permute-start = (f32[256,128]{1,0:T(8,128)}, f32[256,128]{1,0:T(8,128)S(1)}, u32[]{:S(2)}, u32[]{:S(2)}) collective-permute-start(f32[256,128]{1,0:T(8,128)} %get-tuple-element.25), channel_id=1, source_target_pairs={{0,8},{8,16},{16,24},{24,32},{32,40},{40,48},{48,56},{56,64},{64,7... | collective-permute-start | bytes 393224 | tf_op jit(solution)/shard_map/ppermute | solution.py:603
  6.5 16.6 %collective-permute-start.1 = (f32[256,128]{1,0:T(8,128)}, f32[256,128]{1,0:T(8,128)S(1)}, u32[]{:S(2)}, u32[]{:S(2)}) collective-permute-start(f32[256,128]{1,0:T(8,128)} %get-tuple-element.26), channel_id=1, source_target_pairs={{8,0},{16,8},{24,16},{32,24},{40,32},{48,40},{56,48},{64,56},{72,6... | collective-permute-start | bytes 393224 | tf_op jit(solution)/shard_map/ppermute | solution.py:604
  12.7 10.4 %copy-start.2 = (f32[8,2048]{1,0:T(8,128)S(1)}, f32[8,2048]{1,0:T(8,128)}, u32[]{:S(2)}) copy-start(f32[8,2048]{1,0:T(8,128)} %inverse_ref.5) | copy-start | bytes 196612
  12.7 10.4 %copy-start.8 = (f32[2,3,2,16,128]{4,3,2,1,0:T(8,128)S(1)}, f32[2,3,2,16,128]{4,3,2,1,0:T(8,128)}, u32[]{:S(2)}) copy-start(f32[2,3,2,16,128]{4,3,2,1,0:T(8,128)} %get-tuple-element.27.edge_ref) | copy-start | bytes 294916
  12.7 23.1 %all-to-all-start = ((f32[256,1,128]{2,1,0:T(1,128)}), f32[256,1,128]{2,1,0:T(1,128)S(1)}, u32[]{:S(2)}, u32[]{:S(2)}) async-start(f32[256,1,128]{2,1,0:T(1,128)} %bitcast.16), calls=%async_computation | async-start | bytes 262144 | tf_op jit(solution)/shard_map/all_to_all | solution.py:575
  23.1 0.6 copy-start
  23.2 0.7 copy-start.1
  23.9 12.0 %collective-permute-start.2 = (f32[272,128]{1,0:T(8,128)S(1)}, f32[272,128]{1,0:T(8,128)S(1)}, u32[]{:S(2)}, u32[]{:S(2)}) collective-permute-start(f32[272,128]{1,0:T(8,128)S(1)} %get-tuple-element.28), channel_id=1, source_target_pairs={{0,1},{1,2},{2,3},{3,4},{4,5},{5,6},{6,7},{8,9},{9,10},{10,11},{11... | collective-permute-start | bytes 417800 | tf_op jit(solution)/shard_map/ppermute | solution.py:609
  27.4 8.4 %collective-permute-start.3 = (f32[272,128]{1,0:T(8,128)S(1)}, f32[272,128]{1,0:T(8,128)S(1)}, u32[]{:S(2)}, u32[]{:S(2)}) collective-permute-start(f32[272,128]{1,0:T(8,128)S(1)} %get-tuple-element.29), channel_id=1, source_target_pairs={{1,0},{2,1},{3,2},{4,3},{5,4},{6,5},{7,6},{9,8},{10,9},{11,10},{12... | collective-permute-start | bytes 417800 | tf_op jit(solution)/shard_map/ppermute | solution.py:610
  35.8 1.9 %copy-start.13 = (f32[256,1,128]{2,1,0:T(1,128)}, f32[256,1,128]{2,1,0:T(1,128)S(1)}, u32[]{:S(2)}) copy-start(f32[256,1,128]{2,1,0:T(1,128)S(1)} %all-to-all-done) | copy-start | bytes 393220
  35.8 0.9 copy-start.10
  35.8 0.8 copy-start.11
  47.2 23.8 %all-to-all-start.1 = ((f32[256,1,128]{2,1,0:T(1,128)}), f32[256,1,128]{2,1,0:T(1,128)S(1)}, u32[]{:S(2)}, u32[]{:S(2)}) async-start(f32[256,1,128]{2,1,0:T(1,128)} %bitcast.18), calls=%async_computation.1 | async-start | bytes 262144 | tf_op jit(solution)/shard_map/all_to_all | solution.py:575
  71.1 0.7 copy-start.12
  97.5 0.7 copy-start.9
  98.1 1.0 copy-start.3
  99.2 1.0 copy-start.4
  100.2 1.0 copy-start.5
  101.3 1.0 copy-start.6
  102.3 1.0 copy-start.7

commit v4 on v3

--- a/solution.py
+++ b/solution.py
@@ -1,4 +1,5 @@
 import functools
+import math
 
 import jax
 import jax.numpy as jnp
@@ -41,6 +42,25 @@
         pairs.append((fresh * previous, 2.0 * fresh / interval_half))
         previous = fresh
     return 1.0 / interval_mid, pairs
+
+
+def cosine(x):
+    square = x * x
+    out = jnp.full_like(x, -1.0 / math.factorial(14))
+    for k in range(6, -1, -1):
+        out = out * square + (-1.0) ** k / math.factorial(2 * k)
+    return out
+
+
+def place():
+    lat = lax.axis_index("lat")
+    return lax.axis_index("lon") * lax.axis_size("lat") + lat, lat * NY
+
+
+def latitudes(spot, total_rows, start, rows):
+    index = spot[1] - HY + start + lax.broadcasted_iota(jnp.int32, (rows, LANES), 0)
+    inside = (index >= 0) & (index <= total_rows - 2)
+    return (index.astype(F32) + 0.5) * (2.6 / total_rows) - 1.3, inside
 
 
 def lane_ids(rows):
@@ -111,10 +131,10 @@
     return jnp.sum(jnp.sum(x, axis=1, keepdims=True), axis=0, keepdims=True)
 
 
-def own_row(tile_ref, values, scalars=()):
+def own_row(spot, values, scalars=()):
     lane = lane_ids(1)
-    base = (tile_ref[0] % SLOTS) * 8
-    other = ((tile_ref[0] + SLOTS // 2) % SLOTS) * 8
+    base = (spot[0] % SLOTS) * 8
+    other = ((spot[0] + SLOTS // 2) % SLOTS) * 8
     row = jnp.zeros((1, LANES), F32)
     for k, value in enumerate(values):
         row = jnp.where(lane == base + k, value, row)
@@ -137,10 +157,11 @@
 
 
 def pack_kernel(
-    tile_ref, rhs_hbm, depth_hbm, mask_hbm, basis_hbm, inverse_hbm,
-    gather_ref, west_ref, east_ref, edge_ref, wet_ref, res_ref, weight_ref,
-    rhs_ref, depth_ref, mask_ref, basis_ref, inverse_ref, sems,
+    rhs_hbm, depth_hbm, mask_hbm, basis_hbm, inverse_hbm,
+    gather_ref, west_ref, east_ref, edge_ref, fields_out,
+    rhs_ref, depth_ref, mask_ref, basis_ref, inverse_ref, fields_ref, sems,
 ):
+    spot = place()
     pairs = ((rhs_hbm, rhs_ref), (mask_hbm, mask_ref), (basis_hbm, basis_ref), (depth_hbm, depth_ref))
     copies = []
     for g in range(AGG_LAT):
@@ -153,7 +174,7 @@
         copy.start()
     groups = inverse_ref.shape[1] // LANES
     lane = lane_ids(STEP)
-    sums = []
+    sums, outs = [], []
     zero = jnp.zeros((8, LANES), F32)
     for g in range(AGG_LAT):
         for copy in copies[g]:
@@ -170,8 +191,8 @@
                 weight = basis_ref[at] * mask
                 accs[b] = accs[b] + fold(weight * res)
                 fields.append((wet, res, weight))
-                for f, (ref, value) in enumerate(zip((wet_ref, res_ref, weight_ref), fields[b])):
-                    ref[b, start : start + STEP, :] = value
+                for f, value in enumerate(fields[b]):
+                    fields_ref[f, b, start : start + STEP, :] = value
                     for side, first in ((0, 0), (1, NY - HY)):
                         if start == first:
                             edge_ref[side, f, b] = value
@@ -183,12 +204,16 @@
                     packed = jnp.where((lane >= lo) & (lane < lo + WX), moved, packed)
                 ref[out_row : out_row + STEP, :] = packed
         sums += [total(acc) for acc in accs]
-    fill_rows(gather_ref, own_row(tile_ref, sums))
+        rows = (slice(None), slice(None), pl.ds(g * BAND, BAND))
+        outs.append(send_out(fields_ref.at[rows], fields_out.at[rows], sems.at[4 * AGG_LAT + 1 + g]))
+    fill_rows(gather_ref, own_row(spot, sums))
     last.wait()
     for g in range(groups):
         part = inverse_ref[:, g * LANES : (g + 1) * LANES]
         west_ref[BAND + 8 * g : BAND + 8 * g + 8, :] = part
         east_ref[BAND + 8 * g : BAND + 8 * g + 8, :] = part
+    for copy in outs:
+        copy.wait()
 
 
 def unpack_columns(left_ref, right_ref, g, start, rows):
@@ -203,8 +228,13 @@
     return out
 
 
-def edge_kernel(edge_ref, inverse_ref, left_ref, right_ref, south_ref, north_ref):
-    groups = inverse_ref.shape[1] // LANES
+def edge_kernel(edge_hbm, pack_hbm, left_ref, right_ref, south_ref, north_ref, solver_ref, edge_ref, pack_ref, sems):
+    for copy in fetch(((edge_hbm, edge_ref), (pack_hbm, pack_ref)), sems, 0):
+        copy.wait()
+    rows8 = pack_ref.shape[0] - BAND
+    for k, ref in enumerate((pack_ref, left_ref, right_ref)):
+        solver_ref[k * rows8 : (k + 1) * rows8, :] = ref[BAND:, :]
+    groups = (pack_ref.shape[0] - BAND) // 8
     sub = lax.broadcasted_iota(jnp.int32, (8, LANES), 0)
     for side, (ref, start, band) in enumerate(((south_ref, 0, 0), (north_ref, BAND - HY, AGG_LAT - 1))):
         halo = unpack_columns(left_ref, right_ref, band, start, HY)
@@ -214,9 +244,8 @@
                 ref[at : at + HY, :] = edge_ref[side, f, b] if b < 2 else halo[f]
         base = 3 * BLK * HY
         for i in range(groups):
-            own = inverse_ref[:, i * LANES : (i + 1) * LANES]
-            left = left_ref[BAND + 8 * i : BAND + 8 * i + 8, :]
-            right = right_ref[BAND + 8 * i : BAND + 8 * i + 8, :]
+            at = slice(BAND + 8 * i, BAND + 8 * i + 8)
+            own, left, right = pack_ref[at, :], left_ref[at, :], right_ref[at, :]
             own = pltpu.roll(own, (8 - 2 * band) % 8, 0) if band else own
             left = pltpu.roll(left, (2 - 2 * band - 1 + 16) % 8, 0)
             right = pltpu.roll(right, (3 - 2 * band + 16) % 8, 0)
@@ -224,8 +253,24 @@
             ref[base + 8 * i : base + 8 * i + 8, :] = picked
 
 
-def west_of_faces(east_ref, west_ref, start, rows):
-    store(west_ref, start, rows, west_of(load(east_ref, start, rows)))
+def north_faces(spot, total_rows, wet_ref, north_ref, start, rows):
+    wet, nxt = load(wet_ref, start, rows), load(wet_ref, start + 1, rows)
+    latitude, inside = latitudes(spot, total_rows, start, rows)
+    cos_row = jnp.where(inside, cosine(latitude + 1.3 / total_rows), 0.0)
+    store(north_ref, start, rows, [jnp.minimum(wet[b], nxt[b]) * cos_row for b in range(BLK)])
+
+
+def all_faces(spot, total_rows, wet_ref, faces, start, rows):
+    east_ref, west_ref, north_ref, shift_ref = faces
+    wet = load(wet_ref, start, rows)
+    cos_row = cosine(latitudes(spot, total_rows, start, rows)[0])
+    shift_ref[pl.ds(start, rows), :] = SHIFT_SCALE * cos_row
+    over = 1.0 / cos_row
+    nxt = east_of(wet)
+    face = [jnp.minimum(wet[b], nxt[b]) * over for b in range(BLK)]
+    store(east_ref, start, rows, face)
+    store(west_ref, start, rows, west_of(face))
+    north_faces(spot, total_rows, wet_ref, north_ref, start, rows)
 
 
 def first_step(res_ref, inv_ref, faces, est_ref, step_ref, start, rows):
@@ -264,24 +309,18 @@
             for_strips(strip)
 
 
-def coarse_solve(got_ref, inverse_ref, left_ref, right_ref, below_ref, above_ref):
-    groups = inverse_ref.shape[1] // LANES
-    count = got_ref.shape[0] // groups
-    base = 3 * BLK * HY
-    accs = [jnp.zeros((8, LANES), F32) for _ in range(5)]
-    mine = lane_ids(count) // 8 == lax.broadcasted_iota(jnp.int32, (count, LANES), 0)
+def fetch(pairs, sems, first):
+    return [send_out(src, dst, sems.at[first + k]) for k, (src, dst) in enumerate(pairs)]
+
+
+def coarse_solve(got_ref, parts):
+    groups = got_ref.shape[0] // SLOTS
+    accs = [jnp.zeros((8, LANES), F32) for _ in parts]
+    mine = lane_ids(SLOTS) // 8 == lax.broadcasted_iota(jnp.int32, (SLOTS, LANES), 0)
     for i in range(groups):
-        vec = jnp.sum(jnp.where(mine, got_ref[i * count : (i + 1) * count, :], 0.0), axis=0, keepdims=True)
-        at = slice(BAND + 8 * i, BAND + 8 * i + 8)
-        band = slice(base + 8 * i, base + 8 * i + 8)
-        parts = (
-            inverse_ref[:, i * LANES : (i + 1) * LANES],
-            left_ref[at, :],
-            right_ref[at, :],
-            below_ref[band, :],
-            above_ref[band, :],
-        )
-        accs = [acc + part * vec for acc, part in zip(accs, parts)]
+        vec = jnp.sum(jnp.where(mine, got_ref[i * SLOTS : (i + 1) * SLOTS, :], 0.0), axis=0, keepdims=True)
+        for k, (ref, first) in enumerate(parts):
+            accs[k] = accs[k] + ref[first + 8 * i : first + 8 * i + 8, :] * vec
     own, left, right, below, above = [jnp.sum(acc, axis=1, keepdims=True) for acc in accs]
     low = lane_ids(1) < LANES // 2
 
@@ -307,17 +346,22 @@
 
 
 class Stream:
-    def __init__(self, pairs, sems, first=0):
+    def __init__(self, src, refs, sems):
         self.chunks, self.done, self.rows = [], 0, 0
-        for start, rows in CHUNKS:
+        for k, (start, rows) in enumerate(CHUNKS):
             chunk = []
-            for src, dst in pairs:
-                lo, hi = start, start + rows
-                if src.shape[1] == NY:
-                    lo, hi = min(max(lo - HY, 0), NY), min(max(hi - HY, 0), NY)
-                at = (slice(None), pl.ds(lo, hi - lo), slice(None))
-                chunk.append(pltpu.make_async_copy(src.at[at], dst.at[at], sems.at[first]))
-                first += 1
+            for i, dst in enumerate(refs):
+                if dst.shape[0] == BLK:
+                    lo, hi, shift = start, start + rows, 0
+                else:
+                    lo, hi, shift = max(start, HY), min(start + rows, HY + NY), HY
+                chunk.append(
+                    pltpu.make_async_copy(
+                        src.at[i, 0 : dst.shape[0], lo:hi, :],
+                        dst.at[:, lo - shift : hi - shift, :],
+                        sems.at[k * len(refs) + i],
+                    )
+                )
             for copy in chunk:
                 copy.start()
             self.chunks.append(chunk)
@@ -337,44 +381,45 @@
 
 
 def search_kernel(
-    tile_ref, got_ref, inverse_ref, left_ref, right_ref, below_ref, above_ref,
-    wet_in, res_in, weight_in, geo_ref, shift_ref,
-    send_ref, east_out, north_out, weight_out, search_out, applied_out,
-    wet_ref, res_ref, weight_ref, east_ref, west_ref, north_ref, inv_ref,
-    est_a, est_b, step_ref, search_ref, applied_ref, sems,
+    total_rows,
+    got_ref, solver_ref, left_ref, right_ref, below_ref, above_ref, fields_hbm,
+    send_ref, wet_ref, applied_ref, carry_out,
+    fields_ref, east_ref, north_ref, res_ref, weight_ref, west_ref, inv_ref, est_a, est_b, step_ref, search_ref, shift_ref, sems,
 ):
+    spot = place()
     fields = (wet_ref, res_ref, weight_ref)
-    for f, (src, ref) in enumerate(zip((wet_in, res_in, weight_in), fields)):
+    bands = [(slice(None), slice(None), pl.ds(a * BAND, BAND)) for a in range(AGG_LAT)]
+    copies = [send_out(fields_hbm.at[at], fields_ref.at[at], sems.at[5 + a]) for a, at in enumerate(bands)]
+    for f, ref in enumerate(fields):
         for b in range(BLK):
             at = (f * BLK + b) * HY
             ref[b, 0:HY, :] = below_ref[at : at + HY, :]
             ref[b, HY + NY : ROWS, :] = above_ref[at : at + HY, :]
 
     def fill(g, start):
+        if start % BAND == 0:
+            copies[g].wait()
         at = slice(HY + start, HY + start + STEP)
         halo = unpack_columns(left_ref, right_ref, g, start - g * BAND, STEP)
-        for f, (src, ref) in enumerate(zip((wet_in, res_in, weight_in), fields)):
+        for f, ref in enumerate(fields):
             for b in range(2):
-                ref[b, at, :] = src[b, start : start + STEP, :]
+                ref[b, at, :] = fields_ref[f, b, start : start + STEP, :]
             ref[2, at, :] = halo[f]
 
     for_own(fill)
-    outs = [send_out(weight_ref, weight_out, sems.at[0])]
-
-    def east_west(start, rows):
-        wet = load(wet_ref, start, rows)
-        over = geo_ref[0, pl.ds(start, rows), :]
-        nxt = east_of(wet)
-        face = [jnp.minimum(wet[b], nxt[b]) * over for b in range(BLK)]
-        store(east_ref, start, rows, face)
-        store(west_ref, start, rows, west_of(face))
-
-    def north(start, rows):
-        wet, nxt = load(wet_ref, start, rows), load(wet_ref, start + 1, rows)
-        cosine = geo_ref[1, pl.ds(start, rows), :]
-        store(north_ref, start, rows, [jnp.minimum(wet[b], nxt[b]) * cosine for b in range(BLK)])
-
-    north(0, 8)
+    own_rows = (slice(0, AGG_LON), slice(HY, HY + NY))
+    outs = [
+        send_out(weight_ref, carry_out.at[0], sems.at[0]),
+        send_out(res_ref.at[own_rows], carry_out.at[5].at[own_rows], sems.at[3]),
+    ]
+    base, rows8 = 3 * BLK * HY, solver_ref.shape[0] // 3
+    outs += [
+        send_out(solver_ref, carry_out.at[6, 0, 0 : 3 * rows8], sems.at[10]),
+        send_out(below_ref.at[base : base + rows8], carry_out.at[6, 1, 0:rows8], sems.at[11]),
+        send_out(above_ref.at[base : base + rows8], carry_out.at[6, 2, 0:rows8], sems.at[12]),
+    ]
+
+    north_faces(spot, total_rows, wet_ref, north_ref, 0, 8)
     for ref in (est_a, est_b, search_ref, applied_ref, east_ref):
         clear_ends(ref)
     for b in range(BLK):
@@ -382,13 +427,13 @@
     faces = (east_ref, west_ref, north_ref, shift_ref)
 
     def prepare(start, rows):
-        east_west(start, rows)
-        north(start, rows)
+        all_faces(spot, total_rows, wet_ref, faces, start, rows)
         first_step(res_ref, inv_ref, faces, est_a, step_ref, start, rows)
 
     for_strips(prepare)
-    outs += [send_out(east_ref, east_out, sems.at[1]), send_out(north_ref, north_out, sems.at[2])]
-    coarse = coarse_solve(got_ref, inverse_ref, left_ref, right_ref, below_ref, above_ref)
+    outs += [send_out(east_ref, carry_out.at[2], sems.at[4]), send_out(north_ref, carry_out.at[3], sems.at[9])]
+    parts = [(solver_ref, k * rows8) for k in range(3)] + [(below_ref, base), (above_ref, base)]
+    coarse = coarse_solve(got_ref, parts)
 
     def finish(start, rows, band, value):
         wet, weight = load(wet_ref, start, rows), load(weight_ref, start, rows)
@@ -396,7 +441,7 @@
         store(search_ref, start, rows, [part[b] + weight[b] * coarse[band][b] for b in range(BLK)])
 
     smooth(res_ref, inv_ref, faces, (est_a, est_b), step_ref, finish)
-    outs.append(send_out(search_ref, search_out, sems.at[3]))
+    outs.append(send_out(search_ref, carry_out.at[1], sems.at[1]))
     sums = [jnp.zeros((8, LANES), F32)] * (AGG_LAT * AGG_LON + 2)
 
     def apply(start, rows, band):
@@ -410,54 +455,53 @@
                 sums[-1] = sums[-1] + fold(here[b] * res_ref[at])
 
     for_bands(apply)
-    outs.append(send_out(applied_ref, applied_out, sems.at[4]))
+    outs.append(send_out(applied_ref.at[own_rows], carry_out.at[4].at[own_rows], sems.at[2]))
     values = [total(x) for x in sums]
-    fill_rows(send_ref, own_row(tile_ref, values[:-2], values[-2:]))
+    fill_rows(send_ref, own_row(spot, values[:-2], values[-2:]))
     for copy in outs:
         copy.wait()
 
 
 def second_kernel(
-    applied_hbm, east_hbm, north_hbm, weight_hbm, shift_ref,
+    total_rows,
+    applied_ref, wet_ref,
     out_ref,
-    applied_ref, east_ref, north_ref, weight_ref, west_ref, inv_ref, est_a, est_b, step_ref, sems,
+    east_ref, north_ref, west_ref, inv_ref, est_a, est_b, step_ref, shift_ref,
 ):
-    stream = Stream(
-        ((applied_hbm, applied_ref), (east_hbm, east_ref), (north_hbm, north_ref), (weight_hbm, weight_ref)), sems
-    )
-    for ref in (est_a, est_b, out_ref):
+    spot = place()
+    north_faces(spot, total_rows, wet_ref, north_ref, 0, 8)
+    for ref in (est_a, est_b):
         clear_ends(ref)
     faces = (east_ref, west_ref, north_ref, shift_ref)
 
     def prepare(start, rows):
-        stream.need(start + rows)
-        west_of_faces(east_ref, west_ref, start, rows)
+        all_faces(spot, total_rows, wet_ref, faces, start, rows)
         first_step(applied_ref, inv_ref, faces, est_a, step_ref, start, rows)
 
     for_strips(prepare)
-    stream.need(ROWS)
 
     def finish(start, rows, band, value):
-        weight = load(weight_ref, start, rows)
-        store(out_ref, start, rows, [jnp.where(weight[b] > 0.0, value[b], 0.0) for b in range(BLK)])
+        store(out_ref, start, rows, value)
 
     smooth(applied_ref, inv_ref, faces, (est_a, est_b), step_ref, finish)
 
 
 def sums_kernel(
-    got_ref, inverse_ref, left_ref, right_ref, below_ref, above_ref, smooth_ref, shift_ref,
-    east_hbm, north_hbm, weight_hbm, search_hbm, applied_hbm, res_hbm,
-    send_ref, known_ref, search_out, applied_out, update_ref, operated_ref, rest_ref,
-    east_ref, north_ref, weight_ref, search_ref, applied_ref, res_ref, full_ref, sems,
+    total_rows,
+    got_ref, smooth_ref, carry_hbm,
+    send_ref, known_ref, search_out, applied_ref, update_ref, operated_ref, rest_ref,
+    solver_ref, weight_ref, search_ref, east_ref, north_ref, res_ref, full_ref, sems,
 ):
-    stream = Stream(
-        (
-            (weight_hbm, weight_ref), (search_hbm, search_ref), (east_hbm, east_ref),
-            (north_hbm, north_ref), (applied_hbm, applied_ref), (res_hbm, res_ref),
-        ),
-        sems,
-    )
-    coarse = coarse_solve(got_ref, inverse_ref, left_ref, right_ref, below_ref, above_ref)
+    spot = place()
+    rows8 = solver_ref.shape[0] // 5
+    pairs = [(carry_hbm.at[6, 0, 0 : 3 * rows8], solver_ref.at[0 : 3 * rows8])]
+    for k in (1, 2):
+        pairs.append((carry_hbm.at[6, k, 0:rows8], solver_ref.at[(k + 2) * rows8 : (k + 3) * rows8]))
+    solver = fetch(pairs, sems, 6 * len(CHUNKS))
+    stream = Stream(carry_hbm, (weight_ref, search_ref, east_ref, north_ref, applied_ref, res_ref), sems)
+    for copy in solver:
+        copy.wait()
+    coarse = coarse_solve(got_ref, [(solver_ref, k * rows8) for k in range(5)])
     curvature, projection = own_row_sums(got_ref, 2)
     lane = lane_ids(1)
     alpha = jnp.broadcast_to(projection, (1, LANES)) / jnp.broadcast_to(curvature, (1, LANES))
@@ -468,7 +512,10 @@
         part, weight, search = [load(ref, start, rows) for ref in (smooth_ref, weight_ref, search_ref)]
         store(
             full_ref, start, rows,
-            [search[b] - alpha * (part[b] + weight[b] * coarse[band][b]) for b in range(BLK)],
+            [
+                search[b] - alpha * (jnp.where(weight[b] > 0.0, part[b], 0.0) + weight[b] * coarse[band][b])
+                for b in range(BLK)
+            ],
         )
 
     accs = [jnp.zeros((8, LANES), F32)] * 4
@@ -481,7 +528,7 @@
         ef = load(east_ref, start, STEP)
         wf = west_of(ef)
         nf, sf = load(north_ref, start, STEP), load(north_ref, start - 1, STEP)
-        shift = shift_ref[pl.ds(start, STEP), :]
+        shift = SHIFT_SCALE * cosine(latitudes(spot, total_rows, start, STEP)[0])
         for b in range(AGG_LON):
             out = (
                 shift * here[b]
@@ -490,10 +537,9 @@
                 + nf[b] * (here[b] - up[b])
                 + sf[b] * (here[b] - down[b])
             )
-            search, applied = search_ref[b, start : start + STEP, :], applied_ref[b, start : start + STEP, :]
+            search, applied = search_ref[b, start : start + STEP, :], applied_ref[b, at, :]
             rest = res_ref[b, at, :] - alpha * applied
             search_out[b, at, :] = search
-            applied_out[b, at, :] = applied
             update_ref[b, at, :] = here[b]
             operated_ref[b, at, :] = out
             rest_ref[b, at, :] = rest
@@ -554,10 +600,9 @@
         copy.wait()
 
 
-def call(kernel, args, outs, scratch=(), hbm_outs=(), sems=0, flops=0, grant=6, scalars=0, hbm=()):
+def call(kernel, args, outs, scratch=(), hbm_outs=(), sems=0, flops=0, grant=6, hbm=()):
     def spec(i, inside):
-        space = pltpu.SMEM if inside and i < scalars else pl.ANY if i in (hbm if inside else hbm_outs) else pltpu.VMEM
-        return pl.BlockSpec(memory_space=space)
+        return pl.BlockSpec(memory_space=pl.ANY if i in (hbm if inside else hbm_outs) else pltpu.VMEM)
 
     return pl.pallas_call(
         kernel,
@@ -566,7 +611,7 @@
         out_specs=[spec(i, False) for i in range(len(outs))],
         scratch_shapes=[pltpu.VMEM(s, F32) if isinstance(s, tuple) else s for s in scratch]
         + ([pltpu.SemaphoreType.DMA((sems,))] if sems else []),
-        compiler_params=pltpu.CompilerParams(vmem_limit_bytes=grant * 1024 * 1024),
+        compiler_params=pltpu.CompilerParams(vmem_limit_bytes=int(grant * 1024 * 1024)),
         cost_estimate=pl.CostEstimate(flops=flops, bytes_accessed=4 * 1024 * 1024, transcendentals=0),
     )(*args)
 
@@ -579,51 +624,44 @@
     n_lon, n_lat = lax.axis_size("lon"), lax.axis_size("lat")
     devices = n_lon * n_lat
     total_rows = NY * n_lat
-    lat = lax.axis_index("lat")
-    tile = (lax.axis_index("lon") * n_lat + lat).astype(jnp.int32).reshape(1)
     full = (BLK, ROWS, LANES)
     half = (AGG_LON, NY, LANES)
     rows8 = 8 * (inverse.shape[1] // LANES)
     row = (devices, LANES)
 
-    row_index = lat * NY - HY + jnp.arange(ROWS, dtype=jnp.int32)
-    latitude = (row_index.astype(F32) + 0.5) * (2.6 / total_rows) - 1.3
-    inside = ((row_index >= 0) & (row_index <= total_rows - 2)).astype(F32)
-    geo = jnp.stack([1.0 / jnp.cos(latitude), jnp.cos(latitude + 1.3 / total_rows) * inside])
-    geo = jnp.broadcast_to(geo[:, :, None], (2, ROWS, LANES))
-    shift = jnp.broadcast_to((SHIFT_SCALE * jnp.cos(latitude))[:, None], (ROWS, LANES))
-
     loads = [(NY, NX), (NY, NX), pltpu.VMEM((NY, NX), jnp.int32), (NY, NX), inverse.shape]
     pack = (BAND + rows8, LANES)
-    gather, to_west, to_east, edges, *fields = call(
-        pack_kernel, [tile, rhs, depth, mask, basis, inverse], [row, pack, pack, (2, 3, 2, HY, LANES), half, half, half],
-        scratch=loads, sems=4 * AGG_LAT + 1, scalars=1, hbm=range(1, 6), grant=60,
+    gather, to_west, to_east, edges, fields = call(
+        pack_kernel, [rhs, depth, mask, basis, inverse], [row, pack, pack, (2, 3, 2, HY, LANES), (3, *half)], hbm_outs=(4,),
+        scratch=[*loads, (3, *half)], sems=5 * AGG_LAT + 1, hbm=range(5), grant=56,
     )
     ring = [(i, (i + 1) % n_lon) for i in range(n_lon)]
     left = lax.ppermute(to_east, "lon", ring)
     right = lax.ppermute(to_west, "lon", [(j, i) for i, j in ring])
     got = exchange(gather)
     edge = (3 * BLK * HY + rows8, LANES)
-    to_south, to_north = call(edge_kernel, [edges, inverse, left, right], [edge, edge], grant=4)
+    to_south, to_north, solver = call(
+        edge_kernel, [edges, to_west, left, right], [edge, edge, (3 * rows8, LANES)], hbm=range(2),
+        scratch=[edges.shape, pack], sems=2, grant=4,
+    )
     line = [(i, i + 1) for i in range(n_lat - 1)]
     below = lax.ppermute(to_north, "lat", line)
     above = lax.ppermute(to_south, "lat", [(j, i) for i, j in line])
-    solver = (inverse, left, right, below, above)
-
-    send, east, north, weight, search, applied = call(
-        search_kernel, [tile, got, *solver, *fields, geo, shift], [row] + [full] * 5, hbm_outs=range(1, 6),
-        scratch=[full] * 12, sems=5, scalars=1, flops=40000000, grant=59,
+
+    send, wet, applied, carry = call(
+        functools.partial(search_kernel, total_rows), [got, solver, left, right, below, above, fields],
+        [row] + [full] * 2 + [(7, *full)], hbm=(6,), hbm_outs=(3,),
+        scratch=[(3, *half)] + [full] * 10 + [full[1:]], sems=9 + AGG_LAT, flops=40000000, grant=50.5,
     )
     got = exchange(send)
     (smoothed,) = call(
-        second_kernel, [applied, east, north, weight, shift], [full], hbm=range(4),
-        scratch=[full] * 9, sems=4 * len(CHUNKS), flops=20000000, grant=60,
+        functools.partial(second_kernel, total_rows), [applied, wet], [full],
+        scratch=[full] * 7 + [full[1:]], flops=20000000, grant=12,
     )
     send, known, *state = call(
-        sums_kernel,
-        [got, *solver, smoothed, shift, east, north, weight, search, applied, fields[1]],
-        [row, (8, LANES)] + [half] * 5, hbm=range(8, 14),
-        scratch=[full] * 5 + [half, full], sems=6 * len(CHUNKS), flops=8000000, grant=58,
+        functools.partial(sums_kernel, total_rows), [got, smoothed, carry],
+        [row, (8, LANES)] + [half] * 5, hbm=(2,),
+        scratch=[(5 * rows8, LANES), full, full, full, full, half, full], sems=6 * len(CHUNKS) + 3, flops=8000000, grant=49,
     )
     got = exchange(send)
     field, out = call(

time: 105 us -> 92.8 us (0.88)
  local copies, waits for them, and re-layouts: 8.99 us -> 1.79 us
  Pallas kernels: 26.1 us -> 20.7 us
  blocking collectives: 19.9 us -> 18.2 us
  starting transfers between devices: 35.4 us -> 36.8 us
    pallas_call x6, Pallas kernels: 26.1 us -> 20.7 us  [call(): pl.pallas_call(kernel, out_shape=[jax.ShapeDtypeStruct(s, F32) for s in o...]
    unnamed x28 -> x4, local copies, waits for them, and re-layouts: 7.13 us -> 1.79 us
    broadcast_in_dim x2 -> x0, local copies, waits for them, and re-layouts: 1.85 us -> none  [the longest x1 1.02 us: body(): geo = jnp.broadcast_to(geo[:, :, None], (2, ROWS, LANES))]
    all_to_all x1, blocking collectives: 19.9 us -> 18.2 us  [exchange(): return lax.all_to_all(x, AXES, 0, 0, tiled=True)]
    all_to_all x2, starting transfers between devices: 21.2 us -> 22.6 us  [exchange(): return lax.all_to_all(x, AXES, 0, 0, tiled=True)]
  transfers between devices with their start and end apart: 6 -> 6, of which waited for: 2 -> 2; matrix products, arithmetic and copies ran while one was open for 0% -> 0% of each run, Pallas kernels for 6% -> 5%
where the time goes in v4:
time: 92.8 us; the launch traced here: 92.5 us
  starting transfers between devices  36.8 us (40%)
  Pallas kernels  20.7 us (22%)
  blocking collectives  18.2 us (20%)
  waiting for transfers between devices  14.1 us (15%)
  local copies, waits for them, and re-layouts  1.79 us (2%)
    all_to_all x2, starting transfers between devices, exchange(): return lax.all_to_all(x, AXES, 0, 0, tiled=True)  22.6 us
    pallas_call x6, Pallas kernels, call(): pl.pallas_call(kernel, out_shape=[jax.ShapeDtypeStruct(s, F32) for s in o...  20.7 us
    all_to_all x1, blocking collectives, exchange(): return lax.all_to_all(x, AXES, 0, 0, tiled=True)  18.2 us
    all_to_all x2, waiting for transfers between devices, exchange(): return lax.all_to_all(x, AXES, 0, 0, tiled=True)  14.1 us
    ppermute x1, starting transfers between devices, body(): right = lax.ppermute(to_west, 'lon', [(j, i) for i, j in ring])  6.22 us
    ppermute x1, starting transfers between devices, body(): below = lax.ppermute(to_north, 'lat', line)  3.54 us
    ppermute x1, starting transfers between devices, body(): left = lax.ppermute(to_east, 'lon', ring)  2.54 us
    ppermute x1, starting transfers between devices, body(): above = lax.ppermute(to_south, 'lat', [(j, i) for i, j in line])  1.92 us
  transfers between devices with their start and end apart: 6, of which 2 were waited for; matrix products, arithmetic and copies ran while one was open for 0% of the time, Pallas kernels for 5%

profile of v4, /device:TPU:1, one launch (start us, length us, event | category | flops | bytes accessed | tf_op | source)
XLA Modules:
  0.0 92.5 jit_solution(4878817772260638579)
XLA Ops:
  0.6 3.4 %shard_map.68 = (f32[256,128]{1,0:T(8,128)}, f32[256,128]{1,0:T(8,128)}, f32[256,128]{1,0:T(8,128)}, f32[2,3,2,16,128]{4,3,2,1,0:T(8,128)}, f32[3,2,512,128]{3,2,1,0:T(8,128)}) custom-call(f32[512,256]{1,0:T(8,128)} %rhs_hbm.1, f32[512,256]{1,0:T(8,128)} %depth_hbm.1, s32[512,256]{1,0:T(8,128)} %mask_hbm.1, f32[512,256]{1,0:T(8,128)} %basis_hbm.1, ...), custom_call_target="tpu_custom_call" | custom-call | bytes 4194304 | tf_op jit(solution)/shard_map/pallas_call | solution.py:607
  4.1 2.5 %collective-permute-start = (f32[256,128]{1,0:T(8,128)}, f32[256,128]{1,0:T(8,128)S(1)}, u32[]{:S(2)}, u32[]{:S(2)}) collective-permute-start(f32[256,128]{1,0:T(8,128)} %get-tuple-element.24), channel_id=1, source_target_pairs={{0,8},{8,16},{16,24},{24,32},{32,40},{40,48},{48,56},{56,64},{64,7... | collective-permute-start | bytes 393224 | tf_op jit(solution)/shard_map/ppermute | solution.py:639
  6.6 6.2 %collective-permute-start.1 = (f32[256,128]{1,0:T(8,128)}, f32[256,128]{1,0:T(8,128)S(1)}, u32[]{:S(2)}, u32[]{:S(2)}) collective-permute-start(f32[256,128]{1,0:T(8,128)} %get-tuple-element.23.pack_hbm), channel_id=1, source_target_pairs={{8,0},{16,8},{24,16},{32,24},{40,32},{48,40},{56,48},{64,56},{72,6... | collective-permute-start | bytes 393224 | tf_op jit(solution)/shard_map/ppermute | solution.py:640
  12.8 10.2 %all-to-all-start = ((f32[256,1,128]{2,1,0:T(1,128)}), f32[256,1,128]{2,1,0:T(1,128)S(1)}, u32[]{:S(2)}, u32[]{:S(2)}) async-start(f32[256,1,128]{2,1,0:T(1,128)} %bitcast.16), calls=%async_computation | async-start | bytes 262144 | tf_op jit(solution)/shard_map/all_to_all | solution.py:620
  23.1 0.0 collective-permute-done.left_ref
  23.1 0.0 collective-permute-done.1.right_ref
  23.1 0.0 copy-start
  23.1 0.9 copy-done
  24.0 0.0 copy-start.1
  24.0 0.9 copy-done.1
  24.9 0.4 shard_map.69
  25.3 3.5 %collective-permute-start.2 = (f32[272,128]{1,0:T(8,128)S(1)}, f32[272,128]{1,0:T(8,128)S(1)}, u32[]{:S(2)}, u32[]{:S(2)}) collective-permute-start(f32[272,128]{1,0:T(8,128)S(1)} %get-tuple-element.26), channel_id=1, source_target_pairs={{0,1},{1,2},{2,3},{3,4},{4,5},{5,6},{6,7},{8,9},{9,10},{10,11},{11... | collective-permute-start | bytes 417800 | tf_op jit(solution)/shard_map/ppermute | solution.py:648
  28.8 1.9 %collective-permute-start.3 = (f32[272,128]{1,0:T(8,128)S(1)}, f32[272,128]{1,0:T(8,128)S(1)}, u32[]{:S(2)}, u32[]{:S(2)}) collective-permute-start(f32[272,128]{1,0:T(8,128)S(1)} %get-tuple-element.27), channel_id=1, source_target_pairs={{1,0},{2,1},{3,2},{4,3},{5,4},{6,5},{7,6},{9,8},{10,9},{11,10},{12... | collective-permute-start | bytes 417800 | tf_op jit(solution)/shard_map/ppermute | solution.py:649
  30.8 5.1 %all-to-all-done = f32[256,1,128]{2,1,0:T(1,128)S(1)} async-done(((f32[256,1,128]{2,1,0:T(1,128)}), f32[256,1,128]{2,1,0:T(1,128)S(1)}, u32[]{:S(2)}, u32[]{:S(2)}) %all-to-all-start) | async-done | bytes 131104 | tf_op jit(solution)/shard_map/all_to_all | solution.py:620
  35.8 0.0 collective-permute-done.2.below_ref
  35.8 0.0 collective-permute-done.3.above_ref
  35.8 9.0 %shard_map.70 = (f32[256,128]{1,0:T(8,128)}, f32[3,544,128]{2,1,0:T(8,128)S(1)}, f32[3,544,128]{2,1,0:T(8,128)S(1)}, f32[7,3,544,128]{3,2,1,0:T(8,128)}) custom-call(f32[256,128]{1,0:T(8,128)S(1)} %bitcast.12, f32[384,128]{1,0:T(8,128)S(1)} %get-tuple-element.25.solver_ref, f32[256,128]{1,0:T(8,128)S(1)} %collective-permute-done.left_ref, ...), custom_call_target="tpu_custom_call" | custom-call | flops 40000000 | bytes 4194304 | tf_op jit(solution)/shard_map/pallas_call | solution.py:607
  44.8 12.4 %all-to-all-start.1 = ((f32[256,1,128]{2,1,0:T(1,128)}), f32[256,1,128]{2,1,0:T(1,128)S(1)}, u32[]{:S(2)}, u32[]{:S(2)}) async-start(f32[256,1,128]{2,1,0:T(1,128)} %bitcast.4), calls=%async_computation.1 | async-start | bytes 262144 | tf_op jit(solution)/shard_map/all_to_all | solution.py:620
  57.2 3.8 %shard_map.71.smooth_ref = f32[3,544,128]{2,1,0:T(8,128)S(1)} custom-call(f32[3,544,128]{2,1,0:T(8,128)S(1)} %get-tuple-element.30.applied_ref, f32[3,544,128]{2,1,0:T(8,128)S(1)} %get-tuple-element.31.wet_ref), custom_call_target="tpu_custom_call" | custom-call | flops 20000000 | bytes 4194304 | tf_op jit(solution)/shard_map/pallas_call | solution.py:607
  61.0 9.0 %all-to-all-done.1 = f32[256,1,128]{2,1,0:T(1,128)S(1)} async-done(((f32[256,1,128]{2,1,0:T(1,128)}), f32[256,1,128]{2,1,0:T(1,128)S(1)}, u32[]{:S(2)}, u32[]{:S(2)}) %all-to-all-start.1) | async-done | bytes 131104 | tf_op jit(solution)/shard_map/all_to_all | solution.py:620
  70.0 3.0 %shard_map.72 = (f32[256,128]{1,0:T(8,128)S(1)}, f32[8,128]{1,0:T(8,128)S(1)}, f32[2,512,128]{2,1,0:T(8,128)S(1)}, f32[2,512,128]{2,1,0:T(8,128)S(1)}, f32[2,512...) custom-call(f32[256,128]{1,0:T(8,128)S(1)} %bitcast.14, ...), custom_call_target="tpu_custom_call" | custom-call | flops 8000000 | bytes 4194304 | tf_op jit(solution)/shard_map/pallas_call | solution.py:607
  73.0 18.2 %all_to_all.33 = f32[256,1,128]{2,1,0:T(1,128)S(1)} all-to-all(f32[256,1,128]{2,1,0:T(1,128)S(1)} %bitcast.15), channel_id=1, replica_groups=mesh['lon'=32,'lat'=8] {'lon','lat'}, dimensions={0} | all-to-all | bytes 262144 | tf_op jit(solution)/shard_map/all_to_all | solution.py:620
  91.2 1.2 %shard_map.73 = (f32[512,256]{1,0:T(8,128)}, f32[512,256]{1,0:T(8,128)}) custom-call(f32[256,128]{1,0:T(8,128)S(1)} %bitcast.13, f32[8,128]{1,0:T(8,128)S(1)} %get-tuple-element.34.known_ref, f32[2,512,128]{2,1,0:T(8,128)S(1)} %get-tuple-element.35.search_ref, f32[2,512,128]{2,1,0:T(8,128)S(1)} %get-tuple-element.36.applied_ref, ...), custom_call_target="tpu_custom_call" | custom-call | flops 1000000 | bytes 4194304 | tf_op jit(solution)/shard_map/pallas_call | solution.py:607
Async XLA Ops:
  4.1 19.0 %collective-permute-start = (f32[256,128]{1,0:T(8,128)}, f32[256,128]{1,0:T(8,128)S(1)}, u32[]{:S(2)}, u32[]{:S(2)}) collective-permute-start(f32[256,128]{1,0:T(8,128)} %get-tuple-element.24), channel_id=1, source_target_pairs={{0,8},{8,16},{16,24},{24,32},{32,40},{40,48},{48,56},{56,64},{64,7... | collective-permute-start | bytes 393224 | tf_op jit(solution)/shard_map/ppermute | solution.py:639
  6.6 16.4 %collective-permute-start.1 = (f32[256,128]{1,0:T(8,128)}, f32[256,128]{1,0:T(8,128)S(1)}, u32[]{:S(2)}, u32[]{:S(2)}) collective-permute-start(f32[256,128]{1,0:T(8,128)} %get-tuple-element.23.pack_hbm), channel_id=1, source_target_pairs={{8,0},{16,8},{24,16},{32,24},{40,32},{48,40},{56,48},{64,56},{72,6... | collective-permute-start | bytes 393224 | tf_op jit(solution)/shard_map/ppermute | solution.py:640
  12.8 23.0 %all-to-all-start = ((f32[256,1,128]{2,1,0:T(1,128)}), f32[256,1,128]{2,1,0:T(1,128)S(1)}, u32[]{:S(2)}, u32[]{:S(2)}) async-start(f32[256,1,128]{2,1,0:T(1,128)} %bitcast.16), calls=%async_computation | async-start | bytes 262144 | tf_op jit(solution)/shard_map/all_to_all | solution.py:620
  23.1 0.9 copy-start
  24.0 0.9 copy-start.1
  25.3 10.6 %collective-permute-start.2 = (f32[272,128]{1,0:T(8,128)S(1)}, f32[272,128]{1,0:T(8,128)S(1)}, u32[]{:S(2)}, u32[]{:S(2)}) collective-permute-start(f32[272,128]{1,0:T(8,128)S(1)} %get-tuple-element.26), channel_id=1, source_target_pairs={{0,1},{1,2},{2,3},{3,4},{4,5},{5,6},{6,7},{8,9},{9,10},{10,11},{11... | collective-permute-start | bytes 417800 | tf_op jit(solution)/shard_map/ppermute | solution.py:648
  28.8 7.0 %collective-permute-start.3 = (f32[272,128]{1,0:T(8,128)S(1)}, f32[272,128]{1,0:T(8,128)S(1)}, u32[]{:S(2)}, u32[]{:S(2)}) collective-permute-start(f32[272,128]{1,0:T(8,128)S(1)} %get-tuple-element.27), channel_id=1, source_target_pairs={{1,0},{2,1},{3,2},{4,3},{5,4},{6,5},{7,6},{9,8},{10,9},{11,10},{12... | collective-permute-start | bytes 417800 | tf_op jit(solution)/shard_map/ppermute | solution.py:649
  44.8 25.2 %all-to-all-start.1 = ((f32[256,1,128]{2,1,0:T(1,128)}), f32[256,1,128]{2,1,0:T(1,128)S(1)}, u32[]{:S(2)}, u32[]{:S(2)}) async-start(f32[256,1,128]{2,1,0:T(1,128)} %bitcast.4), calls=%async_computation.1 | async-start | bytes 262144 | tf_op jit(solution)/shard_map/all_to_all | solution.py:620

commit v5 on v4

--- a/solution.py
+++ b/solution.py
@@ -158,8 +158,8 @@
 
 def pack_kernel(
     rhs_hbm, depth_hbm, mask_hbm, basis_hbm, inverse_hbm,
-    gather_ref, west_ref, east_ref, edge_ref, fields_out,
-    rhs_ref, depth_ref, mask_ref, basis_ref, inverse_ref, fields_ref, sems,
+    gather_ref, west_ref, east_ref, fields_out,
+    rhs_ref, depth_ref, mask_ref, basis_ref, inverse_ref, edge_ref, fields_ref, sems,
 ):
     spot = place()
     pairs = ((rhs_hbm, rhs_ref), (mask_hbm, mask_ref), (basis_hbm, basis_ref), (depth_hbm, depth_ref))
@@ -195,7 +195,8 @@
                     fields_ref[f, b, start : start + STEP, :] = value
                     for side, first in ((0, 0), (1, NY - HY)):
                         if start == first:
-                            edge_ref[side, f, b] = value
+                            at = ((side * 3 + f) * 2 + b) * HY
+                            edge_ref[at : at + HY, :] = value
             for ref, b, extra in ((west_ref, 0, 0), (east_ref, 1, WX)):
                 packed = jnp.zeros((STEP, LANES), F32) if g == 0 else ref[out_row : out_row + STEP, :]
                 for f in range(3):
@@ -205,13 +206,15 @@
                 ref[out_row : out_row + STEP, :] = packed
         sums += [total(acc) for acc in accs]
         rows = (slice(None), slice(None), pl.ds(g * BAND, BAND))
-        outs.append(send_out(fields_ref.at[rows], fields_out.at[rows], sems.at[4 * AGG_LAT + 1 + g]))
+        outs.append(send_out(fields_ref.at[rows], fields_out.at[0:3].at[rows], sems.at[4 * AGG_LAT + 1 + g]))
     fill_rows(gather_ref, own_row(spot, sums))
     last.wait()
     for g in range(groups):
         part = inverse_ref[:, g * LANES : (g + 1) * LANES]
         west_ref[BAND + 8 * g : BAND + 8 * g + 8, :] = part
         east_ref[BAND + 8 * g : BAND + 8 * g + 8, :] = part
+    outs.append(send_out(edge_ref, fields_out.at[3, 0, 0 : edge_ref.shape[0]], sems.at[5 * AGG_LAT + 1]))
+    outs.append(send_out(west_ref.at[BAND:], fields_out.at[3, 1, 0 : 8 * groups], sems.at[5 * AGG_LAT + 2]))
     for copy in outs:
         copy.wait()
 
@@ -228,24 +231,28 @@
     return out
 
 
-def edge_kernel(edge_hbm, pack_hbm, left_ref, right_ref, south_ref, north_ref, solver_ref, edge_ref, pack_ref, sems):
-    for copy in fetch(((edge_hbm, edge_ref), (pack_hbm, pack_ref)), sems, 0):
+def edge_kernel(fields_hbm, left_ref, right_ref, south_ref, north_ref, solver_ref, edge_ref, own_ref, sems):
+    rows8 = own_ref.shape[0]
+    groups = rows8 // 8
+    pairs = ((fields_hbm.at[3, 0, 0 : edge_ref.shape[0]], edge_ref), (fields_hbm.at[3, 1, 0:rows8], own_ref))
+    copies = fetch(pairs, sems, 0)
+    for k, ref in ((1, left_ref), (2, right_ref)):
+        solver_ref[k * rows8 : (k + 1) * rows8, :] = ref[BAND:, :]
+    for copy in copies:
         copy.wait()
-    rows8 = pack_ref.shape[0] - BAND
-    for k, ref in enumerate((pack_ref, left_ref, right_ref)):
-        solver_ref[k * rows8 : (k + 1) * rows8, :] = ref[BAND:, :]
-    groups = (pack_ref.shape[0] - BAND) // 8
+    solver_ref[0:rows8, :] = own_ref[...]
     sub = lax.broadcasted_iota(jnp.int32, (8, LANES), 0)
     for side, (ref, start, band) in enumerate(((south_ref, 0, 0), (north_ref, BAND - HY, AGG_LAT - 1))):
         halo = unpack_columns(left_ref, right_ref, band, start, HY)
         for f in range(3):
             for b in range(BLK):
                 at = (f * BLK + b) * HY
-                ref[at : at + HY, :] = edge_ref[side, f, b] if b < 2 else halo[f]
+                row = ((side * 3 + f) * 2 + b) * HY
+                ref[at : at + HY, :] = edge_ref[row : row + HY, :] if b < 2 else halo[f]
         base = 3 * BLK * HY
         for i in range(groups):
             at = slice(BAND + 8 * i, BAND + 8 * i + 8)
-            own, left, right = pack_ref[at, :], left_ref[at, :], right_ref[at, :]
+            own, left, right = own_ref[8 * i : 8 * i + 8, :], left_ref[at, :], right_ref[at, :]
             own = pltpu.roll(own, (8 - 2 * band) % 8, 0) if band else own
             left = pltpu.roll(left, (2 - 2 * band - 1 + 16) % 8, 0)
             right = pltpu.roll(right, (3 - 2 * band + 16) % 8, 0)
@@ -389,7 +396,7 @@
     spot = place()
     fields = (wet_ref, res_ref, weight_ref)
     bands = [(slice(None), slice(None), pl.ds(a * BAND, BAND)) for a in range(AGG_LAT)]
-    copies = [send_out(fields_hbm.at[at], fields_ref.at[at], sems.at[5 + a]) for a, at in enumerate(bands)]
+    copies = [send_out(fields_hbm.at[0:3].at[at], fields_ref.at[at], sems.at[5 + a]) for a, at in enumerate(bands)]
     for f, ref in enumerate(fields):
         for b in range(BLK):
             at = (f * BLK + b) * HY
@@ -410,13 +417,13 @@
     own_rows = (slice(0, AGG_LON), slice(HY, HY + NY))
     outs = [
         send_out(weight_ref, carry_out.at[0], sems.at[0]),
-        send_out(res_ref.at[own_rows], carry_out.at[5].at[own_rows], sems.at[3]),
+        send_out(res_ref.at[own_rows], carry_out.at[4].at[own_rows], sems.at[3]),
     ]
     base, rows8 = 3 * BLK * HY, solver_ref.shape[0] // 3
     outs += [
-        send_out(solver_ref, carry_out.at[6, 0, 0 : 3 * rows8], sems.at[10]),
-        send_out(below_ref.at[base : base + rows8], carry_out.at[6, 1, 0:rows8], sems.at[11]),
-        send_out(above_ref.at[base : base + rows8], carry_out.at[6, 2, 0:rows8], sems.at[12]),
+        send_out(solver_ref, carry_out.at[5, 0, 0 : 3 * rows8], sems.at[10]),
+        send_out(below_ref.at[base : base + rows8], carry_out.at[5, 1, 0:rows8], sems.at[11]),
+        send_out(above_ref.at[base : base + rows8], carry_out.at[5, 2, 0:rows8], sems.at[12]),
     ]
 
     north_faces(spot, total_rows, wet_ref, north_ref, 0, 8)
@@ -455,7 +462,6 @@
                 sums[-1] = sums[-1] + fold(here[b] * res_ref[at])
 
     for_bands(apply)
-    outs.append(send_out(applied_ref.at[own_rows], carry_out.at[4].at[own_rows], sems.at[2]))
     values = [total(x) for x in sums]
     fill_rows(send_ref, own_row(spot, values[:-2], values[-2:]))
     for copy in outs:
@@ -488,17 +494,17 @@
 
 def sums_kernel(
     total_rows,
-    got_ref, smooth_ref, carry_hbm,
-    send_ref, known_ref, search_out, applied_ref, update_ref, operated_ref, rest_ref,
+    got_ref, smooth_ref, applied_ref, carry_hbm,
+    send_ref, known_ref, search_out, applied_out, update_ref, operated_ref, rest_ref,
     solver_ref, weight_ref, search_ref, east_ref, north_ref, res_ref, full_ref, sems,
 ):
     spot = place()
     rows8 = solver_ref.shape[0] // 5
-    pairs = [(carry_hbm.at[6, 0, 0 : 3 * rows8], solver_ref.at[0 : 3 * rows8])]
+    pairs = [(carry_hbm.at[5, 0, 0 : 3 * rows8], solver_ref.at[0 : 3 * rows8])]
     for k in (1, 2):
-        pairs.append((carry_hbm.at[6, k, 0:rows8], solver_ref.at[(k + 2) * rows8 : (k + 3) * rows8]))
-    solver = fetch(pairs, sems, 6 * len(CHUNKS))
-    stream = Stream(carry_hbm, (weight_ref, search_ref, east_ref, north_ref, applied_ref, res_ref), sems)
+        pairs.append((carry_hbm.at[5, k, 0:rows8], solver_ref.at[(k + 2) * rows8 : (k + 3) * rows8]))
+    solver = fetch(pairs, sems, 5 * len(CHUNKS))
+    stream = Stream(carry_hbm, (weight_ref, search_ref, east_ref, north_ref, res_ref), sems)
     for copy in solver:
         copy.wait()
     coarse = coarse_solve(got_ref, [(solver_ref, k * rows8) for k in range(5)])
@@ -537,9 +543,10 @@
                 + nf[b] * (here[b] - up[b])
                 + sf[b] * (here[b] - down[b])
             )
-            search, applied = search_ref[b, start : start + STEP, :], applied_ref[b, at, :]
+            search, applied = search_ref[b, start : start + STEP, :], applied_ref[b, start : start + STEP, :]
             rest = res_ref[b, at, :] - alpha * applied
             search_out[b, at, :] = search
+            applied_out[b, at, :] = applied
             update_ref[b, at, :] = here[b]
             operated_ref[b, at, :] = out
             rest_ref[b, at, :] = rest
@@ -631,9 +638,9 @@
 
     loads = [(NY, NX), (NY, NX), pltpu.VMEM((NY, NX), jnp.int32), (NY, NX), inverse.shape]
     pack = (BAND + rows8, LANES)
-    gather, to_west, to_east, edges, fields = call(
-        pack_kernel, [rhs, depth, mask, basis, inverse], [row, pack, pack, (2, 3, 2, HY, LANES), (3, *half)], hbm_outs=(4,),
-        scratch=[*loads, (3, *half)], sems=5 * AGG_LAT + 1, hbm=range(5), grant=56,
+    gather, to_west, to_east, fields = call(
+        pack_kernel, [rhs, depth, mask, basis, inverse], [row, pack, pack, (4, *half)], hbm_outs=(3,),
+        scratch=[*loads, (12 * HY, LANES), (3, *half)], sems=5 * AGG_LAT + 3, hbm=range(5), grant=56,
     )
     ring = [(i, (i + 1) % n_lon) for i in range(n_lon)]
     left = lax.ppermute(to_east, "lon", ring)
@@ -641,8 +648,8 @@
     got = exchange(gather)
     edge = (3 * BLK * HY + rows8, LANES)
     to_south, to_north, solver = call(
-        edge_kernel, [edges, to_west, left, right], [edge, edge, (3 * rows8, LANES)], hbm=range(2),
-        scratch=[edges.shape, pack], sems=2, grant=4,
+        edge_kernel, [fields, left, right], [edge, edge, (3 * rows8, LANES)], hbm=(0,),
+        scratch=[(12 * HY, LANES), (rows8, LANES)], sems=2, grant=52.5,
     )
     line = [(i, i + 1) for i in range(n_lat - 1)]
     below = lax.ppermute(to_north, "lat", line)
@@ -650,7 +657,7 @@
 
     send, wet, applied, carry = call(
         functools.partial(search_kernel, total_rows), [got, solver, left, right, below, above, fields],
-        [row] + [full] * 2 + [(7, *full)], hbm=(6,), hbm_outs=(3,),
+        [row] + [full] * 2 + [(6, *full)], hbm=(6,), hbm_outs=(3,),
         scratch=[(3, *half)] + [full] * 10 + [full[1:]], sems=9 + AGG_LAT, flops=40000000, grant=50.5,
     )
     got = exchange(send)
@@ -659,9 +666,9 @@
         scratch=[full] * 7 + [full[1:]], flops=20000000, grant=12,
     )
     send, known, *state = call(
-        functools.partial(sums_kernel, total_rows), [got, smoothed, carry],
-        [row, (8, LANES)] + [half] * 5, hbm=(2,),
-        scratch=[(5 * rows8, LANES), full, full, full, full, half, full], sems=6 * len(CHUNKS) + 3, flops=8000000, grant=49,
+        functools.partial(sums_kernel, total_rows), [got, smoothed, applied, carry],
+        [row, (8, LANES)] + [half] * 5, hbm=(3,),
+        scratch=[(5 * rows8, LANES), full, full, full, full, half, full], sems=5 * len(CHUNKS) + 3, flops=8000000, grant=48.5,
     )
     got = exchange(send)
     field, out = call(

time: 92.8 us -> 91.3 us (0.984)
  local copies, waits for them, and re-layouts: 1.79 us -> 0 us
  waiting for transfers between devices: 14.1 us -> 15.5 us
  starting transfers between devices: 36.8 us -> 35.7 us
    unnamed x4 -> x0, local copies, waits for them, and re-layouts: 1.79 us -> none
    all_to_all x2, waiting for transfers between devices: 14.1 us -> 15.5 us  [exchange(): return lax.all_to_all(x, AXES, 0, 0, tiled=True)]
    all_to_all x2, starting transfers between devices: 22.6 us -> 21.4 us  [exchange(): return lax.all_to_all(x, AXES, 0, 0, tiled=True)]
where the time goes in v5:
time: 91.3 us; the launch traced here: 91 us
  starting transfers between devices  35.7 us (39%)
  Pallas kernels  20.8 us (23%)
  blocking collectives  18.2 us (20%)
  waiting for transfers between devices  15.5 us (17%)
    all_to_all x2, starting transfers between devices, exchange(): return lax.all_to_all(x, AXES, 0, 0, tiled=True)  21.4 us
    pallas_call x6, Pallas kernels, call(): pl.pallas_call(kernel, out_shape=[jax.ShapeDtypeStruct(s, F32) for s in o...  20.8 us
    all_to_all x1, blocking collectives, exchange(): return lax.all_to_all(x, AXES, 0, 0, tiled=True)  18.2 us
    all_to_all x2, waiting for transfers between devices, exchange(): return lax.all_to_all(x, AXES, 0, 0, tiled=True)  15.5 us
    ppermute x1, starting transfers between devices, body(): right = lax.ppermute(to_west, 'lon', [(j, i) for i, j in ring])  6.22 us
    ppermute x1, starting transfers between devices, body(): below = lax.ppermute(to_north, 'lat', line)  3.54 us
    ppermute x1, starting transfers between devices, body(): left = lax.ppermute(to_east, 'lon', ring)  2.54 us
    ppermute x1, starting transfers between devices, body(): above = lax.ppermute(to_south, 'lat', [(j, i) for i, j in line])  1.92 us
  transfers between devices with their start and end apart: 6, of which 2 were waited for; matrix products, arithmetic and copies ran while one was open for 0% of the time, Pallas kernels for 5%

profile of v5, /device:TPU:1, one launch (start us, length us, event | category | flops | bytes accessed | tf_op | source)
XLA Modules:
  0.0 91.0 jit_solution(12287380470058476491)
XLA Ops:
  0.6 3.5 %shard_map.68 = (f32[256,128]{1,0:T(8,128)}, f32[256,128]{1,0:T(8,128)}, f32[256,128]{1,0:T(8,128)}, f32[4,2,512,128]{3,2,1,0:T(8,128)}) custom-call(f32[512,256]{1,0:T(8,128)} %rhs_hbm.1, f32[512,256]{1,0:T(8,128)} %depth_hbm.1, s32[512,256]{1,0:T(8,128)} %mask_hbm.1, f32[512,256]{1,0:T(8,128)} %basis_hbm.1, f32[8,2048]{1,0:T(8,128)} %inverse_hbm.1), custom_call_target="tpu_custom_call" | custom-call | bytes 4194304 | tf_op jit(solution)/shard_map/pallas_call | solution.py:614
  4.1 2.5 %collective-permute-start = (f32[256,128]{1,0:T(8,128)}, f32[256,128]{1,0:T(8,128)S(1)}, u32[]{:S(2)}, u32[]{:S(2)}) collective-permute-start(f32[256,128]{1,0:T(8,128)} %get-tuple-element.22), channel_id=1, source_target_pairs={{0,8},{8,16},{16,24},{24,32},{32,40},{40,48},{48,56},{56,64},{64,7... | collective-permute-start | bytes 393224 | tf_op jit(solution)/shard_map/ppermute | solution.py:646
  6.7 6.2 %collective-permute-start.1 = (f32[256,128]{1,0:T(8,128)}, f32[256,128]{1,0:T(8,128)S(1)}, u32[]{:S(2)}, u32[]{:S(2)}) collective-permute-start(f32[256,128]{1,0:T(8,128)} %get-tuple-element.23), channel_id=1, source_target_pairs={{8,0},{16,8},{24,16},{32,24},{40,32},{48,40},{56,48},{64,56},{72,6... | collective-permute-start | bytes 393224 | tf_op jit(solution)/shard_map/ppermute | solution.py:647
  12.9 10.2 %all-to-all-start = ((f32[256,1,128]{2,1,0:T(1,128)}), f32[256,1,128]{2,1,0:T(1,128)S(1)}, u32[]{:S(2)}, u32[]{:S(2)}) async-start(f32[256,1,128]{2,1,0:T(1,128)} %bitcast.16), calls=%async_computation | async-start | bytes 262144 | tf_op jit(solution)/shard_map/all_to_all | solution.py:627
  23.1 0.0 collective-permute-done.left_ref
  23.1 0.0 collective-permute-done.1.right_ref
  23.1 1.0 %shard_map.69 = (f32[272,128]{1,0:T(8,128)S(1)}, f32[272,128]{1,0:T(8,128)S(1)}, f32[384,128]{1,0:T(8,128)S(1)}) custom-call(f32[4,2,512,128]{3,2,1,0:T(8,128)} %get-tuple-element.21.fields_hbm, f32[256,128]{1,0:T(8,128)S(1)} %collective-permute-done.left_ref, f32[256,128]{1,0:T(8,128)S(1)} %collective-permute-done.1.right_ref), custom_call_target="tpu_custom_call" | custom-call | bytes 4194304 | tf_op jit(solution)/shard_map/pallas_call | solution.py:614
  24.1 3.5 %collective-permute-start.2 = (f32[272,128]{1,0:T(8,128)S(1)}, f32[272,128]{1,0:T(8,128)S(1)}, u32[]{:S(2)}, u32[]{:S(2)}) collective-permute-start(f32[272,128]{1,0:T(8,128)S(1)} %get-tuple-element.25), channel_id=1, source_target_pairs={{0,1},{1,2},{2,3},{3,4},{4,5},{5,6},{6,7},{8,9},{9,10},{10,11},{11... | collective-permute-start | bytes 417800 | tf_op jit(solution)/shard_map/ppermute | solution.py:655
  27.7 1.9 %collective-permute-start.3 = (f32[272,128]{1,0:T(8,128)S(1)}, f32[272,128]{1,0:T(8,128)S(1)}, u32[]{:S(2)}, u32[]{:S(2)}) collective-permute-start(f32[272,128]{1,0:T(8,128)S(1)} %get-tuple-element.26), channel_id=1, source_target_pairs={{1,0},{2,1},{3,2},{4,3},{5,4},{6,5},{7,6},{9,8},{10,9},{11,10},{12... | collective-permute-start | bytes 417800 | tf_op jit(solution)/shard_map/ppermute | solution.py:656
  29.6 6.3 %all-to-all-done = f32[256,1,128]{2,1,0:T(1,128)S(1)} async-done(((f32[256,1,128]{2,1,0:T(1,128)}), f32[256,1,128]{2,1,0:T(1,128)S(1)}, u32[]{:S(2)}, u32[]{:S(2)}) %all-to-all-start) | async-done | bytes 131104 | tf_op jit(solution)/shard_map/all_to_all | solution.py:627
  35.9 0.0 collective-permute-done.2.below_ref
  35.9 0.0 collective-permute-done.3.above_ref
  35.9 8.7 %shard_map.70 = (f32[256,128]{1,0:T(8,128)}, f32[3,544,128]{2,1,0:T(8,128)S(1)}, f32[3,544,128]{2,1,0:T(8,128)S(1)}, f32[6,3,544,128]{3,2,1,0:T(8,128)}) custom-call(f32[256,128]{1,0:T(8,128)S(1)} %bitcast.12, f32[384,128]{1,0:T(8,128)S(1)} %get-tuple-element.24.solver_ref, f32[256,128]{1,0:T(8,128)S(1)} %collective-permute-done.left_ref, ...), custom_call_target="tpu_custom_call" | custom-call | flops 40000000 | bytes 4194304 | tf_op jit(solution)/shard_map/pallas_call | solution.py:614
  44.6 11.2 %all-to-all-start.1 = ((f32[256,1,128]{2,1,0:T(1,128)}), f32[256,1,128]{2,1,0:T(1,128)S(1)}, u32[]{:S(2)}, u32[]{:S(2)}) async-start(f32[256,1,128]{2,1,0:T(1,128)} %bitcast.4), calls=%async_computation.1 | async-start | bytes 262144 | tf_op jit(solution)/shard_map/all_to_all | solution.py:627
  55.9 3.6 %shard_map.71.smooth_ref = f32[3,544,128]{2,1,0:T(8,128)S(1)} custom-call(f32[3,544,128]{2,1,0:T(8,128)S(1)} %get-tuple-element.28.applied_ref, f32[3,544,128]{2,1,0:T(8,128)S(1)} %get-tuple-element.29.wet_ref), custom_call_target="tpu_custom_call" | custom-call | flops 20000000 | bytes 4194304 | tf_op jit(solution)/shard_map/pallas_call | solution.py:614
  59.5 9.2 %all-to-all-done.1 = f32[256,1,128]{2,1,0:T(1,128)S(1)} async-done(((f32[256,1,128]{2,1,0:T(1,128)}), f32[256,1,128]{2,1,0:T(1,128)S(1)}, u32[]{:S(2)}, u32[]{:S(2)}) %all-to-all-start.1) | async-done | bytes 131104 | tf_op jit(solution)/shard_map/all_to_all | solution.py:627
  68.7 2.8 %shard_map.72 = (f32[256,128]{1,0:T(8,128)S(1)}, f32[8,128]{1,0:T(8,128)S(1)}, f32[2,512,128]{2,1,0:T(8,128)S(1)}, f32[2,512,128]{2,1,0:T(8,128)S(1)}, f32[2,512...) custom-call(f32[256,128]{1,0:T(8,128)S(1)} %bitcast.14, ...), custom_call_target="tpu_custom_call" | custom-call | flops 8000000 | bytes 4194304 | tf_op jit(solution)/shard_map/pallas_call | solution.py:614
  71.5 18.2 %all_to_all.33 = f32[256,1,128]{2,1,0:T(1,128)S(1)} all-to-all(f32[256,1,128]{2,1,0:T(1,128)S(1)} %bitcast.15), channel_id=1, replica_groups=mesh['lon'=32,'lat'=8] {'lon','lat'}, dimensions={0} | all-to-all | bytes 262144 | tf_op jit(solution)/shard_map/all_to_all | solution.py:627
  89.6 1.2 %shard_map.73 = (f32[512,256]{1,0:T(8,128)}, f32[512,256]{1,0:T(8,128)}) custom-call(f32[256,128]{1,0:T(8,128)S(1)} %bitcast.13, f32[8,128]{1,0:T(8,128)S(1)} %get-tuple-element.32.known_ref, f32[2,512,128]{2,1,0:T(8,128)S(1)} %get-tuple-element.33.search_ref, f32[2,512,128]{2,1,0:T(8,128)S(1)} %get-tuple-element.34.applied_ref, ...), custom_call_target="tpu_custom_call" | custom-call | flops 1000000 | bytes 4194304 | tf_op jit(solution)/shard_map/pallas_call | solution.py:614
Async XLA Ops:
  4.1 19.0 %collective-permute-start = (f32[256,128]{1,0:T(8,128)}, f32[256,128]{1,0:T(8,128)S(1)}, u32[]{:S(2)}, u32[]{:S(2)}) collective-permute-start(f32[256,128]{1,0:T(8,128)} %get-tuple-element.22), channel_id=1, source_target_pairs={{0,8},{8,16},{16,24},{24,32},{32,40},{40,48},{48,56},{56,64},{64,7... | collective-permute-start | bytes 393224 | tf_op jit(solution)/shard_map/ppermute | solution.py:646
  6.7 16.4 %collective-permute-start.1 = (f32[256,128]{1,0:T(8,128)}, f32[256,128]{1,0:T(8,128)S(1)}, u32[]{:S(2)}, u32[]{:S(2)}) collective-permute-start(f32[256,128]{1,0:T(8,128)} %get-tuple-element.23), channel_id=1, source_target_pairs={{8,0},{16,8},{24,16},{32,24},{40,32},{48,40},{56,48},{64,56},{72,6... | collective-permute-start | bytes 393224 | tf_op jit(solution)/shard_map/ppermute | solution.py:647
  12.9 23.0 %all-to-all-start = ((f32[256,1,128]{2,1,0:T(1,128)}), f32[256,1,128]{2,1,0:T(1,128)S(1)}, u32[]{:S(2)}, u32[]{:S(2)}) async-start(f32[256,1,128]{2,1,0:T(1,128)} %bitcast.16), calls=%async_computation | async-start | bytes 262144 | tf_op jit(solution)/shard_map/all_to_all | solution.py:627
  24.1 11.7 %collective-permute-start.2 = (f32[272,128]{1,0:T(8,128)S(1)}, f32[272,128]{1,0:T(8,128)S(1)}, u32[]{:S(2)}, u32[]{:S(2)}) collective-permute-start(f32[272,128]{1,0:T(8,128)S(1)} %get-tuple-element.25), channel_id=1, source_target_pairs={{0,1},{1,2},{2,3},{3,4},{4,5},{5,6},{6,7},{8,9},{9,10},{10,11},{11... | collective-permute-start | bytes 417800 | tf_op jit(solution)/shard_map/ppermute | solution.py:655
  27.7 8.2 %collective-permute-start.3 = (f32[272,128]{1,0:T(8,128)S(1)}, f32[272,128]{1,0:T(8,128)S(1)}, u32[]{:S(2)}, u32[]{:S(2)}) collective-permute-start(f32[272,128]{1,0:T(8,128)S(1)} %get-tuple-element.26), channel_id=1, source_target_pairs={{1,0},{2,1},{3,2},{4,3},{5,4},{6,5},{7,6},{9,8},{10,9},{11,10},{12... | collective-permute-start | bytes 417800 | tf_op jit(solution)/shard_map/ppermute | solution.py:656
  44.6 24.0 %all-to-all-start.1 = ((f32[256,1,128]{2,1,0:T(1,128)}), f32[256,1,128]{2,1,0:T(1,128)S(1)}, u32[]{:S(2)}, u32[]{:S(2)}) async-start(f32[256,1,128]{2,1,0:T(1,128)} %bitcast.4), calls=%async_computation.1 | async-start | bytes 262144 | tf_op jit(solution)/shard_map/all_to_all | solution.py:627

commit v6 on v5

--- a/solution.py
+++ b/solution.py
@@ -387,43 +387,58 @@
     return copy
 
 
+def fill_from(fields_hbm, which, refs, bufs, left_ref, right_ref, sems):
+    bands = [(slice(None), pl.ds(a * BAND, BAND)) for a in range(AGG_LAT)]
+    copies = [
+        fetch([(fields_hbm.at[f].at[at], buf.at[at]) for f, buf in zip(which, bufs)], sems, a * len(which))
+        for a, at in enumerate(bands)
+    ]
+
+    def fill(g, start):
+        if start % BAND == 0:
+            for copy in copies[g]:
+                copy.wait()
+        at = slice(HY + start, HY + start + STEP)
+        halo = unpack_columns(left_ref, right_ref, g, start - g * BAND, STEP)
+        for f, ref, buf in zip(which, refs, bufs):
+            for b in range(2):
+                ref[b, at, :] = buf[b, start : start + STEP, :]
+            ref[2, at, :] = halo[f]
+
+    return lambda: for_own(fill)
+
+
+def fill_rows_around(f, ref, below_ref, above_ref):
+    for b in range(BLK):
+        at = (f * BLK + b) * HY
+        ref[b, 0:HY, :] = below_ref[at : at + HY, :]
+        ref[b, HY + NY : ROWS, :] = above_ref[at : at + HY, :]
+
+
+def fill_kernel(left_ref, right_ref, fields_hbm, wet_ref, res_ref, buf_a, buf_b, sems):
+    fill_from(fields_hbm, (0, 1), (wet_ref, res_ref), (buf_a, buf_b), left_ref, right_ref, sems)()
+
+
 def search_kernel(
     total_rows,
-    got_ref, solver_ref, left_ref, right_ref, below_ref, above_ref, fields_hbm,
-    send_ref, wet_ref, applied_ref, carry_out,
-    fields_ref, east_ref, north_ref, res_ref, weight_ref, west_ref, inv_ref, est_a, est_b, step_ref, search_ref, shift_ref, sems,
+    wet_in, res_in, got_ref, solver_ref, left_ref, right_ref, below_ref, above_ref, fields_hbm,
+    wet_ref, res_ref, send_ref, applied_ref, carry_out,
+    buf_ref, search_ref, weight_ref, east_ref, north_ref, west_ref, inv_ref, est_a, est_b, step_ref, shift_ref, sems,
 ):
     spot = place()
-    fields = (wet_ref, res_ref, weight_ref)
-    bands = [(slice(None), slice(None), pl.ds(a * BAND, BAND)) for a in range(AGG_LAT)]
-    copies = [send_out(fields_hbm.at[0:3].at[at], fields_ref.at[at], sems.at[5 + a]) for a, at in enumerate(bands)]
-    for f, ref in enumerate(fields):
-        for b in range(BLK):
-            at = (f * BLK + b) * HY
-            ref[b, 0:HY, :] = below_ref[at : at + HY, :]
-            ref[b, HY + NY : ROWS, :] = above_ref[at : at + HY, :]
-
-    def fill(g, start):
-        if start % BAND == 0:
-            copies[g].wait()
-        at = slice(HY + start, HY + start + STEP)
-        halo = unpack_columns(left_ref, right_ref, g, start - g * BAND, STEP)
-        for f, ref in enumerate(fields):
-            for b in range(2):
-                ref[b, at, :] = fields_ref[f, b, start : start + STEP, :]
-            ref[2, at, :] = halo[f]
-
-    for_own(fill)
+    fill_weight = fill_from(fields_hbm, (2,), (weight_ref,), (buf_ref,), left_ref, right_ref, sems.at[8:12])
+    for f, ref in enumerate((wet_ref, res_ref, weight_ref)):
+        fill_rows_around(f, ref, below_ref, above_ref)
     own_rows = (slice(0, AGG_LON), slice(HY, HY + NY))
     outs = [
-        send_out(weight_ref, carry_out.at[0], sems.at[0]),
-        send_out(res_ref.at[own_rows], carry_out.at[4].at[own_rows], sems.at[3]),
+        send_out(wet_ref, carry_out.at[5], sems.at[7]),
+        send_out(res_ref.at[own_rows], carry_out.at[3].at[own_rows], sems.at[3]),
     ]
     base, rows8 = 3 * BLK * HY, solver_ref.shape[0] // 3
     outs += [
-        send_out(solver_ref, carry_out.at[5, 0, 0 : 3 * rows8], sems.at[10]),
-        send_out(below_ref.at[base : base + rows8], carry_out.at[5, 1, 0:rows8], sems.at[11]),
-        send_out(above_ref.at[base : base + rows8], carry_out.at[5, 2, 0:rows8], sems.at[12]),
+        send_out(solver_ref, carry_out.at[6, 0, 0 : 3 * rows8], sems.at[1]),
+        send_out(below_ref.at[base : base + rows8], carry_out.at[6, 1, 0:rows8], sems.at[2]),
+        send_out(above_ref.at[base : base + rows8], carry_out.at[6, 2, 0:rows8], sems.at[5]),
     ]
 
     north_faces(spot, total_rows, wet_ref, north_ref, 0, 8)
@@ -438,7 +453,9 @@
         first_step(res_ref, inv_ref, faces, est_a, step_ref, start, rows)
 
     for_strips(prepare)
-    outs += [send_out(east_ref, carry_out.at[2], sems.at[4]), send_out(north_ref, carry_out.at[3], sems.at[9])]
+    outs += [send_out(east_ref, carry_out.at[1], sems.at[4]), send_out(north_ref, carry_out.at[2], sems.at[6])]
+    fill_weight()
+    outs.append(send_out(weight_ref, carry_out.at[0], sems.at[0]))
     parts = [(solver_ref, k * rows8) for k in range(3)] + [(below_ref, base), (above_ref, base)]
     coarse = coarse_solve(got_ref, parts)
 
@@ -448,7 +465,7 @@
         store(search_ref, start, rows, [part[b] + weight[b] * coarse[band][b] for b in range(BLK)])
 
     smooth(res_ref, inv_ref, faces, (est_a, est_b), step_ref, finish)
-    outs.append(send_out(search_ref, carry_out.at[1], sems.at[1]))
+    outs.append(send_out(search_ref, carry_out.at[4], sems.at[12]))
     sums = [jnp.zeros((8, LANES), F32)] * (AGG_LAT * AGG_LON + 2)
 
     def apply(start, rows, band):
@@ -470,17 +487,20 @@
 
 def second_kernel(
     total_rows,
-    applied_ref, wet_ref,
+    applied_ref, carry_hbm,
     out_ref,
-    east_ref, north_ref, west_ref, inv_ref, est_a, est_b, step_ref, shift_ref,
+    wet_ref, east_ref, north_ref, west_ref, inv_ref, est_a, est_b, step_ref, shift_ref, sems,
 ):
     spot = place()
+    stream = Stream(carry_hbm.at[5:6], (wet_ref,), sems)
+    stream.need(HY)
     north_faces(spot, total_rows, wet_ref, north_ref, 0, 8)
     for ref in (est_a, est_b):
         clear_ends(ref)
     faces = (east_ref, west_ref, north_ref, shift_ref)
 
     def prepare(start, rows):
+        stream.need(start + rows + 1)
         all_faces(spot, total_rows, wet_ref, faces, start, rows)
         first_step(applied_ref, inv_ref, faces, est_a, step_ref, start, rows)
 
@@ -496,15 +516,15 @@
     total_rows,
     got_ref, smooth_ref, applied_ref, carry_hbm,
     send_ref, known_ref, search_out, applied_out, update_ref, operated_ref, rest_ref,
-    solver_ref, weight_ref, search_ref, east_ref, north_ref, res_ref, full_ref, sems,
+    solver_ref, weight_ref, east_ref, north_ref, res_ref, search_ref, full_ref, sems,
 ):
     spot = place()
     rows8 = solver_ref.shape[0] // 5
-    pairs = [(carry_hbm.at[5, 0, 0 : 3 * rows8], solver_ref.at[0 : 3 * rows8])]
+    pairs = [(carry_hbm.at[6, 0, 0 : 3 * rows8], solver_ref.at[0 : 3 * rows8])]
     for k in (1, 2):
-        pairs.append((carry_hbm.at[5, k, 0:rows8], solver_ref.at[(k + 2) * rows8 : (k + 3) * rows8]))
+        pairs.append((carry_hbm.at[6, k, 0:rows8], solver_ref.at[(k + 2) * rows8 : (k + 3) * rows8]))
     solver = fetch(pairs, sems, 5 * len(CHUNKS))
-    stream = Stream(carry_hbm, (weight_ref, search_ref, east_ref, north_ref, res_ref), sems)
+    stream = Stream(carry_hbm, (weight_ref, east_ref, north_ref, res_ref, search_ref), sems)
     for copy in solver:
         copy.wait()
     coarse = coarse_solve(got_ref, [(solver_ref, k * rows8) for k in range(5)])
@@ -607,7 +627,7 @@
         copy.wait()
 
 
-def call(kernel, args, outs, scratch=(), hbm_outs=(), sems=0, flops=0, grant=6, hbm=()):
+def call(kernel, args, outs, scratch=(), hbm_outs=(), sems=0, flops=0, grant=6, hbm=(), aliases=None):
     def spec(i, inside):
         return pl.BlockSpec(memory_space=pl.ANY if i in (hbm if inside else hbm_outs) else pltpu.VMEM)
 
@@ -618,6 +638,7 @@
         out_specs=[spec(i, False) for i in range(len(outs))],
         scratch_shapes=[pltpu.VMEM(s, F32) if isinstance(s, tuple) else s for s in scratch]
         + ([pltpu.SemaphoreType.DMA((sems,))] if sems else []),
+        input_output_aliases=aliases or {},
         compiler_params=pltpu.CompilerParams(vmem_limit_bytes=int(grant * 1024 * 1024)),
         cost_estimate=pl.CostEstimate(flops=flops, bytes_accessed=4 * 1024 * 1024, transcendentals=0),
     )(*args)
@@ -655,20 +676,24 @@
     below = lax.ppermute(to_north, "lat", line)
     above = lax.ppermute(to_south, "lat", [(j, i) for i, j in line])
 
-    send, wet, applied, carry = call(
-        functools.partial(search_kernel, total_rows), [got, solver, left, right, below, above, fields],
-        [row] + [full] * 2 + [(6, *full)], hbm=(6,), hbm_outs=(3,),
-        scratch=[(3, *half)] + [full] * 10 + [full[1:]], sems=9 + AGG_LAT, flops=40000000, grant=50.5,
+    ext = call(
+        fill_kernel, [left, right, fields], [full] * 2, hbm=(2,), scratch=[half, half], sems=2 * AGG_LAT,
+        flops=20000000, grant=50.5,
+    )
+    _, _, send, applied, carry = call(
+        functools.partial(search_kernel, total_rows), [*ext, got, solver, left, right, below, above, fields],
+        [full] * 2 + [row, full, (7, *full)], hbm=(8,), hbm_outs=(4,), aliases={0: 0, 1: 1},
+        scratch=[half] + [full] * 9 + [full[1:]], sems=13, flops=40000000, grant=49.5,
     )
     got = exchange(send)
     (smoothed,) = call(
-        functools.partial(second_kernel, total_rows), [applied, wet], [full],
-        scratch=[full] * 7 + [full[1:]], flops=20000000, grant=12,
+        functools.partial(second_kernel, total_rows), [applied, carry], [full], hbm=(1,),
+        scratch=[full] * 8 + [full[1:]], sems=len(CHUNKS), flops=20000000, grant=50,
     )
     send, known, *state = call(
         functools.partial(sums_kernel, total_rows), [got, smoothed, applied, carry],
         [row, (8, LANES)] + [half] * 5, hbm=(3,),
-        scratch=[(5 * rows8, LANES), full, full, full, full, half, full], sems=5 * len(CHUNKS) + 3, flops=8000000, grant=48.5,
+        scratch=[(5 * rows8, LANES), full, full, full, half, full, full], sems=5 * len(CHUNKS) + 3, flops=8000000, grant=48.5,
     )
     got = exchange(send)
     field, out = call(

time: 91.3 us -> 89.1 us (0.976)
  waiting for transfers between devices: 15.5 us -> 13.4 us
    all_to_all x2, waiting for transfers between devices: 15.5 us -> 13.4 us  [exchange(): return lax.all_to_all(x, AXES, 0, 0, tiled=True)]
    pallas_call x6 -> x7, Pallas kernels: 20.8 us -> 20.6 us  [call(): pl.pallas_call(kernel, out_shape=[jax.ShapeDtypeStruct(s, F32) for s in o...]
  transfers between devices with their start and end apart: 6 -> 6, of which waited for: 2 -> 2; matrix products, arithmetic and copies ran while one was open for 0% -> 0% of each run, Pallas kernels for 5% -> 7%
where the time goes in v6:
time: 89.1 us; the launch traced here: 88.8 us
  starting transfers between devices  35.7 us (40%)
  Pallas kernels  20.6 us (23%)
  blocking collectives  18.2 us (20%)
  waiting for transfers between devices  13.4 us (15%)
    all_to_all x2, starting transfers between devices, exchange(): return lax.all_to_all(x, AXES, 0, 0, tiled=True)  21.4 us
    pallas_call x7, Pallas kernels, call(): pl.pallas_call(kernel, out_shape=[jax.ShapeDtypeStruct(s, F32) for s in o...  20.6 us
    all_to_all x1, blocking collectives, exchange(): return lax.all_to_all(x, AXES, 0, 0, tiled=True)  18.2 us
    all_to_all x2, waiting for transfers between devices, exchange(): return lax.all_to_all(x, AXES, 0, 0, tiled=True)  13.4 us
    ppermute x1, starting transfers between devices, body(): right = lax.ppermute(to_west, 'lon', [(j, i) for i, j in ring])  6.22 us
    ppermute x1, starting transfers between devices, body(): below = lax.ppermute(to_north, 'lat', line)  3.54 us
    ppermute x1, starting transfers between devices, body(): left = lax.ppermute(to_east, 'lon', ring)  2.54 us
    ppermute x1, starting transfers between devices, body(): above = lax.ppermute(to_south, 'lat', [(j, i) for i, j in line])  1.92 us
  transfers between devices with their start and end apart: 6, of which 2 were waited for; matrix products, arithmetic and copies ran while one was open for 0% of the time, Pallas kernels for 7%

profile of v6, /device:TPU:1, one launch (start us, length us, event | category | flops | bytes accessed | tf_op | source)
XLA Modules:
  0.0 88.8 jit_solution(15669657655939615222)
XLA Ops:
  0.6 3.5 %shard_map.68 = (f32[256,128]{1,0:T(8,128)}, f32[256,128]{1,0:T(8,128)}, f32[256,128]{1,0:T(8,128)}, f32[4,2,512,128]{3,2,1,0:T(8,128)}) custom-call(f32[512,256]{1,0:T(8,128)} %rhs_hbm.1, f32[512,256]{1,0:T(8,128)} %depth_hbm.1, s32[512,256]{1,0:T(8,128)} %mask_hbm.1, f32[512,256]{1,0:T(8,128)} %basis_hbm.1, f32[8,2048]{1,0:T(8,128)} %inverse_hbm.1), custom_call_target="tpu_custom_call" | custom-call | bytes 4194304 | tf_op jit(solution)/shard_map/pallas_call | solution.py:634
  4.1 2.5 %collective-permute-start = (f32[256,128]{1,0:T(8,128)}, f32[256,128]{1,0:T(8,128)S(1)}, u32[]{:S(2)}, u32[]{:S(2)}) collective-permute-start(f32[256,128]{1,0:T(8,128)} %get-tuple-element.21), channel_id=1, source_target_pairs={{0,8},{8,16},{16,24},{24,32},{32,40},{40,48},{48,56},{56,64},{64,7... | collective-permute-start | bytes 393224 | tf_op jit(solution)/shard_map/ppermute | solution.py:667
  6.7 6.2 %collective-permute-start.1 = (f32[256,128]{1,0:T(8,128)}, f32[256,128]{1,0:T(8,128)S(1)}, u32[]{:S(2)}, u32[]{:S(2)}) collective-permute-start(f32[256,128]{1,0:T(8,128)} %get-tuple-element.22), channel_id=1, source_target_pairs={{8,0},{16,8},{24,16},{32,24},{40,32},{48,40},{56,48},{64,56},{72,6... | collective-permute-start | bytes 393224 | tf_op jit(solution)/shard_map/ppermute | solution.py:668
  12.9 10.2 %all-to-all-start = ((f32[256,1,128]{2,1,0:T(1,128)}), f32[256,1,128]{2,1,0:T(1,128)S(1)}, u32[]{:S(2)}, u32[]{:S(2)}) async-start(f32[256,1,128]{2,1,0:T(1,128)} %bitcast.16), calls=%async_computation | async-start | bytes 262144 | tf_op jit(solution)/shard_map/all_to_all | solution.py:648
  23.1 0.0 collective-permute-done.left_ref
  23.1 0.0 collective-permute-done.1.right_ref
  23.1 1.0 %shard_map.70 = (f32[272,128]{1,0:T(8,128)S(1)}, f32[272,128]{1,0:T(8,128)S(1)}, f32[384,128]{1,0:T(8,128)S(1)}) custom-call(f32[4,2,512,128]{3,2,1,0:T(8,128)} %get-tuple-element.23.fields_hbm, f32[256,128]{1,0:T(8,128)S(1)} %collective-permute-done.left_ref, f32[256,128]{1,0:T(8,128)S(1)} %collective-permute-done.1.right_ref), custom_call_target="tpu_custom_call" | custom-call | bytes 4194304 | tf_op jit(solution)/shard_map/pallas_call | solution.py:634
  24.2 3.5 %collective-permute-start.2 = (f32[272,128]{1,0:T(8,128)S(1)}, f32[272,128]{1,0:T(8,128)S(1)}, u32[]{:S(2)}, u32[]{:S(2)}) collective-permute-start(f32[272,128]{1,0:T(8,128)S(1)} %get-tuple-element.28), channel_id=1, source_target_pairs={{0,1},{1,2},{2,3},{3,4},{4,5},{5,6},{6,7},{8,9},{9,10},{10,11},{11... | collective-permute-start | bytes 417800 | tf_op jit(solution)/shard_map/ppermute | solution.py:676
  27.7 1.9 %collective-permute-start.3 = (f32[272,128]{1,0:T(8,128)S(1)}, f32[272,128]{1,0:T(8,128)S(1)}, u32[]{:S(2)}, u32[]{:S(2)}) collective-permute-start(f32[272,128]{1,0:T(8,128)S(1)} %get-tuple-element.29), channel_id=1, source_target_pairs={{1,0},{2,1},{3,2},{4,3},{5,4},{6,5},{7,6},{9,8},{10,9},{11,10},{12... | collective-permute-start | bytes 417800 | tf_op jit(solution)/shard_map/ppermute | solution.py:677
  29.6 1.6 %shard_map.69 = (f32[3,544,128]{2,1,0:T(8,128)S(1)}, f32[3,544,128]{2,1,0:T(8,128)S(1)}) custom-call(f32[256,128]{1,0:T(8,128)S(1)} %collective-permute-done.left_ref, f32[256,128]{1,0:T(8,128)S(1)} %collective-permute-done.1.right_ref, f32[4,2,512,128]{3,2,1,0:T(8,128)} %get-tuple-element.23.fields_hbm), custom_call_target="tpu_custom_call" | custom-call | flops 20000000 | bytes 4194304 | tf_op jit(solution)/shard_map/pallas_call | solution.py:634
  31.3 4.6 %all-to-all-done = f32[256,1,128]{2,1,0:T(1,128)S(1)} async-done(((f32[256,1,128]{2,1,0:T(1,128)}), f32[256,1,128]{2,1,0:T(1,128)S(1)}, u32[]{:S(2)}, u32[]{:S(2)}) %all-to-all-start) | async-done | bytes 131104 | tf_op jit(solution)/shard_map/all_to_all | solution.py:648
  35.9 0.0 collective-permute-done.2.below_ref
  35.9 0.0 collective-permute-done.3.above_ref
  35.9 6.6 %shard_map.71 = (f32[3,544,128]{2,1,0:T(8,128)S(1)}, f32[3,544,128]{2,1,0:T(8,128)S(1)}, f32[256,128]{1,0:T(8,128)}, f32[3,544,128]{2,1,0:T(8,128)S(1)}, f32[7,3,544,128]{3,2,1,0:T(8,128)}) custom-call(f32[3,544,128]{2,1,0:T(8,128)S(1)} %get-tuple-element.24.wet_in, ...), custom_call_target="tpu_custom_call", output_to_operand_aliasing={{0}: (0, {}), {1}: (1, {})} | custom-call | flops 40000000 | bytes 4194304 | tf_op jit(solution)/shard_map/pallas_call | solution.py:634
  42.5 11.2 %all-to-all-start.1 = ((f32[256,1,128]{2,1,0:T(1,128)}), f32[256,1,128]{2,1,0:T(1,128)S(1)}, u32[]{:S(2)}, u32[]{:S(2)}) async-start(f32[256,1,128]{2,1,0:T(1,128)} %bitcast.4), calls=%async_computation.1 | async-start | bytes 262144 | tf_op jit(solution)/shard_map/all_to_all | solution.py:648
  53.7 4.0 %shard_map.72.smooth_ref = f32[3,544,128]{2,1,0:T(8,128)S(1)} custom-call(f32[3,544,128]{2,1,0:T(8,128)S(1)} %get-tuple-element.31.applied_ref, f32[7,3,544,128]{3,2,1,0:T(8,128)} %get-tuple-element.32.carry_hbm), custom_call_target="tpu_custom_call" | custom-call | flops 20000000 | bytes 4194304 | tf_op jit(solution)/shard_map/pallas_call | solution.py:634
  57.7 8.8 %all-to-all-done.1 = f32[256,1,128]{2,1,0:T(1,128)S(1)} async-done(((f32[256,1,128]{2,1,0:T(1,128)}), f32[256,1,128]{2,1,0:T(1,128)S(1)}, u32[]{:S(2)}, u32[]{:S(2)}) %all-to-all-start.1) | async-done | bytes 131104 | tf_op jit(solution)/shard_map/all_to_all | solution.py:648
  66.5 2.8 %shard_map.73 = (f32[256,128]{1,0:T(8,128)S(1)}, f32[8,128]{1,0:T(8,128)S(1)}, f32[2,512,128]{2,1,0:T(8,128)S(1)}, f32[2,512,128]{2,1,0:T(8,128)S(1)}, f32[2,512...) custom-call(f32[256,128]{1,0:T(8,128)S(1)} %bitcast.14, ...), custom_call_target="tpu_custom_call" | custom-call | flops 8000000 | bytes 4194304 | tf_op jit(solution)/shard_map/pallas_call | solution.py:634
  69.3 18.2 %all_to_all.33 = f32[256,1,128]{2,1,0:T(1,128)S(1)} all-to-all(f32[256,1,128]{2,1,0:T(1,128)S(1)} %bitcast.15), channel_id=1, replica_groups=mesh['lon'=32,'lat'=8] {'lon','lat'}, dimensions={0} | all-to-all | bytes 262144 | tf_op jit(solution)/shard_map/all_to_all | solution.py:648
  87.4 1.2 %shard_map.74 = (f32[512,256]{1,0:T(8,128)}, f32[512,256]{1,0:T(8,128)}) custom-call(f32[256,128]{1,0:T(8,128)S(1)} %bitcast.13, f32[8,128]{1,0:T(8,128)S(1)} %get-tuple-element.34.known_ref, f32[2,512,128]{2,1,0:T(8,128)S(1)} %get-tuple-element.35.search_ref, f32[2,512,128]{2,1,0:T(8,128)S(1)} %get-tuple-element.36.applied_ref, ...), custom_call_target="tpu_custom_call" | custom-call | flops 1000000 | bytes 4194304 | tf_op jit(solution)/shard_map/pallas_call | solution.py:634
Async XLA Ops:
  4.1 19.0 %collective-permute-start = (f32[256,128]{1,0:T(8,128)}, f32[256,128]{1,0:T(8,128)S(1)}, u32[]{:S(2)}, u32[]{:S(2)}) collective-permute-start(f32[256,128]{1,0:T(8,128)} %get-tuple-element.21), channel_id=1, source_target_pairs={{0,8},{8,16},{16,24},{24,32},{32,40},{40,48},{48,56},{56,64},{64,7... | collective-permute-start | bytes 393224 | tf_op jit(solution)/shard_map/ppermute | solution.py:667
  6.7 16.4 %collective-permute-start.1 = (f32[256,128]{1,0:T(8,128)}, f32[256,128]{1,0:T(8,128)S(1)}, u32[]{:S(2)}, u32[]{:S(2)}) collective-permute-start(f32[256,128]{1,0:T(8,128)} %get-tuple-element.22), channel_id=1, source_target_pairs={{8,0},{16,8},{24,16},{32,24},{40,32},{48,40},{56,48},{64,56},{72,6... | collective-permute-start | bytes 393224 | tf_op jit(solution)/shard_map/ppermute | solution.py:668
  12.9 23.0 %all-to-all-start = ((f32[256,1,128]{2,1,0:T(1,128)}), f32[256,1,128]{2,1,0:T(1,128)S(1)}, u32[]{:S(2)}, u32[]{:S(2)}) async-start(f32[256,1,128]{2,1,0:T(1,128)} %bitcast.16), calls=%async_computation | async-start | bytes 262144 | tf_op jit(solution)/shard_map/all_to_all | solution.py:648
  24.2 11.7 %collective-permute-start.2 = (f32[272,128]{1,0:T(8,128)S(1)}, f32[272,128]{1,0:T(8,128)S(1)}, u32[]{:S(2)}, u32[]{:S(2)}) collective-permute-start(f32[272,128]{1,0:T(8,128)S(1)} %get-tuple-element.28), channel_id=1, source_target_pairs={{0,1},{1,2},{2,3},{3,4},{4,5},{5,6},{6,7},{8,9},{9,10},{10,11},{11... | collective-permute-start | bytes 417800 | tf_op jit(solution)/shard_map/ppermute | solution.py:676
  27.7 8.2 %collective-permute-start.3 = (f32[272,128]{1,0:T(8,128)S(1)}, f32[272,128]{1,0:T(8,128)S(1)}, u32[]{:S(2)}, u32[]{:S(2)}) collective-permute-start(f32[272,128]{1,0:T(8,128)S(1)} %get-tuple-element.29), channel_id=1, source_target_pairs={{1,0},{2,1},{3,2},{4,3},{5,4},{6,5},{7,6},{9,8},{10,9},{11,10},{12... | collective-permute-start | bytes 417800 | tf_op jit(solution)/shard_map/ppermute | solution.py:677
  42.5 24.0 %all-to-all-start.1 = ((f32[256,1,128]{2,1,0:T(1,128)}), f32[256,1,128]{2,1,0:T(1,128)S(1)}, u32[]{:S(2)}, u32[]{:S(2)}) async-start(f32[256,1,128]{2,1,0:T(1,128)} %bitcast.4), calls=%async_computation.1 | async-start | bytes 262144 | tf_op jit(solution)/shard_map/all_to_all | solution.py:648

commit v7 on v6

--- a/solution.py
+++ b/solution.py
@@ -488,11 +488,19 @@
 def second_kernel(
     total_rows,
     applied_ref, carry_hbm,
-    out_ref,
+    out_ref, search_ref, rows_ref,
     wet_ref, east_ref, north_ref, west_ref, inv_ref, est_a, est_b, step_ref, shift_ref, sems,
 ):
     spot = place()
     stream = Stream(carry_hbm.at[5:6], (wet_ref,), sems)
+    rows8 = rows_ref.shape[0] // 5
+    pairs = [
+        (carry_hbm.at[6, 0, 0 : 3 * rows8], rows_ref.at[0 : 3 * rows8]),
+        (carry_hbm.at[6, 1, 0:rows8], rows_ref.at[3 * rows8 : 4 * rows8]),
+        (carry_hbm.at[6, 2, 0:rows8], rows_ref.at[4 * rows8 : 5 * rows8]),
+        (carry_hbm.at[4], search_ref),
+    ]
+    back = fetch(pairs, sems, len(CHUNKS))
     stream.need(HY)
     north_faces(spot, total_rows, wet_ref, north_ref, 0, 8)
     for ref in (est_a, est_b):
@@ -510,24 +518,20 @@
         store(out_ref, start, rows, value)
 
     smooth(applied_ref, inv_ref, faces, (est_a, est_b), step_ref, finish)
+    for copy in back:
+        copy.wait()
 
 
 def sums_kernel(
     total_rows,
-    got_ref, smooth_ref, applied_ref, carry_hbm,
+    got_ref, smooth_ref, applied_ref, search_ref, rows_ref, carry_hbm,
     send_ref, known_ref, search_out, applied_out, update_ref, operated_ref, rest_ref,
-    solver_ref, weight_ref, east_ref, north_ref, res_ref, search_ref, full_ref, sems,
+    weight_ref, east_ref, north_ref, res_ref, full_ref, sems,
 ):
     spot = place()
-    rows8 = solver_ref.shape[0] // 5
-    pairs = [(carry_hbm.at[6, 0, 0 : 3 * rows8], solver_ref.at[0 : 3 * rows8])]
-    for k in (1, 2):
-        pairs.append((carry_hbm.at[6, k, 0:rows8], solver_ref.at[(k + 2) * rows8 : (k + 3) * rows8]))
-    solver = fetch(pairs, sems, 5 * len(CHUNKS))
-    stream = Stream(carry_hbm, (weight_ref, east_ref, north_ref, res_ref, search_ref), sems)
-    for copy in solver:
-        copy.wait()
-    coarse = coarse_solve(got_ref, [(solver_ref, k * rows8) for k in range(5)])
+    rows8 = rows_ref.shape[0] // 5
+    stream = Stream(carry_hbm, (weight_ref, east_ref, north_ref, res_ref), sems)
+    coarse = coarse_solve(got_ref, [(rows_ref, k * rows8) for k in range(5)])
     curvature, projection = own_row_sums(got_ref, 2)
     lane = lane_ids(1)
     alpha = jnp.broadcast_to(projection, (1, LANES)) / jnp.broadcast_to(curvature, (1, LANES))
@@ -686,14 +690,14 @@
         scratch=[half] + [full] * 9 + [full[1:]], sems=13, flops=40000000, grant=49.5,
     )
     got = exchange(send)
-    (smoothed,) = call(
-        functools.partial(second_kernel, total_rows), [applied, carry], [full], hbm=(1,),
-        scratch=[full] * 8 + [full[1:]], sems=len(CHUNKS), flops=20000000, grant=50,
+    smoothed, search, solver = call(
+        functools.partial(second_kernel, total_rows), [applied, carry],
+        [full, full, (5 * rows8, LANES)], hbm=(1,), scratch=[full] * 8 + [full[1:]], sems=len(CHUNKS) + 4, flops=20000000, grant=50,
     )
     send, known, *state = call(
-        functools.partial(sums_kernel, total_rows), [got, smoothed, applied, carry],
-        [row, (8, LANES)] + [half] * 5, hbm=(3,),
-        scratch=[(5 * rows8, LANES), full, full, full, half, full, full], sems=5 * len(CHUNKS) + 3, flops=8000000, grant=48.5,
+        functools.partial(sums_kernel, total_rows), [got, smoothed, applied, search, solver, carry],
+        [row, (8, LANES)] + [half] * 5, hbm=(5,),
+        scratch=[full, full, full, half, full], sems=4 * len(CHUNKS), flops=8000000, grant=48,
     )
     got = exchange(send)
     field, out = call(

time: 89.1 us -> 88.9 us (level)
  transfers between devices with their start and end apart: 6 -> 6, of which waited for: 2 -> 2; matrix products, arithmetic and copies ran while one was open for 0% -> 0% of each run, Pallas kernels for 7% -> 8%
where the time goes in v7:
time: 88.9 us; the launch traced here: 88.5 us
  starting transfers between devices  35.7 us (40%)
  Pallas kernels  20.4 us (23%)
  blocking collectives  18.2 us (20%)
  waiting for transfers between devices  13.4 us (15%)
  between operations  0.89 us (1%)
    all_to_all x2, starting transfers between devices, exchange(): return lax.all_to_all(x, AXES, 0, 0, tiled=True)  21.4 us
    pallas_call x7, Pallas kernels, call(): pl.pallas_call(kernel, out_shape=[jax.ShapeDtypeStruct(s, F32) for s in o...  20.4 us
    all_to_all x1, blocking collectives, exchange(): return lax.all_to_all(x, AXES, 0, 0, tiled=True)  18.2 us
    all_to_all x2, waiting for transfers between devices, exchange(): return lax.all_to_all(x, AXES, 0, 0, tiled=True)  13.4 us
    ppermute x1, starting transfers between devices, body(): right = lax.ppermute(to_west, 'lon', [(j, i) for i, j in ring])  6.22 us
    ppermute x1, starting transfers between devices, body(): below = lax.ppermute(to_north, 'lat', line)  3.54 us
    ppermute x1, starting transfers between devices, body(): left = lax.ppermute(to_east, 'lon', ring)  2.54 us
    ppermute x1, starting transfers between devices, body(): above = lax.ppermute(to_south, 'lat', [(j, i) for i, j in line])  1.92 us
  transfers between devices with their start and end apart: 6, of which 2 were waited for; matrix products, arithmetic and copies ran while one was open for 0% of the time, Pallas kernels for 8%

profile of v7, /device:TPU:1, one launch (start us, length us, event | category | flops | bytes accessed | tf_op | source)
XLA Modules:
  0.0 88.5 jit_solution(16891012844033885479)
XLA Ops:
  0.6 3.5 %shard_map.68 = (f32[256,128]{1,0:T(8,128)}, f32[256,128]{1,0:T(8,128)}, f32[256,128]{1,0:T(8,128)}, f32[4,2,512,128]{3,2,1,0:T(8,128)}) custom-call(f32[512,256]{1,0:T(8,128)} %rhs_hbm.1, f32[512,256]{1,0:T(8,128)} %depth_hbm.1, s32[512,256]{1,0:T(8,128)} %mask_hbm.1, f32[512,256]{1,0:T(8,128)} %basis_hbm.1, f32[8,2048]{1,0:T(8,128)} %inverse_hbm.1), custom_call_target="tpu_custom_call" | custom-call | bytes 4194304 | tf_op jit(solution)/shard_map/pallas_call | solution.py:638
  4.2 2.5 %collective-permute-start = (f32[256,128]{1,0:T(8,128)}, f32[256,128]{1,0:T(8,128)S(1)}, u32[]{:S(2)}, u32[]{:S(2)}) collective-permute-start(f32[256,128]{1,0:T(8,128)} %get-tuple-element.24), channel_id=1, source_target_pairs={{0,8},{8,16},{16,24},{24,32},{32,40},{40,48},{48,56},{56,64},{64,7... | collective-permute-start | bytes 393224 | tf_op jit(solution)/shard_map/ppermute | solution.py:671
  6.7 6.2 %collective-permute-start.1 = (f32[256,128]{1,0:T(8,128)}, f32[256,128]{1,0:T(8,128)S(1)}, u32[]{:S(2)}, u32[]{:S(2)}) collective-permute-start(f32[256,128]{1,0:T(8,128)} %get-tuple-element.25), channel_id=1, source_target_pairs={{8,0},{16,8},{24,16},{32,24},{40,32},{48,40},{56,48},{64,56},{72,6... | collective-permute-start | bytes 393224 | tf_op jit(solution)/shard_map/ppermute | solution.py:672
  12.9 10.2 %all-to-all-start = ((f32[256,1,128]{2,1,0:T(1,128)}), f32[256,1,128]{2,1,0:T(1,128)S(1)}, u32[]{:S(2)}, u32[]{:S(2)}) async-start(f32[256,1,128]{2,1,0:T(1,128)} %bitcast.16), calls=%async_computation | async-start | bytes 262144 | tf_op jit(solution)/shard_map/all_to_all | solution.py:652
  23.1 0.0 collective-permute-done.left_ref
  23.1 0.0 collective-permute-done.1.right_ref
  23.2 1.0 %shard_map.70 = (f32[272,128]{1,0:T(8,128)S(1)}, f32[272,128]{1,0:T(8,128)S(1)}, f32[384,128]{1,0:T(8,128)S(1)}) custom-call(f32[4,2,512,128]{3,2,1,0:T(8,128)} %get-tuple-element.26.fields_hbm, f32[256,128]{1,0:T(8,128)S(1)} %collective-permute-done.left_ref, f32[256,128]{1,0:T(8,128)S(1)} %collective-permute-done.1.right_ref), custom_call_target="tpu_custom_call" | custom-call | bytes 4194304 | tf_op jit(solution)/shard_map/pallas_call | solution.py:638
  24.2 3.5 %collective-permute-start.2 = (f32[272,128]{1,0:T(8,128)S(1)}, f32[272,128]{1,0:T(8,128)S(1)}, u32[]{:S(2)}, u32[]{:S(2)}) collective-permute-start(f32[272,128]{1,0:T(8,128)S(1)} %get-tuple-element.31), channel_id=1, source_target_pairs={{0,1},{1,2},{2,3},{3,4},{4,5},{5,6},{6,7},{8,9},{9,10},{10,11},{11... | collective-permute-start | bytes 417800 | tf_op jit(solution)/shard_map/ppermute | solution.py:680
  27.7 1.9 %collective-permute-start.3 = (f32[272,128]{1,0:T(8,128)S(1)}, f32[272,128]{1,0:T(8,128)S(1)}, u32[]{:S(2)}, u32[]{:S(2)}) collective-permute-start(f32[272,128]{1,0:T(8,128)S(1)} %get-tuple-element.32), channel_id=1, source_target_pairs={{1,0},{2,1},{3,2},{4,3},{5,4},{6,5},{7,6},{9,8},{10,9},{11,10},{12... | collective-permute-start | bytes 417800 | tf_op jit(solution)/shard_map/ppermute | solution.py:681
  29.7 1.6 %shard_map.69 = (f32[3,544,128]{2,1,0:T(8,128)S(1)}, f32[3,544,128]{2,1,0:T(8,128)S(1)}) custom-call(f32[256,128]{1,0:T(8,128)S(1)} %collective-permute-done.left_ref, f32[256,128]{1,0:T(8,128)S(1)} %collective-permute-done.1.right_ref, f32[4,2,512,128]{3,2,1,0:T(8,128)} %get-tuple-element.26.fields_hbm), custom_call_target="tpu_custom_call" | custom-call | flops 20000000 | bytes 4194304 | tf_op jit(solution)/shard_map/pallas_call | solution.py:638
  31.3 4.6 %all-to-all-done = f32[256,1,128]{2,1,0:T(1,128)S(1)} async-done(((f32[256,1,128]{2,1,0:T(1,128)}), f32[256,1,128]{2,1,0:T(1,128)S(1)}, u32[]{:S(2)}, u32[]{:S(2)}) %all-to-all-start) | async-done | bytes 131104 | tf_op jit(solution)/shard_map/all_to_all | solution.py:652
  35.9 0.0 collective-permute-done.2.below_ref
  35.9 0.0 collective-permute-done.3.above_ref
  35.9 6.5 %shard_map.71 = (f32[3,544,128]{2,1,0:T(8,128)S(1)}, f32[3,544,128]{2,1,0:T(8,128)S(1)}, f32[256,128]{1,0:T(8,128)}, f32[3,544,128]{2,1,0:T(8,128)S(1)}, f32[7,3,544,128]{3,2,1,0:T(8,128)}) custom-call(f32[3,544,128]{2,1,0:T(8,128)S(1)} %get-tuple-element.27.wet_in, ...), custom_call_target="tpu_custom_call", output_to_operand_aliasing={{0}: (0, {}), {1}: (1, {})} | custom-call | flops 40000000 | bytes 4194304 | tf_op jit(solution)/shard_map/pallas_call | solution.py:638
  42.5 11.2 %all-to-all-start.1 = ((f32[256,1,128]{2,1,0:T(1,128)}), f32[256,1,128]{2,1,0:T(1,128)S(1)}, u32[]{:S(2)}, u32[]{:S(2)}) async-start(f32[256,1,128]{2,1,0:T(1,128)} %bitcast.4), calls=%async_computation.1 | async-start | bytes 262144 | tf_op jit(solution)/shard_map/all_to_all | solution.py:652
  53.7 4.0 %shard_map.72 = (f32[3,544,128]{2,1,0:T(8,128)S(1)}, f32[3,544,128]{2,1,0:T(8,128)S(1)}, f32[640,128]{1,0:T(8,128)S(1)}) custom-call(f32[3,544,128]{2,1,0:T(8,128)S(1)} %get-tuple-element.34.applied_ref, f32[7,3,544,128]{3,2,1,0:T(8,128)} %get-tuple-element.35.carry_hbm), custom_call_target="tpu_custom_call" | custom-call | flops 20000000 | bytes 4194304 | tf_op jit(solution)/shard_map/pallas_call | solution.py:638
  57.7 8.8 %all-to-all-done.1 = f32[256,1,128]{2,1,0:T(1,128)S(1)} async-done(((f32[256,1,128]{2,1,0:T(1,128)}), f32[256,1,128]{2,1,0:T(1,128)S(1)}, u32[]{:S(2)}, u32[]{:S(2)}) %all-to-all-start.1) | async-done | bytes 131104 | tf_op jit(solution)/shard_map/all_to_all | solution.py:652
  66.5 2.5 %shard_map.73 = (f32[256,128]{1,0:T(8,128)S(1)}, f32[8,128]{1,0:T(8,128)S(1)}, f32[2,512,128]{2,1,0:T(8,128)S(1)}, f32[2,512,128]{2,1,0:T(8,128)S(1)}, f32[2,512...) custom-call(f32[256,128]{1,0:T(8,128)S(1)} %bitcast.12, ...), custom_call_target="tpu_custom_call" | custom-call | flops 8000000 | bytes 4194304 | tf_op jit(solution)/shard_map/pallas_call | solution.py:638
  69.0 18.2 %all_to_all.33 = f32[256,1,128]{2,1,0:T(1,128)S(1)} all-to-all(f32[256,1,128]{2,1,0:T(1,128)S(1)} %bitcast.15), channel_id=1, replica_groups=mesh['lon'=32,'lat'=8] {'lon','lat'}, dimensions={0} | all-to-all | bytes 262144 | tf_op jit(solution)/shard_map/all_to_all | solution.py:652
  87.1 1.2 %shard_map.74 = (f32[512,256]{1,0:T(8,128)}, f32[512,256]{1,0:T(8,128)}) custom-call(f32[256,128]{1,0:T(8,128)S(1)} %bitcast.14, f32[8,128]{1,0:T(8,128)S(1)} %get-tuple-element.40.known_ref, f32[2,512,128]{2,1,0:T(8,128)S(1)} %get-tuple-element.41.search_ref, f32[2,512,128]{2,1,0:T(8,128)S(1)} %get-tuple-element.42.applied_ref, ...), custom_call_target="tpu_custom_call" | custom-call | flops 1000000 | bytes 4194304 | tf_op jit(solution)/shard_map/pallas_call | solution.py:638
Async XLA Ops:
  4.2 19.0 %collective-permute-start = (f32[256,128]{1,0:T(8,128)}, f32[256,128]{1,0:T(8,128)S(1)}, u32[]{:S(2)}, u32[]{:S(2)}) collective-permute-start(f32[256,128]{1,0:T(8,128)} %get-tuple-element.24), channel_id=1, source_target_pairs={{0,8},{8,16},{16,24},{24,32},{32,40},{40,48},{48,56},{56,64},{64,7... | collective-permute-start | bytes 393224 | tf_op jit(solution)/shard_map/ppermute | solution.py:671
  6.7 16.4 %collective-permute-start.1 = (f32[256,128]{1,0:T(8,128)}, f32[256,128]{1,0:T(8,128)S(1)}, u32[]{:S(2)}, u32[]{:S(2)}) collective-permute-start(f32[256,128]{1,0:T(8,128)} %get-tuple-element.25), channel_id=1, source_target_pairs={{8,0},{16,8},{24,16},{32,24},{40,32},{48,40},{56,48},{64,56},{72,6... | collective-permute-start | bytes 393224 | tf_op jit(solution)/shard_map/ppermute | solution.py:672
  12.9 23.0 %all-to-all-start = ((f32[256,1,128]{2,1,0:T(1,128)}), f32[256,1,128]{2,1,0:T(1,128)S(1)}, u32[]{:S(2)}, u32[]{:S(2)}) async-start(f32[256,1,128]{2,1,0:T(1,128)} %bitcast.16), calls=%async_computation | async-start | bytes 262144 | tf_op jit(solution)/shard_map/all_to_all | solution.py:652
  24.2 11.7 %collective-permute-start.2 = (f32[272,128]{1,0:T(8,128)S(1)}, f32[272,128]{1,0:T(8,128)S(1)}, u32[]{:S(2)}, u32[]{:S(2)}) collective-permute-start(f32[272,128]{1,0:T(8,128)S(1)} %get-tuple-element.31), channel_id=1, source_target_pairs={{0,1},{1,2},{2,3},{3,4},{4,5},{5,6},{6,7},{8,9},{9,10},{10,11},{11... | collective-permute-start | bytes 417800 | tf_op jit(solution)/shard_map/ppermute | solution.py:680
  27.7 8.2 %collective-permute-start.3 = (f32[272,128]{1,0:T(8,128)S(1)}, f32[272,128]{1,0:T(8,128)S(1)}, u32[]{:S(2)}, u32[]{:S(2)}) collective-permute-start(f32[272,128]{1,0:T(8,128)S(1)} %get-tuple-element.32), channel_id=1, source_target_pairs={{1,0},{2,1},{3,2},{4,3},{5,4},{6,5},{7,6},{9,8},{10,9},{11,10},{12... | collective-permute-start | bytes 417800 | tf_op jit(solution)/shard_map/ppermute | solution.py:681
  42.5 24.0 %all-to-all-start.1 = ((f32[256,1,128]{2,1,0:T(1,128)}), f32[256,1,128]{2,1,0:T(1,128)S(1)}, u32[]{:S(2)}, u32[]{:S(2)}) async-start(f32[256,1,128]{2,1,0:T(1,128)} %bitcast.4), calls=%async_computation.1 | async-start | bytes 262144 | tf_op jit(solution)/shard_map/all_to_all | solution.py:652

commit v8 on v7

--- a/solution.py
+++ b/solution.py
@@ -24,7 +24,7 @@
 BLK = 3
 BAND = NY // AGG_LAT
 STEP = 16
-SWEEP = 24
+SWEEP = 16
 CHUNKS = ((0, 152), (152, 128), (280, 128), (408, 136))
 SLOTS = LANES // 8
 AXES = ("lon", "lat")

time: 88.9 us -> 89.6 us (level)
  no operation moved by 1% of the time
where the time goes in v8:
time: 89.6 us; the launch traced here: 89.2 us
  starting transfers between devices  35.7 us (40%)
  Pallas kernels  21.2 us (24%)
  blocking collectives  18.2 us (20%)
  waiting for transfers between devices  13.3 us (15%)
    all_to_all x2, starting transfers between devices, exchange(): return lax.all_to_all(x, AXES, 0, 0, tiled=True)  21.4 us
    pallas_call x7, Pallas kernels, call(): pl.pallas_call(kernel, out_shape=[jax.ShapeDtypeStruct(s, F32) for s in o...  21.2 us
    all_to_all x1, blocking collectives, exchange(): return lax.all_to_all(x, AXES, 0, 0, tiled=True)  18.2 us
    all_to_all x2, waiting for transfers between devices, exchange(): return lax.all_to_all(x, AXES, 0, 0, tiled=True)  13.3 us
    ppermute x1, starting transfers between devices, body(): right = lax.ppermute(to_west, 'lon', [(j, i) for i, j in ring])  6.22 us
    ppermute x1, starting transfers between devices, body(): below = lax.ppermute(to_north, 'lat', line)  3.54 us
    ppermute x1, starting transfers between devices, body(): left = lax.ppermute(to_east, 'lon', ring)  2.54 us
    ppermute x1, starting transfers between devices, body(): above = lax.ppermute(to_south, 'lat', [(j, i) for i, j in line])  1.92 us
  transfers between devices with their start and end apart: 6, of which 2 were waited for; matrix products, arithmetic and copies ran while one was open for 0% of the time, Pallas kernels for 8%

profile of v8, /device:TPU:1, one launch (start us, length us, event | category | flops | bytes accessed | tf_op | source)
XLA Modules:
  0.0 89.2 jit_solution(4822462856789165349)
XLA Ops:
  0.6 3.5 %shard_map.68 = (f32[256,128]{1,0:T(8,128)}, f32[256,128]{1,0:T(8,128)}, f32[256,128]{1,0:T(8,128)}, f32[4,2,512,128]{3,2,1,0:T(8,128)}) custom-call(f32[512,256]{1,0:T(8,128)} %rhs_hbm.1, f32[512,256]{1,0:T(8,128)} %depth_hbm.1, s32[512,256]{1,0:T(8,128)} %mask_hbm.1, f32[512,256]{1,0:T(8,128)} %basis_hbm.1, f32[8,2048]{1,0:T(8,128)} %inverse_hbm.1), custom_call_target="tpu_custom_call" | custom-call | bytes 4194304 | tf_op jit(solution)/shard_map/pallas_call | solution.py:638
  4.2 2.5 %collective-permute-start = (f32[256,128]{1,0:T(8,128)}, f32[256,128]{1,0:T(8,128)S(1)}, u32[]{:S(2)}, u32[]{:S(2)}) collective-permute-start(f32[256,128]{1,0:T(8,128)} %get-tuple-element.24), channel_id=1, source_target_pairs={{0,8},{8,16},{16,24},{24,32},{32,40},{40,48},{48,56},{56,64},{64,7... | collective-permute-start | bytes 393224 | tf_op jit(solution)/shard_map/ppermute | solution.py:671
  6.7 6.2 %collective-permute-start.1 = (f32[256,128]{1,0:T(8,128)}, f32[256,128]{1,0:T(8,128)S(1)}, u32[]{:S(2)}, u32[]{:S(2)}) collective-permute-start(f32[256,128]{1,0:T(8,128)} %get-tuple-element.25), channel_id=1, source_target_pairs={{8,0},{16,8},{24,16},{32,24},{40,32},{48,40},{56,48},{64,56},{72,6... | collective-permute-start | bytes 393224 | tf_op jit(solution)/shard_map/ppermute | solution.py:672
  12.9 10.2 %all-to-all-start = ((f32[256,1,128]{2,1,0:T(1,128)}), f32[256,1,128]{2,1,0:T(1,128)S(1)}, u32[]{:S(2)}, u32[]{:S(2)}) async-start(f32[256,1,128]{2,1,0:T(1,128)} %bitcast.16), calls=%async_computation | async-start | bytes 262144 | tf_op jit(solution)/shard_map/all_to_all | solution.py:652
  23.1 0.0 collective-permute-done.left_ref
  23.1 0.0 collective-permute-done.1.right_ref
  23.2 1.0 %shard_map.70 = (f32[272,128]{1,0:T(8,128)S(1)}, f32[272,128]{1,0:T(8,128)S(1)}, f32[384,128]{1,0:T(8,128)S(1)}) custom-call(f32[4,2,512,128]{3,2,1,0:T(8,128)} %get-tuple-element.26.fields_hbm, f32[256,128]{1,0:T(8,128)S(1)} %collective-permute-done.left_ref, f32[256,128]{1,0:T(8,128)S(1)} %collective-permute-done.1.right_ref), custom_call_target="tpu_custom_call" | custom-call | bytes 4194304 | tf_op jit(solution)/shard_map/pallas_call | solution.py:638
  24.2 3.5 %collective-permute-start.2 = (f32[272,128]{1,0:T(8,128)S(1)}, f32[272,128]{1,0:T(8,128)S(1)}, u32[]{:S(2)}, u32[]{:S(2)}) collective-permute-start(f32[272,128]{1,0:T(8,128)S(1)} %get-tuple-element.31), channel_id=1, source_target_pairs={{0,1},{1,2},{2,3},{3,4},{4,5},{5,6},{6,7},{8,9},{9,10},{10,11},{11... | collective-permute-start | bytes 417800 | tf_op jit(solution)/shard_map/ppermute | solution.py:680
  27.7 1.9 %collective-permute-start.3 = (f32[272,128]{1,0:T(8,128)S(1)}, f32[272,128]{1,0:T(8,128)S(1)}, u32[]{:S(2)}, u32[]{:S(2)}) collective-permute-start(f32[272,128]{1,0:T(8,128)S(1)} %get-tuple-element.32), channel_id=1, source_target_pairs={{1,0},{2,1},{3,2},{4,3},{5,4},{6,5},{7,6},{9,8},{10,9},{11,10},{12... | collective-permute-start | bytes 417800 | tf_op jit(solution)/shard_map/ppermute | solution.py:681
  29.7 1.6 %shard_map.69 = (f32[3,544,128]{2,1,0:T(8,128)S(1)}, f32[3,544,128]{2,1,0:T(8,128)S(1)}) custom-call(f32[256,128]{1,0:T(8,128)S(1)} %collective-permute-done.left_ref, f32[256,128]{1,0:T(8,128)S(1)} %collective-permute-done.1.right_ref, f32[4,2,512,128]{3,2,1,0:T(8,128)} %get-tuple-element.26.fields_hbm), custom_call_target="tpu_custom_call" | custom-call | flops 20000000 | bytes 4194304 | tf_op jit(solution)/shard_map/pallas_call | solution.py:638
  31.3 4.6 %all-to-all-done = f32[256,1,128]{2,1,0:T(1,128)S(1)} async-done(((f32[256,1,128]{2,1,0:T(1,128)}), f32[256,1,128]{2,1,0:T(1,128)S(1)}, u32[]{:S(2)}, u32[]{:S(2)}) %all-to-all-start) | async-done | bytes 131104 | tf_op jit(solution)/shard_map/all_to_all | solution.py:652
  35.9 0.0 collective-permute-done.2.below_ref
  35.9 0.0 collective-permute-done.3.above_ref
  35.9 7.3 %shard_map.71 = (f32[3,544,128]{2,1,0:T(8,128)S(1)}, f32[3,544,128]{2,1,0:T(8,128)S(1)}, f32[256,128]{1,0:T(8,128)}, f32[3,544,128]{2,1,0:T(8,128)S(1)}, f32[7,3,544,128]{3,2,1,0:T(8,128)}) custom-call(f32[3,544,128]{2,1,0:T(8,128)S(1)} %get-tuple-element.27.wet_in, ...), custom_call_target="tpu_custom_call", output_to_operand_aliasing={{0}: (0, {}), {1}: (1, {})} | custom-call | flops 40000000 | bytes 4194304 | tf_op jit(solution)/shard_map/pallas_call | solution.py:638
  43.2 11.2 %all-to-all-start.1 = ((f32[256,1,128]{2,1,0:T(1,128)}), f32[256,1,128]{2,1,0:T(1,128)S(1)}, u32[]{:S(2)}, u32[]{:S(2)}) async-start(f32[256,1,128]{2,1,0:T(1,128)} %bitcast.4), calls=%async_computation.1 | async-start | bytes 262144 | tf_op jit(solution)/shard_map/all_to_all | solution.py:652
  54.4 4.1 %shard_map.72 = (f32[3,544,128]{2,1,0:T(8,128)S(1)}, f32[3,544,128]{2,1,0:T(8,128)S(1)}, f32[640,128]{1,0:T(8,128)S(1)}) custom-call(f32[3,544,128]{2,1,0:T(8,128)S(1)} %get-tuple-element.34.applied_ref, f32[7,3,544,128]{3,2,1,0:T(8,128)} %get-tuple-element.35.carry_hbm), custom_call_target="tpu_custom_call" | custom-call | flops 20000000 | bytes 4194304 | tf_op jit(solution)/shard_map/pallas_call | solution.py:638
  58.5 8.7 %all-to-all-done.1 = f32[256,1,128]{2,1,0:T(1,128)S(1)} async-done(((f32[256,1,128]{2,1,0:T(1,128)}), f32[256,1,128]{2,1,0:T(1,128)S(1)}, u32[]{:S(2)}, u32[]{:S(2)}) %all-to-all-start.1) | async-done | bytes 131104 | tf_op jit(solution)/shard_map/all_to_all | solution.py:652
  67.2 2.5 %shard_map.73 = (f32[256,128]{1,0:T(8,128)S(1)}, f32[8,128]{1,0:T(8,128)S(1)}, f32[2,512,128]{2,1,0:T(8,128)S(1)}, f32[2,512,128]{2,1,0:T(8,128)S(1)}, f32[2,512...) custom-call(f32[256,128]{1,0:T(8,128)S(1)} %bitcast.12, ...), custom_call_target="tpu_custom_call" | custom-call | flops 8000000 | bytes 4194304 | tf_op jit(solution)/shard_map/pallas_call | solution.py:638
  69.7 18.2 %all_to_all.33 = f32[256,1,128]{2,1,0:T(1,128)S(1)} all-to-all(f32[256,1,128]{2,1,0:T(1,128)S(1)} %bitcast.15), channel_id=1, replica_groups=mesh['lon'=32,'lat'=8] {'lon','lat'}, dimensions={0} | all-to-all | bytes 262144 | tf_op jit(solution)/shard_map/all_to_all | solution.py:652
  87.9 1.2 %shard_map.74 = (f32[512,256]{1,0:T(8,128)}, f32[512,256]{1,0:T(8,128)}) custom-call(f32[256,128]{1,0:T(8,128)S(1)} %bitcast.14, f32[8,128]{1,0:T(8,128)S(1)} %get-tuple-element.40.known_ref, f32[2,512,128]{2,1,0:T(8,128)S(1)} %get-tuple-element.41.search_ref, f32[2,512,128]{2,1,0:T(8,128)S(1)} %get-tuple-element.42.applied_ref, ...), custom_call_target="tpu_custom_call" | custom-call | flops 1000000 | bytes 4194304 | tf_op jit(solution)/shard_map/pallas_call | solution.py:638
Async XLA Ops:
  4.2 19.0 %collective-permute-start = (f32[256,128]{1,0:T(8,128)}, f32[256,128]{1,0:T(8,128)S(1)}, u32[]{:S(2)}, u32[]{:S(2)}) collective-permute-start(f32[256,128]{1,0:T(8,128)} %get-tuple-element.24), channel_id=1, source_target_pairs={{0,8},{8,16},{16,24},{24,32},{32,40},{40,48},{48,56},{56,64},{64,7... | collective-permute-start | bytes 393224 | tf_op jit(solution)/shard_map/ppermute | solution.py:671
  6.7 16.4 %collective-permute-start.1 = (f32[256,128]{1,0:T(8,128)}, f32[256,128]{1,0:T(8,128)S(1)}, u32[]{:S(2)}, u32[]{:S(2)}) collective-permute-start(f32[256,128]{1,0:T(8,128)} %get-tuple-element.25), channel_id=1, source_target_pairs={{8,0},{16,8},{24,16},{32,24},{40,32},{48,40},{56,48},{64,56},{72,6... | collective-permute-start | bytes 393224 | tf_op jit(solution)/shard_map/ppermute | solution.py:672
  12.9 23.0 %all-to-all-start = ((f32[256,1,128]{2,1,0:T(1,128)}), f32[256,1,128]{2,1,0:T(1,128)S(1)}, u32[]{:S(2)}, u32[]{:S(2)}) async-start(f32[256,1,128]{2,1,0:T(1,128)} %bitcast.16), calls=%async_computation | async-start | bytes 262144 | tf_op jit(solution)/shard_map/all_to_all | solution.py:652
  24.2 11.7 %collective-permute-start.2 = (f32[272,128]{1,0:T(8,128)S(1)}, f32[272,128]{1,0:T(8,128)S(1)}, u32[]{:S(2)}, u32[]{:S(2)}) collective-permute-start(f32[272,128]{1,0:T(8,128)S(1)} %get-tuple-element.31), channel_id=1, source_target_pairs={{0,1},{1,2},{2,3},{3,4},{4,5},{5,6},{6,7},{8,9},{9,10},{10,11},{11... | collective-permute-start | bytes 417800 | tf_op jit(solution)/shard_map/ppermute | solution.py:680
  27.7 8.2 %collective-permute-start.3 = (f32[272,128]{1,0:T(8,128)S(1)}, f32[272,128]{1,0:T(8,128)S(1)}, u32[]{:S(2)}, u32[]{:S(2)}) collective-permute-start(f32[272,128]{1,0:T(8,128)S(1)} %get-tuple-element.32), channel_id=1, source_target_pairs={{1,0},{2,1},{3,2},{4,3},{5,4},{6,5},{7,6},{9,8},{10,9},{11,10},{12... | collective-permute-start | bytes 417800 | tf_op jit(solution)/shard_map/ppermute | solution.py:681
  43.2 24.0 %all-to-all-start.1 = ((f32[256,1,128]{2,1,0:T(1,128)}), f32[256,1,128]{2,1,0:T(1,128)S(1)}, u32[]{:S(2)}, u32[]{:S(2)}) async-start(f32[256,1,128]{2,1,0:T(1,128)} %bitcast.4), calls=%async_computation.1 | async-start | bytes 262144 | tf_op jit(solution)/shard_map/all_to_all | solution.py:652
